TPU v7x, 32 devices: a whole 2x2x4 slice. The times are simulated.
32 devices in a mesh: gr: 8 (over y, x, core), gc: 4 (over z).
Axes of the slice: x: 2, y: 2, z: 4, core: 2. Of those that a mesh axis runs over, the one named last changes fastest.
Arguments:
- x_states: bfloat16 [32768, 512], P(('gr', 'gc'))
- y_states: bfloat16 [32768, 512], P(('gr', 'gc')), as said below
Outputs:
- proj_x: bfloat16 [32768, 512], P(('gr', 'gc'))
- proj_y: bfloat16 [32768, 512], P(('gr', 'gc'))
- cross: float32 [512, 512], replicated
Inputs may be any that keep to these rules, and one draw needn't show every extreme that they name: `y_states`: paired with x_states row by row.
All inputs are finite; a program needn't handle non-finite values.
Results may differ from a plain program's by a relative error of at most 0.0015.
Values sent between devices are 32-bit elements; how exact they have to be, the bound alone decides.
No kernel may reach another device: no remote copies, remote signals or barrier semaphores. Data moves between devices by JAX's collectives and lax.ppermute only.
A program may use at most 64 MiB of HBM per device.

v0:
```python
import jax
import jax.numpy as jnp
from jax import lax
from jax.sharding import PartitionSpec as P

RIDGE = 0.1


def on_device(x_states, y_states):
    width = x_states.shape[1]
    partial_rows = lax.psum_scatter(
        jnp.concatenate(
            [
                jnp.dot(x_states.T, x_states, preferred_element_type=jnp.float32),
                jnp.dot(y_states.T, y_states, preferred_element_type=jnp.float32),
                jnp.dot(x_states.T, y_states, preferred_element_type=jnp.float32),
            ],
            axis=1,
        ),
        "gr",
        scatter_dimension=0,
        tiled=True,
    )
    tile = lax.psum_scatter(partial_rows, "gc", scatter_dimension=1, tiled=True)
    row_block = lax.all_gather(tile, "gc", axis=1, tiled=True)
    sums = lax.all_gather(row_block, "gr", axis=0, tiled=True)
    sum_x = sums[:, :width]
    sum_y = sums[:, width : 2 * width]
    sum_xy = sums[:, 2 * width :]
    total_rows = x_states.shape[0] * lax.axis_size("gr") * lax.axis_size("gc")
    eye = jnp.eye(width, dtype=jnp.float32)
    cov_x = sum_x / total_rows + RIDGE * eye
    cov_y = sum_y / total_rows + RIDGE * eye
    cov_xy = sum_xy / total_rows
    low_x = jnp.linalg.cholesky(cov_x)
    low_y = jnp.linalg.cholesky(cov_y)
    left = jax.scipy.linalg.solve_triangular(low_x, cov_xy, lower=True)
    cross = jax.scipy.linalg.solve_triangular(low_y, left.T, lower=True).T
    white_x = jax.scipy.linalg.solve_triangular(low_x, x_states.astype(jnp.float32).T, lower=True).T
    white_y = jax.scipy.linalg.solve_triangular(low_y, y_states.astype(jnp.float32).T, lower=True).T
    proj_x = jnp.dot(white_x, cross, precision=lax.Precision.HIGHEST).astype(jnp.bfloat16)
    proj_y = jnp.dot(white_y, cross.T, precision=lax.Precision.HIGHEST).astype(jnp.bfloat16)
    return (proj_x, proj_y, cross)


def solution(mesh):
    return jax.shard_map(
        on_device,
        mesh=mesh,
        in_specs=(P(("gr", "gc"), None), P(("gr", "gc"), None)),
        out_specs=(P(("gr", "gc"), None), P(("gr", "gc"), None), P()),
        check_vma=False,
    )
```

profile of v0, /device:TPU:0, one launch (start us, length us, event | category | flops | bytes accessed | tf_op | source)
XLA Modules:
  0.0 505.9 jit_solution(16684515446495486894)
XLA Ops:
  7.2 2.4 fusion.133
  11.5 2.4 copy.15
  14.0 49.0 %reduce-scatter.7.cloned.1.call-done = f32[64,1536]{1,0:T(8,128)} async-done(((f32[512,1536]{1,0:T(8,128)}), f32[64,1536]{1,0:T(8,128)}) %reduce-scatter.7.cloned.1.call-update) | async-done | bytes 393232
  63.0 2.1 copy.16
  65.2 24.1 %reduce-scatter.5.cloned.1.call-done = f32[64,384]{0,1:T(8,128)} async-done(((f32[64,1536]{0,1:T(8,128)}), f32[64,384]{0,1:T(8,128)}) %reduce-scatter.5.cloned.1.call-update) | async-done | bytes 98320 | tf_op jit(solution)/shard_map/reduce_scatter | solution.py:24
  89.3 18.4 %all_gather.6 = f32[64,1536]{0,1:T(8,128)S(1)} all-gather(f32[64,384]{0,1:T(8,128)} %reduce-scatter.5.cloned.1.call-done), channel_id=1, replica_groups=mesh['gr'=8,'gc'=4] {'gc'}, dimensions={1}, use_global_device_ids=true | all-gather | bytes 491520 | tf_op jit(solution)/shard_map/all_gather | solution.py:25
  111.9 28.5 %all-gather.2.cloned.1.call-done = f32[512,1536]{1,0:T(8,128)} async-done(((f32[64,1536]{1,0:T(8,128)}), f32[512,1536]{1,0:T(8,128)}) %all-gather.2.cloned.1.call-update) | async-done | bytes 3145744 | tf_op jit(solution)/shard_map/all_gather | solution.py:26
  140.5 3.6 fusion.131
  146.7 2.5 copy.10
  151.7 11.7 %cholesky.286 = f32[128,128]{1,0:T(8,128)S(1)} custom-call(f32[128,128]{1,0:T(8,128)S(1)} %cholesky.426), custom_call_target="Cholesky" | custom-call | tf_op jit(solution)/shard_map/jit(cholesky)/cholesky | solution.py:35
  163.6 9.8 %custom-call.31 = f32[1,128,128]{1,2,0:T(8,128)S(1)} custom-call(f32[1,128,128]{2,1,0:T(8,128)S(1)} %get-tuple-element.86), custom_call_target="InvertDiagBlocksLowerTriangular" | custom-call | tf_op jit(solution)/shard_map/jit(cholesky)/cholesky | solution.py:35
  175.9 12.1 %cholesky.305 = f32[128,128]{1,0:T(8,128)S(1)} custom-call(f32[128,128]{1,0:T(8,128)S(1)} %cholesky.430), custom_call_target="Cholesky" | custom-call | tf_op jit(solution)/shard_map/jit(cholesky)/cholesky | solution.py:35
  188.0 9.8 %custom-call.32 = f32[1,128,128]{1,2,0:T(8,128)S(1)} custom-call(f32[1,128,128]{2,1,0:T(8,128)S(1)} %get-tuple-element.83), custom_call_target="InvertDiagBlocksLowerTriangular" | custom-call | tf_op jit(solution)/shard_map/jit(cholesky)/cholesky | solution.py:35
  199.4 11.7 %cholesky.326 = f32[128,128]{1,0:T(8,128)S(1)} custom-call(f32[128,128]{1,0:T(8,128)S(1)} %cholesky.435), custom_call_target="Cholesky" | custom-call | tf_op jit(solution)/shard_map/jit(cholesky)/cholesky | solution.py:35
  211.2 9.8 %custom-call.33 = f32[1,128,128]{1,2,0:T(8,128)S(1)} custom-call(f32[1,128,128]{2,1,0:T(8,128)S(1)} %get-tuple-element.80), custom_call_target="InvertDiagBlocksLowerTriangular" | custom-call | tf_op jit(solution)/shard_map/jit(cholesky)/cholesky | solution.py:35
  222.4 11.9 %cholesky.343 = f32[128,128]{1,0:T(8,128)S(1)} custom-call(f32[128,128]{1,0:T(8,128)S(1)} %convolution_subtract_fusion.15), custom_call_target="Cholesky" | custom-call | tf_op jit(solution)/shard_map/jit(cholesky)/cholesky | solution.py:35
  240.7 14.1 %while.8 = (s32[]{:T(128)}, f32[512,512]{1,0:T(8,128)}, s32[4,2]{0,1:T(2,128)S(1)}, f32[4,128,128]{2,1,0:T(8,128)}, s32[]{:T(128)}) while((s32[]{:T(128)}, f32[512,512]{1,0:T(8,128)}, s32[4,2]{0,1:T(2,128)S(1)}, f32[4,128,128]{2,1,0:T(8,128)}, s32[]{:T(128)}) %tuple.68), condition=%wide.while_cond, body=%wide.while_body.sunk | while | flops 2 | bytes 132205 | solution.py:39
  241.4 2.9 bitcast_dynamic-update-slice_fusion.4
  244.9 2.9 bitcast_dynamic-update-slice_fusion.4
  248.4 2.9 bitcast_dynamic-update-slice_fusion.4
  252.0 2.8 bitcast_dynamic-update-slice_fusion.4
  254.8 40.2 %custom-call.34 = f32[4,128,128]{1,2,0:T(8,128)S(1)} custom-call(f32[4,128,128]{2,1,0:T(8,128)} %get-tuple-element.34), custom_call_target="InvertDiagBlocksLowerTriangular" | custom-call | tf_op jit(solution)/shard_map/jit(_solve_triangular)/triangular_solve | solution.py:39
  295.0 1.8 fusion.60
  296.8 2.3 convolution_subtract_fusion.3
  299.8 1.8 convolution_subtract_fusion.1
  302.3 2.7 fusion.37
  306.4 2.5 copy.19
  313.2 1.9 convolution_subtract_fusion.9
  319.2 2.5 copy.12
  324.2 11.7 %cholesky.358 = f32[128,128]{1,0:T(8,128)S(1)} custom-call(f32[128,128]{1,0:T(8,128)S(1)} %cholesky.439), custom_call_target="Cholesky" | custom-call | tf_op jit(solution)/shard_map/jit(cholesky)/cholesky | solution.py:36
  336.1 9.8 %custom-call.35 = f32[1,128,128]{1,2,0:T(8,128)S(1)} custom-call(f32[1,128,128]{2,1,0:T(8,128)S(1)} %get-tuple-element.76), custom_call_target="InvertDiagBlocksLowerTriangular" | custom-call | tf_op jit(solution)/shard_map/jit(cholesky)/cholesky | solution.py:36
  348.4 11.7 %cholesky.377 = f32[128,128]{1,0:T(8,128)S(1)} custom-call(f32[128,128]{1,0:T(8,128)S(1)} %cholesky.443), custom_call_target="Cholesky" | custom-call | tf_op jit(solution)/shard_map/jit(cholesky)/cholesky | solution.py:36
  360.2 10.0 %custom-call.36 = f32[1,128,128]{1,2,0:T(8,128)S(1)} custom-call(f32[1,128,128]{2,1,0:T(8,128)S(1)} %get-tuple-element.73), custom_call_target="InvertDiagBlocksLowerTriangular" | custom-call | tf_op jit(solution)/shard_map/jit(cholesky)/cholesky | solution.py:36
  371.7 11.7 %cholesky.398 = f32[128,128]{1,0:T(8,128)S(1)} custom-call(f32[128,128]{1,0:T(8,128)S(1)} %cholesky.448), custom_call_target="Cholesky" | custom-call | tf_op jit(solution)/shard_map/jit(cholesky)/cholesky | solution.py:36
  383.4 9.8 %custom-call.37 = f32[1,128,128]{1,2,0:T(8,128)S(1)} custom-call(f32[1,128,128]{2,1,0:T(8,128)S(1)} %get-tuple-element.70), custom_call_target="InvertDiagBlocksLowerTriangular" | custom-call | tf_op jit(solution)/shard_map/jit(cholesky)/cholesky | solution.py:36
  394.7 12.1 %cholesky.415 = f32[128,128]{1,0:T(8,128)S(1)} custom-call(f32[128,128]{1,0:T(8,128)S(1)} %convolution_subtract_fusion.14), custom_call_target="Cholesky" | custom-call | tf_op jit(solution)/shard_map/jit(cholesky)/cholesky | solution.py:36
  413.1 13.8 %while.9 = (s32[]{:T(128)}, f32[512,512]{1,0:T(8,128)}, s32[4,2]{0,1:T(2,128)S(1)}, f32[4,128,128]{2,1,0:T(8,128)}, s32[]{:T(128)}) while((s32[]{:T(128)}, f32[512,512]{1,0:T(8,128)}, s32[4,2]{0,1:T(2,128)S(1)}, f32[4,128,128]{2,1,0:T(8,128)}, s32[]{:T(128)}) %tuple.80), condition=%wide.while_cond.1.clone, body=%wide.while_body.1.clone.sunk | while | flops 2 | bytes 132205 | solution.py:38
  413.7 2.9 bitcast_dynamic-update-slice_fusion.5
  417.2 2.9 bitcast_dynamic-update-slice_fusion.5
  420.7 2.9 bitcast_dynamic-update-slice_fusion.5
  424.2 2.8 bitcast_dynamic-update-slice_fusion.5
  427.0 40.2 %custom-call.39 = f32[4,128,128]{1,2,0:T(8,128)S(1)} custom-call(f32[4,128,128]{2,1,0:T(8,128)} %get-tuple-element.36), custom_call_target="InvertDiagBlocksLowerTriangular" | custom-call | tf_op jit(solution)/shard_map/jit(_solve_triangular)/triangular_solve | solution.py:38
  470.6 2.0 convolution_subtract_fusion.4
  473.0 2.6 convolution_subtract_fusion.8
  477.1 7.9 %fusion.31 = bf16[1024,512]{1,0:T(8,128)(2,1)} fusion(f32[128,1024]{1,0:T(8,128)S(1)} %copy-done.15, f32[128,1024]{1,0:T(8,128)S(1)} %copy-done.11, f32[128,1024]{1,0:T(8,128)S(1)} %copy-done.4, f32[128,1024]{1,0:T(8,128)S(1)} %copy-done.2, f32[128,512]{1,0:T(8,128)S(1)} %fusion.114, f32[128,512]{1,0:T(8,128)S(1)} %fusion.112, f32[128,512]{1,0:T(8,128)S(1)} %fusion.110, ...), kind=kOutput, calls=%fused_computation.36 | convolution fusion | flops 3224109056 | bytes 4194304 | tf_op jit(solution)/shard_map/dot_general | solution.py:41
  487.4 1.8 convolution_subtract_fusion
  489.9 2.8 fusion.34
  493.4 4.5 fusion.28
  (129 shorter events, 59.2 us)
Async XLA Ops:
  7.2 2.5 copy-start.14
  7.2 2.5 copy-start.12
  7.2 55.8 %reduce-scatter.7.cloned.1.call-start = ((), (), s32[]{:S(2)}) async-start(), calls=%async_computation.4 | async-start | bytes 3538944
  13.9 94.8 %copy-start.13 = (bf16[1024,512]{1,0:T(8,128)(2,1)S(1)}, bf16[1024,512]{1,0:T(8,128)(2,1)}, u32[]{:S(2)}) copy-start(bf16[1024,512]{1,0:T(8,128)(2,1)} %param.7) | copy-start | bytes 3145732
  13.9 75.4 %reduce-scatter.5.cloned.1.call-start = ((), (), s32[]{:S(2)}) async-start(), calls=%async_computation.2 | async-start | bytes 983040 | tf_op jit(solution)/shard_map/reduce_scatter | solution.py:24
  65.2 75.3 %all-gather.2.cloned.1.call-start = ((), (), s32[]{:S(2)}) async-start(), calls=%async_computation.3 | async-start | bytes 3538944 | tf_op jit(solution)/shard_map/all_gather | solution.py:26
  150.7 1.0 copy-start.8
  254.8 45.0 %copy-start.6 = (f32[512,512]{1,0:T(8,128)S(1)}, f32[512,512]{1,0:T(8,128)}, u32[]{:S(2)}) copy-start(f32[512,512]{1,0:T(8,128)} %get-tuple-element.189) | copy-start | bytes 3145732
  295.0 4.8 copy-start
  296.8 5.4 %copy-start.1 = (f32[128,1024]{1,0:T(8,128)}, f32[128,1024]{1,0:T(8,128)S(1)}, u32[]{:S(2)}) copy-start(f32[128,1024]{1,0:T(8,128)S(1)} %fusion.60) | copy-start | bytes 1572868
  299.8 5.2 %copy-start.3 = (f32[128,1024]{1,0:T(8,128)}, f32[128,1024]{1,0:T(8,128)S(1)}, u32[]{:S(2)}) copy-start(f32[128,1024]{1,0:T(8,128)S(1)} %fusion.104) | copy-start | bytes 1572868
  302.3 4.2 copy-start.10
  323.2 1.0 copy-start.9
  427.0 43.6 %copy-start.5 = (f32[512,512]{1,0:T(8,128)S(1)}, f32[512,512]{1,0:T(8,128)}, u32[]{:S(2)}) copy-start(f32[512,512]{1,0:T(8,128)} %get-tuple-element.188) | copy-start | bytes 3145732
  473.0 4.1 copy-start.2
  473.0 4.1 copy-start.4
  473.0 4.1 copy-start.11
  473.0 4.1 copy-start.15
  493.4 4.5 copy-start.7
Sparse Core Ops, SparseCore 0:
  14.0 48.9 reduce-scatter.6
  66.0 23.2 reduce-scatter.4
  108.9 31.5 all-gather.1
where the time goes:
time: 510 us; the launch traced here: 506 us
  other arithmetic  252 us (49%)
  waiting for transfers between devices  102 us (20%)
  matrix products  60.8 us (12%)
  local copies, waits for them, and re-layouts  52.7 us (10%)
  between operations  19.7 us (4%)
  blocking collectives  18.4 us (4%)
    another operation x14, other arithmetic, on_device(): low_x = jnp.linalg.cholesky(cov_x)  79 us
    another operation x14, other arithmetic, on_device(): low_y = jnp.linalg.cholesky(cov_y)  78.9 us
    unnamed x4, waiting for transfers between devices  49.1 us
    another operation x3, other arithmetic, on_device(): jax.scipy.linalg.solve_triangular(low_x, x_states.astype(jnp.float32).T,...  41.3 us
    another operation x2, other arithmetic, on_device(): cross = jax.scipy.linalg.solve_triangular(low_y, left.T, lower=True).T  41.3 us
    all_gather x1, waiting for transfers between devices, on_device(): sums = lax.all_gather(row_block, 'gr', axis=0, tiled=True)  28.5 us
    reduce_scatter x1, waiting for transfers between devices, on_device(): tile = lax.psum_scatter(partial_rows, 'gc', scatter_dimension=1, tiled=True)  24.1 us
    all_gather x1, blocking collectives, on_device(): row_block = lax.all_gather(tile, 'gc', axis=1, tiled=True)  18.4 us
  transfers between devices with their start and end apart: 3, of which 3 were waited for; matrix products, arithmetic and copies ran while one was open for 1% of the time, Pallas kernels for 0%

commit v1 on v0

v1 whole, which is shorter than its diff:
```python
import jax
import jax.numpy as jnp
from jax import lax
from jax.experimental import pallas as pl
from jax.experimental.pallas import tpu as pltpu
from jax.sharding import PartitionSpec as P

RIDGE = 0.1
B = 128
NB = 16
BF = jnp.bfloat16
F32 = jnp.float32
VMEM_LIMIT = 48 * 1024 * 1024


def dot(a, b, ca=1, cb=0, precision=None):
    return lax.dot_general(a, b, (((ca,), (cb,)), ((), ())), preferred_element_type=F32, precision=precision)


def dot_f32(a, b, ca=1, cb=0):
    return dot(a, b, ca, cb, lax.Precision.HIGHEST)


def split2(a):
    high = a.astype(BF)
    return high, (a - high.astype(F32)).astype(BF)


def split3(a):
    high = a.astype(BF)
    rest = a - high.astype(F32)
    mid = rest.astype(BF)
    return high, mid, (rest - mid.astype(F32)).astype(BF)


def dot_x3(a, b, ca=1, cb=0):
    ah, al = a
    bh, bl = b
    return dot(ah, bh, ca, cb) + (dot(ah, bl, ca, cb) + dot(al, bh, ca, cb))


def outer_sum(u, v):
    uh, um, ul = split3(u)
    vh, vm, vl = split3(v)
    a = jnp.concatenate([uh, uh, um, uh, ul, um], 0)
    b = jnp.concatenate([vh, vm, vh, vl, vh, vm], 0)
    return dot(a, b, 0, 0)


def inverse_factor(a):
    n = a.shape[0]
    r = lax.broadcasted_iota(jnp.int32, (n, n), 0)
    c = lax.broadcasted_iota(jnp.int32, (n, n), 1)
    z = jnp.where(r == c, 1.0, 0.0).astype(F32)
    rows = lax.broadcasted_iota(jnp.int32, (NB, n), 0)
    out = []
    for s in range(n // NB):
        t, v = a[:NB], z[:NB]
        cols = [jnp.broadcast_to(t[:, NB * s + q : NB * s + q + 1], (NB, n)) for q in range(NB)]
        pivots = jnp.zeros((NB, n), F32)
        for k in range(NB):
            d = cols[k][k : k + 1, :]
            pivots = jnp.where(rows == k, d, pivots)
            if k == NB - 1:
                break
            m = jnp.where(rows > k, cols[k] * (1.0 / d), 0.0)
            t = t - m * t[k : k + 1, :]
            v = v - m * v[k : k + 1, :]
            for q in range(k + 1, NB):
                cols[q] = cols[q] - m * cols[q][k : k + 1, :]
        scale = lax.rsqrt(pivots)
        t, v = t * scale, v * scale
        out.append(v)
        if NB * (s + 1) < n:
            update = outer_sum(t[:, NB * (s + 1) :], jnp.concatenate([t, v], 1))
            a, z = a[NB:] - update[:, :n], z[NB:] - update[:, n:]
    return jnp.concatenate(out, 0)


def upper_blocks(n):
    return [(i, j) for i in range(n) for j in range(i, n)]


def lower_blocks(n):
    return [(i, j) for i in range(n) for j in range(i + 1)]


def gram_kernel(partner, core_ref, x_ref, y_ref, o_ref, a_ref):
    width = x_ref.shape[1]
    n = width // B
    core = core_ref[0]
    owner = 1 - core if partner else core

    @pl.when(owner == 0)
    def _():
        a_ref[...] = x_ref[...]

    @pl.when(owner == 1)
    def _():
        a_ref[...] = y_ref[...]

    row = 0
    for i in range(n):
        g = dot(a_ref[:, B * i : B * (i + 1)], a_ref[:, B * i :], 0, 0)
        for j in range(n - i):
            o_ref[row : row + B, :] = g[:, B * j : B * (j + 1)]
            row += B
    half = width // 2
    columns = pl.ds(pl.multiple_of(owner * half, half), half)
    g = dot(x_ref[...], y_ref[:, columns], 0, 0)
    for j in range(half // B):
        o_ref[row : row + width, :] = g[:, B * j : B * (j + 1)]
        row += width


def factor_kernel(total_rows, n, s_ref, o_ref, f_ref):
    r = lax.broadcasted_iota(jnp.int32, (B, B), 0)
    c = lax.broadcasted_iota(jnp.int32, (B, B), 1)
    ridge = jnp.where(r == c, RIDGE, 0.0).astype(F32)
    at = lambda i: slice(B * i, B * (i + 1))
    for k, (i, j) in enumerate(upper_blocks(n)):
        block = s_ref[at(k), :] / total_rows
        f_ref[at(i), at(j)] = block + ridge if i == j else block
    for b in range(n):
        w = inverse_factor(f_ref[at(b), at(b)])
        f_ref[at(b), at(b)] = w
        if b > 0:
            f_ref[at(b), : B * b] = dot_f32(w, f_ref[at(b), : B * b])
        if b < n - 1:
            f_ref[at(b), B * (b + 1) :] = dot_f32(w, f_ref[at(b), B * (b + 1) :])
        for i in range(b + 1, n):
            u = f_ref[at(b), at(i)]
            f_ref[at(i), B * i :] -= dot_f32(u, f_ref[at(b), B * i :], 0, 0)
            if b > 0:
                f_ref[at(i), : B * b] -= dot_f32(u, f_ref[at(b), : B * b], 0, 0)
            f_ref[at(i), at(b)] = -dot_f32(u, w, 0, 0)
    for k, (i, j) in enumerate(lower_blocks(n)):
        o_ref[at(k), :] = f_ref[at(i), at(j)]


def project_kernel(core_ref, x_ref, y_ref, wm_ref, wo_ref, cm_ref, co_ref, px_ref, py_ref, cross_ref, wx_ref, wy_ref, c_ref):
    width = x_ref.shape[1]
    n = width // B
    half = width // 2
    core = core_ref[0]
    at = lambda i: slice(B * i, B * (i + 1))

    def unpack(w_x, w_y, c_0, c_1):
        for k, (i, j) in enumerate(lower_blocks(n)):
            wx_ref[at(i), at(j)] = w_x[at(k), :]
            wy_ref[at(i), at(j)] = w_y[at(k), :]
        for j in range(half // B):
            c_ref[:, B * j : B * (j + 1)] = c_0[width * j : width * (j + 1), :]
            c_ref[:, half + B * j : half + B * (j + 1)] = c_1[width * j : width * (j + 1), :]

    @pl.when(core == 0)
    def _():
        unpack(wm_ref, wo_ref, cm_ref, co_ref)

    @pl.when(core == 1)
    def _():
        unpack(wo_ref, wm_ref, co_ref, cm_ref)

    c_hl = split2(c_ref[...])
    left = []
    for i in range(n):
        k = B * (i + 1)
        left.append(dot_x3(split2(wx_ref[at(i), :k]), [e[:k] for e in c_hl]))
    left = split2(jnp.concatenate(left, 0))
    for j in range(n):
        k = B * (j + 1)
        cross_ref[:, at(j)] = dot_x3([e[:, :k] for e in left], split2(wy_ref[at(j), :k]), 1, 1)
    cross = split2(cross_ref[...])
    map_x, map_y = [], []
    for i in range(n):
        k = B * i
        map_x.append(dot_x3(split2(wx_ref[k:, at(i)]), [e[k:] for e in cross], 0, 0))
        map_y.append(dot_x3([e[:, k:] for e in cross], split2(wy_ref[k:, at(i)])))
    high, low = split2(jnp.concatenate(map_x, 0))
    px_ref[...] = (dot(x_ref[...], high) + dot(x_ref[...], low)).astype(BF)
    high, low = split2(jnp.concatenate(map_y, 1))
    py_ref[...] = (dot(y_ref[...], high, 1, 1) + dot(y_ref[...], low, 1, 1)).astype(BF)


def params():
    return pltpu.CompilerParams(vmem_limit_bytes=VMEM_LIMIT)


def reduce_scatter(v, axis, n, step, index):
    rows = v.shape[0] // n
    block = lambda k: lax.dynamic_slice_in_dim(v, k * rows, rows, 0)
    total = block(index)
    for m in range(1, n):
        pairs = [(i, i ^ (m * step)) for i in range(n * step)]
        total = total + lax.ppermute(block(index ^ m), axis, pairs)
    return total


def all_gather(v, axis, n, step, index):
    parts = [v]
    for m in range(1, n):
        pairs = [(i, i ^ (m * step)) for i in range(n * step)]
        parts.append(lax.ppermute(v, axis, pairs))
    parts = jnp.stack(parts)
    return jnp.concatenate([lax.dynamic_index_in_dim(parts, index ^ k, 0, keepdims=False) for k in range(n)], 0)


def on_device(x_states, y_states):
    rows, width = x_states.shape
    n = width // B
    gr, gc = lax.axis_size("gr"), lax.axis_size("gc")
    chips = gr // 2
    total_rows = rows * gr * gc
    core = lax.axis_index("gr") % 2
    chip = lax.axis_index("gr") // 2
    plane = lax.axis_index("gc")
    swap = lambda v: lax.ppermute(v, "gr", [(i, i ^ 1) for i in range(gr)])
    core_arg = jnp.reshape(core, (1,)).astype(jnp.int32)
    smem = pl.BlockSpec(memory_space=pltpu.SMEM)
    vmem = pl.BlockSpec(memory_space=pltpu.VMEM)

    tri = B * len(upper_blocks(n))
    packed = tri + width * width // 2 // B

    def gram(partner):
        return pl.pallas_call(
            lambda *refs: gram_kernel(partner, *refs),
            out_shape=jax.ShapeDtypeStruct((packed, B), F32),
            in_specs=[smem, vmem, vmem],
            out_specs=vmem,
            scratch_shapes=[pltpu.VMEM((rows, width), BF)],
            compiler_params=params(),
            cost_estimate=pl.CostEstimate(flops=2 * rows * packed * B, bytes_accessed=4 * rows * width, transcendentals=0),
            name="gram_partner" if partner else "gram_own",
        )(core_arg, x_states, y_states)

    sums = swap(gram(True))
    sums = gram(False) + sums
    sums = reduce_scatter(sums, "gr", chips, 2, chip)
    sums = reduce_scatter(sums, "gc", gc, 1, plane)
    sums = all_gather(sums, "gc", gc, 1, plane)
    sums = all_gather(sums, "gr", chips, 2, chip)

    cov_xy = sums[tri:] / total_rows
    cov_xy_other = swap(cov_xy)
    white = pl.pallas_call(
        lambda *refs: factor_kernel(float(total_rows), n, *refs),
        out_shape=jax.ShapeDtypeStruct((tri, B), F32),
        in_specs=[vmem],
        out_specs=vmem,
        scratch_shapes=[pltpu.VMEM((width, width), F32)],
        compiler_params=params(),
        cost_estimate=pl.CostEstimate(flops=20_000_000_000, bytes_accessed=8 * tri * B, transcendentals=0),
        name="factor",
    )(sums[:tri])
    white_other = swap(white)

    return pl.pallas_call(
        project_kernel,
        out_shape=(
            jax.ShapeDtypeStruct((rows, width), BF),
            jax.ShapeDtypeStruct((rows, width), BF),
            jax.ShapeDtypeStruct((width, width), F32),
        ),
        in_specs=[smem] + [vmem] * 6,
        out_specs=(vmem,) * 3,
        scratch_shapes=[pltpu.VMEM((width, width), F32)] * 3,
        compiler_params=params(),
        cost_estimate=pl.CostEstimate(flops=8 * rows * width * width, bytes_accessed=16 * rows * width, transcendentals=0),
        name="project",
    )(core_arg, x_states, y_states, white, white_other, cov_xy, cov_xy_other)


def solution(mesh):
    return jax.shard_map(
        on_device,
        mesh=mesh,
        in_specs=(P(("gr", "gc"), None), P(("gr", "gc"), None)),
        out_specs=(P(("gr", "gc"), None), P(("gr", "gc"), None), P()),
        check_vma=False,
    )
```

time: 510 us -> 94.1 us (0.18)
  other arithmetic: 252 us -> 4.42 us
  waiting for transfers between devices: 102 us -> 37.9 us
  matrix products: 60.8 us -> 0 us
  local copies, waits for them, and re-layouts: 52.7 us -> 4.3 us
  Pallas kernels: 0 us -> 28.7 us
  between operations: 19.7 us -> 0.76 us
  blocking collectives: 18.4 us -> 0 us
  starting transfers between devices: 0.12 us -> 17.7 us
    another operation x33 -> x3, other arithmetic: 240 us -> 0.85 us  [all_gather(): parts = jnp.stack(parts)]
    unnamed x4 -> x0, waiting for transfers between devices: 49.1 us -> none
    another operation x40 -> x0, matrix products: 44.5 us -> none  [the longest x7 11.3 us: on_device(): jax.scipy.linalg.solve_triangular(low_x, x_states.astype(jnp.float32).T,...]
    ppermute x0 -> x15, waiting for transfers between devices: none -> 37.9 us  [the longest x6 21.6 us: reduce_scatter(): total = total + lax.ppermute(block(index ^ m), axis, pairs)]
    another operation x35 -> x0, local copies, waits for them, and re-layouts: 29.6 us -> none  [the longest x15 15.5 us: on_device(): jax.scipy.linalg.solve_triangular(low_x, x_states.astype(jnp.float32).T,...]
    pallas_call x0 -> x4, Pallas kernels: none -> 28.7 us  [the longest x1 18.3 us: on_device(): pl.pallas_call(lambda *refs: factor_kernel(float(total_rows), n, *refs),...]
    all_gather x1 -> x0, waiting for transfers between devices: 28.5 us -> none  [on_device(): sums = lax.all_gather(row_block, 'gr', axis=0, tiled=True)]
    reduce_scatter x1 -> x0, waiting for transfers between devices: 24.1 us -> none  [on_device(): tile = lax.psum_scatter(partial_rows, 'gc', scatter_dimension=1, tiled=True)]
  transfers between devices with their start and end apart: 3 -> 15, of which waited for: 3 -> 12; matrix products, arithmetic and copies ran while one was open for 1% -> 0% of each run, Pallas kernels for 0% -> 1%
where the time goes in v1:
time: 94.1 us; the launch traced here: 93.8 us
  waiting for transfers between devices  37.9 us (40%)
  Pallas kernels  28.7 us (30%)
  starting transfers between devices  17.7 us (19%)
  other arithmetic  4.42 us (5%)
  local copies, waits for them, and re-layouts  4.3 us (5%)
    ppermute x6, waiting for transfers between devices, reduce_scatter(): total = total + lax.ppermute(block(index ^ m), axis, pairs)  21.6 us
    pallas_call x1, Pallas kernels, on_device(): pl.pallas_call(lambda *refs: factor_kernel(float(total_rows), n, *refs),...  18.3 us
    ppermute x6, waiting for transfers between devices, all_gather(): parts.append(lax.ppermute(v, axis, pairs))  12.5 us
    ppermute x6, starting transfers between devices, reduce_scatter(): total = total + lax.ppermute(block(index ^ m), axis, pairs)  8.61 us
    pallas_call x1, Pallas kernels, on_device(): pl.pallas_call(project_kernel, out_shape=(jax.ShapeDtypeStruct((rows, wid...  8.49 us
    ppermute x6, starting transfers between devices, all_gather(): parts.append(lax.ppermute(v, axis, pairs))  7.94 us
    ppermute x3, waiting for transfers between devices, on_device(): swap = lambda v: lax.ppermute(v, 'gr', [(i, i ^ 1) for i in range(gr)])  3.82 us
    unnamed x10, local copies, waits for them, and re-layouts  3.22 us
  transfers between devices with their start and end apart: 15, of which 12 were waited for; matrix products, arithmetic and copies ran while one was open for 0% of the time, Pallas kernels for 1%

profile of v1, /device:TPU:0, one launch (start us, length us, event | category | flops | bytes accessed | tf_op | source)
XLA Modules:
  0.0 93.8 jit_solution(6742395477720710776)
XLA Ops:
  0.6 0.0 copy-start
  0.7 1.2 %copy-done = bf16[1024,512]{1,0:T(8,128)(2,1)S(1)} copy-done((bf16[1024,512]{1,0:T(8,128)(2,1)S(1)}, bf16[1024,512]{1,0:T(8,128)(2,1)}, u32[]{:S(2)}) %copy-start) | copy-done | bytes 1048600
  1.9 1.2 %copy-done.2 = bf16[1024,512]{1,0:T(8,128)(2,1)S(1)} copy-done((bf16[1024,512]{1,0:T(8,128)(2,1)S(1)}, bf16[1024,512]{1,0:T(8,128)(2,1)}, u32[]{:S(2)}) %copy-start.2) | copy-done | bytes 1048600
  3.1 1.0 %gram_partner.1 = f32[2304,128]{1,0:T(8,128)S(1)} custom-call(s32[1]{0:T(128)} %bitcast.refs_0_.core_ref, bf16[1024,512]{1,0:T(8,128)(2,1)S(1)} %copy-done, bf16[1024,512]{1,0:T(8,128)(2,1)S(1)} %copy-done.2), custom_call_target="tpu_custom_call" | custom-call | flops 603979776 | bytes 2097152 | tf_op jit(solution)/shard_map/gram_partner/pallas_call | solution.py:226
  4.1 0.5 collective-permute-start
  4.6 0.0 copy-done.1
  4.6 0.1 copy-done.3
  4.6 0.9 %gram_own.1 = f32[2304,128]{1,0:T(8,128)S(1)} custom-call(s32[1]{0:T(128)} %bitcast.refs_0_.core_ref, bf16[1024,512]{1,0:T(8,128)(2,1)S(1)} %copy-done.1, bf16[1024,512]{1,0:T(8,128)(2,1)S(1)} %copy-done.3), custom_call_target="tpu_custom_call" | custom-call | flops 603979776 | bytes 2097152 | tf_op jit(solution)/shard_map/gram_own/pallas_call | solution.py:226
  5.6 1.6 %collective-permute-done = f32[2304,128]{1,0:T(8,128)} collective-permute-done((f32[2304,128]{1,0:T(8,128)S(1)}, f32[2304,128]{1,0:T(8,128)}, u32[]{:S(2)}, u32[]{:S(2)}) %collective-permute-start) | collective-permute-done | bytes 1179680 | tf_op jit(solution)/shard_map/ppermute | solution.py:217
  7.2 1.4 %add.77 = f32[2304,128]{1,0:T(8,128)S(1)} add(f32[2304,128]{1,0:T(8,128)S(1)} %gram_own.1, f32[2304,128]{1,0:T(8,128)} %collective-permute-done) | non-fusion elementwise | flops 294912 | bytes 3538944 | tf_op jit(solution)/shard_map/add | solution.py:238
  8.6 0.9 %constant_dynamic-slice_fusion.5 = (f32[576,128]{1,0:T(8,128)}, f32[576,128]{1,0:T(8,128)}, f32[576,128]{1,0:T(8,128)}) fusion(f32[2304,128]{1,0:T(8,128)S(1)} %add.77, s32[]{:T(128)S(6)} %select_n.64, s32[]{:T(128)S(6)} %select_n.66, s32[]{:T(128)S(6)} %select_n.65), kind=kLoop, calls=%fused_computation.22 | loop fusion | bytes 1769484 | tf_op jit(solution)/shard_map/dynamic_slice | solution.py:191
  9.5 2.9 %collective-permute-start.1 = (f32[576,128]{1,0:T(8,128)}, f32[576,128]{1,0:T(8,128)}, u32[]{:S(2)}, u32[]{:S(2)}) collective-permute-start(f32[576,128]{1,0:T(8,128)} %get-tuple-element.7), channel_id=1, source_target_pairs={{0,8},{4,12},{8,0},{12,4},{16,24},{20,28},{24,16},{28,20},{1,9},{5... | collective-permute-start | bytes 884744 | tf_op jit(solution)/shard_map/ppermute | solution.py:195
  12.4 1.5 %collective-permute-start.3 = (f32[576,128]{1,0:T(8,128)}, f32[576,128]{1,0:T(8,128)}, u32[]{:S(2)}, u32[]{:S(2)}) collective-permute-start(f32[576,128]{1,0:T(8,128)} %get-tuple-element.8), channel_id=1, source_target_pairs={{0,24},{4,28},{8,16},{12,20},{16,8},{20,12},{24,0},{28,4},{1,25},{... | collective-permute-start | bytes 884744 | tf_op jit(solution)/shard_map/ppermute | solution.py:195
  13.9 0.0 collective-permute-start.2
  13.9 6.6 %collective-permute-done.1 = f32[576,128]{1,0:T(8,128)} collective-permute-done((f32[576,128]{1,0:T(8,128)}, f32[576,128]{1,0:T(8,128)}, u32[]{:S(2)}, u32[]{:S(2)}) %collective-permute-start.1) | collective-permute-done | bytes 294944 | tf_op jit(solution)/shard_map/ppermute | solution.py:195
  20.5 7.2 %collective-permute-done.3 = f32[576,128]{1,0:T(8,128)} collective-permute-done((f32[576,128]{1,0:T(8,128)}, f32[576,128]{1,0:T(8,128)}, u32[]{:S(2)}, u32[]{:S(2)}) %collective-permute-start.3) | collective-permute-done | bytes 294944 | tf_op jit(solution)/shard_map/ppermute | solution.py:195
  27.6 1.4 %collective-permute-done.2 = f32[576,128]{1,0:T(8,128)} collective-permute-done((f32[576,128]{1,0:T(8,128)}, f32[576,128]{1,0:T(8,128)}, u32[]{:S(2)}, u32[]{:S(2)}) %collective-permute-start.2) | collective-permute-done | bytes 294944 | tf_op jit(solution)/shard_map/ppermute | solution.py:195
  29.0 1.2 %add_add_fusion = f32[576,128]{1,0:T(8,128)S(1)} fusion(f32[576,128]{1,0:T(8,128)} %collective-permute-done.3, f32[576,128]{1,0:T(8,128)} %collective-permute-done.2, f32[576,128]{1,0:T(8,128)} %collective-permute-done.1, f32[2304,128]{1,0:T(8,128)S(1)} %add.77, s32[]{:T(128)S(6)} %select_n.63), kind=kLoop, calls=%fused_computation.11 | loop fusion | flops 221184 | bytes 1474564 | tf_op jit(solution)/shard_map/add | solution.py:195
  30.2 0.0 copy-start.4
  30.2 0.7 copy-done.4
  30.9 1.6 %collective-permute-start.4 = (f32[144,128]{1,0:T(8,128)S(1)}, f32[144,128]{1,0:T(8,128)S(1)}, u32[]{:S(2)}, u32[]{:S(2)}) collective-permute-start(f32[144,128]{1,0:T(8,128)S(1)} %get-tuple-element.16), channel_id=1, source_target_pairs={{0,1},{1,0},{2,3},{3,2},{4,5},{5,4},{6,7},{7,6},{8,9},{9,8},{10,11... | collective-permute-start | bytes 221192 | tf_op jit(solution)/shard_map/ppermute | solution.py:195
  32.6 2.5 %collective-permute-start.6 = (f32[144,128]{1,0:T(8,128)S(1)}, f32[144,128]{1,0:T(8,128)S(1)}, u32[]{:S(2)}, u32[]{:S(2)}) collective-permute-start(f32[144,128]{1,0:T(8,128)S(1)} %get-tuple-element.17), channel_id=1, source_target_pairs={{0,3},{1,2},{2,1},{3,0},{4,7},{5,6},{6,5},{7,4},{8,11},{9,10},{10,... | collective-permute-start | bytes 221192 | tf_op jit(solution)/shard_map/ppermute | solution.py:195
  35.0 0.1 collective-permute-start.5
  35.2 1.2 %collective-permute-done.4 = f32[144,128]{1,0:T(8,128)S(1)} collective-permute-done((f32[144,128]{1,0:T(8,128)S(1)}, f32[144,128]{1,0:T(8,128)S(1)}, u32[]{:S(2)}, u32[]{:S(2)}) %collective-permute-start.4) | collective-permute-done | bytes 73760 | tf_op jit(solution)/shard_map/ppermute | solution.py:195
  36.4 2.5 %collective-permute-done.6 = f32[144,128]{1,0:T(8,128)S(1)} collective-permute-done((f32[144,128]{1,0:T(8,128)S(1)}, f32[144,128]{1,0:T(8,128)S(1)}, u32[]{:S(2)}, u32[]{:S(2)}) %collective-permute-start.6) | collective-permute-done | bytes 73760 | tf_op jit(solution)/shard_map/ppermute | solution.py:195
  38.8 2.8 %collective-permute-done.5 = f32[144,128]{1,0:T(8,128)S(1)} collective-permute-done((f32[144,128]{1,0:T(8,128)S(1)}, f32[144,128]{1,0:T(8,128)S(1)}, u32[]{:S(2)}, u32[]{:S(2)}) %collective-permute-start.5) | collective-permute-done | bytes 73760 | tf_op jit(solution)/shard_map/ppermute | solution.py:195
  41.7 0.9 add_add_fusion.1
  42.6 1.2 %collective-permute-start.9 = (f32[144,128]{1,0:T(8,128)S(1)}, f32[144,128]{1,0:T(8,128)S(1)}, u32[]{:S(2)}, u32[]{:S(2)}) collective-permute-start(f32[144,128]{1,0:T(8,128)S(1)} %add_add_fusion.1), channel_id=1, source_target_pairs={{0,3},{1,2},{2,1},{3,0},{4,7},{5,6},{6,5},{7,4},{8,11},{9,10},{10,... | collective-permute-start | bytes 221192 | tf_op jit(solution)/shard_map/ppermute | solution.py:203
  43.8 0.0 collective-permute-start.8
  43.8 3.3 %collective-permute-start.7 = (f32[144,128]{1,0:T(8,128)S(1)}, f32[144,128]{1,0:T(8,128)S(1)}, u32[]{:S(2)}, u32[]{:S(2)}) collective-permute-start(f32[144,128]{1,0:T(8,128)S(1)} %add_add_fusion.1), channel_id=1, source_target_pairs={{0,1},{1,0},{2,3},{3,2},{4,5},{5,4},{6,7},{7,6},{8,9},{9,8},{10,11... | collective-permute-start | bytes 221192 | tf_op jit(solution)/shard_map/ppermute | solution.py:203
  47.0 1.9 %collective-permute-done.9 = f32[144,128]{1,0:T(8,128)S(1)} collective-permute-done((f32[144,128]{1,0:T(8,128)S(1)}, f32[144,128]{1,0:T(8,128)S(1)}, u32[]{:S(2)}, u32[]{:S(2)}) %collective-permute-start.9) | collective-permute-done | bytes 73760 | tf_op jit(solution)/shard_map/ppermute | solution.py:203
  48.9 1.5 %collective-permute-done.8 = f32[144,128]{1,0:T(8,128)S(1)} collective-permute-done((f32[144,128]{1,0:T(8,128)S(1)}, f32[144,128]{1,0:T(8,128)S(1)}, u32[]{:S(2)}, u32[]{:S(2)}) %collective-permute-start.8) | collective-permute-done | bytes 73760 | tf_op jit(solution)/shard_map/ppermute | solution.py:203
  50.4 0.0 collective-permute-done.7
  50.4 0.8 fusion.1
  51.2 0.5 collective-permute-start.11
  51.7 1.5 %collective-permute-start.10 = (f32[576,128]{1,0:T(8,128)}, f32[576,128]{1,0:T(8,128)S(1)}, u32[]{:S(2)}, u32[]{:S(2)}) collective-permute-start(f32[576,128]{1,0:T(8,128)} %get-tuple-element.11), channel_id=1, source_target_pairs={{0,8},{4,12},{8,0},{12,4},{16,24},{20,28},{24,16},{28,20},{1,9},{5... | collective-permute-start | bytes 884744 | tf_op jit(solution)/shard_map/ppermute | solution.py:203
  53.2 1.5 %collective-permute-start.12 = (f32[576,128]{1,0:T(8,128)}, f32[576,128]{1,0:T(8,128)S(1)}, u32[]{:S(2)}, u32[]{:S(2)}) collective-permute-start(f32[576,128]{1,0:T(8,128)} %get-tuple-element.11), channel_id=1, source_target_pairs={{0,24},{4,28},{8,16},{12,20},{16,8},{20,12},{24,0},{28,4},{1,25},{... | collective-permute-start | bytes 884744 | tf_op jit(solution)/shard_map/ppermute | solution.py:203
  54.7 6.0 %collective-permute-done.11 = f32[576,128]{1,0:T(8,128)S(1)} collective-permute-done((f32[576,128]{1,0:T(8,128)}, f32[576,128]{1,0:T(8,128)S(1)}, u32[]{:S(2)}, u32[]{:S(2)}) %collective-permute-start.11) | collective-permute-done | bytes 294944 | tf_op jit(solution)/shard_map/ppermute | solution.py:203
  60.7 0.0 collective-permute-done.10
  60.7 3.2 %collective-permute-done.12 = f32[576,128]{1,0:T(8,128)S(1)} collective-permute-done((f32[576,128]{1,0:T(8,128)}, f32[576,128]{1,0:T(8,128)S(1)}, u32[]{:S(2)}, u32[]{:S(2)}) %collective-permute-start.12) | collective-permute-done | bytes 294944 | tf_op jit(solution)/shard_map/ppermute | solution.py:203
  63.8 0.1 pad_maximum_fusion
  63.9 0.1 dynamic-slice_bitcast_fusion
  64.1 18.3 %factor.1.wm_ref = f32[1280,128]{1,0:T(8,128)S(1)} custom-call(f32[1280,128]{1,0:T(8,128)S(1)} %pad_maximum_fusion.1.refs_0_), custom_call_target="tpu_custom_call" | custom-call | flops 20000000000 | bytes 1310720 | tf_op jit(solution)/shard_map/factor/pallas_call | solution.py:246
  82.4 0.1 collective-permute-start.13
  82.5 0.6 collective-permute-start.14
  83.1 2.2 %collective-permute-done.14.co_ref = f32[1024,128]{1,0:T(8,128)S(1)} collective-permute-done((f32[1024,128]{1,0:T(8,128)S(1)}, f32[1024,128]{1,0:T(8,128)S(1)}, u32[]{:S(2)}, u32[]{:S(2)}) %collective-permute-start.14) | collective-permute-done | bytes 524320 | tf_op jit(solution)/shard_map/ppermute | solution.py:217
  85.3 0.0 collective-permute-done.13.wo_ref
  85.3 8.5 %project.1 = (bf16[1024,512]{1,0:T(8,128)(2,1)}, bf16[1024,512]{1,0:T(8,128)(2,1)}, f32[512,512]{1,0:T(8,128)}) custom-call(s32[1]{0:T(128)} %bitcast.refs_0_.core_ref, bf16[1024,512]{1,0:T(8,128)(2,1)S(1)} %copy-done.1, bf16[1024,512]{1,0:T(8,128)(2,1)S(1)} %copy-done.3, f32[1280,128]{1,0:T(8,128)S(1)} %factor.1.wm_ref, ...), custom_call_target="tpu_custom_call" | custom-call | flops 2147483648 | bytes 8388608 | tf_op jit(solution)/shard_map/project/pallas_call | solution.py:258
  (8 shorter events, 0.2 us)
Async XLA Ops:
  0.6 1.2 %copy-start = (bf16[1024,512]{1,0:T(8,128)(2,1)S(1)}, bf16[1024,512]{1,0:T(8,128)(2,1)}, u32[]{:S(2)}) copy-start(bf16[1024,512]{1,0:T(8,128)(2,1)} %x_ref.1) | copy-start | bytes 3145732
  1.9 1.2 %copy-start.2 = (bf16[1024,512]{1,0:T(8,128)(2,1)S(1)}, bf16[1024,512]{1,0:T(8,128)(2,1)}, u32[]{:S(2)}) copy-start(bf16[1024,512]{1,0:T(8,128)(2,1)} %y_ref.1) | copy-start | bytes 3145732
  3.1 1.5 %copy-start.1 = (bf16[1024,512]{1,0:T(8,128)(2,1)S(1)}, bf16[1024,512]{1,0:T(8,128)(2,1)}, u32[]{:S(2)}) copy-start(bf16[1024,512]{1,0:T(8,128)(2,1)} %x_ref.1) | copy-start | bytes 3145732
  3.1 1.5 %copy-start.3 = (bf16[1024,512]{1,0:T(8,128)(2,1)S(1)}, bf16[1024,512]{1,0:T(8,128)(2,1)}, u32[]{:S(2)}) copy-start(bf16[1024,512]{1,0:T(8,128)(2,1)} %y_ref.1) | copy-start | bytes 3145732
  4.1 3.1 %collective-permute-start = (f32[2304,128]{1,0:T(8,128)S(1)}, f32[2304,128]{1,0:T(8,128)}, u32[]{:S(2)}, u32[]{:S(2)}) collective-permute-start(f32[2304,128]{1,0:T(8,128)S(1)} %gram_partner.1), channel_id=1, source_target_pairs={{0,4},{4,0},{8,12},{12,8},{16,20},{20,16},{24,28},{28,24},{1,5},{5... | collective-permute-start | bytes 3538952 | tf_op jit(solution)/shard_map/ppermute | solution.py:217
  9.5 11.0 %collective-permute-start.1 = (f32[576,128]{1,0:T(8,128)}, f32[576,128]{1,0:T(8,128)}, u32[]{:S(2)}, u32[]{:S(2)}) collective-permute-start(f32[576,128]{1,0:T(8,128)} %get-tuple-element.7), channel_id=1, source_target_pairs={{0,8},{4,12},{8,0},{12,4},{16,24},{20,28},{24,16},{28,20},{1,9},{5... | collective-permute-start | bytes 884744 | tf_op jit(solution)/shard_map/ppermute | solution.py:195
  12.4 15.3 %collective-permute-start.3 = (f32[576,128]{1,0:T(8,128)}, f32[576,128]{1,0:T(8,128)}, u32[]{:S(2)}, u32[]{:S(2)}) collective-permute-start(f32[576,128]{1,0:T(8,128)} %get-tuple-element.8), channel_id=1, source_target_pairs={{0,24},{4,28},{8,16},{12,20},{16,8},{20,12},{24,0},{28,4},{1,25},{... | collective-permute-start | bytes 884744 | tf_op jit(solution)/shard_map/ppermute | solution.py:195
  13.9 15.1 %collective-permute-start.2 = (f32[576,128]{1,0:T(8,128)}, f32[576,128]{1,0:T(8,128)}, u32[]{:S(2)}, u32[]{:S(2)}) collective-permute-start(f32[576,128]{1,0:T(8,128)} %get-tuple-element.9), channel_id=1, source_target_pairs={{0,16},{4,20},{8,24},{12,28},{16,0},{20,4},{24,8},{28,12},{1,17},{... | collective-permute-start | bytes 884744 | tf_op jit(solution)/shard_map/ppermute | solution.py:195
  30.2 0.7 copy-start.4
  30.9 5.4 %collective-permute-start.4 = (f32[144,128]{1,0:T(8,128)S(1)}, f32[144,128]{1,0:T(8,128)S(1)}, u32[]{:S(2)}, u32[]{:S(2)}) collective-permute-start(f32[144,128]{1,0:T(8,128)S(1)} %get-tuple-element.16), channel_id=1, source_target_pairs={{0,1},{1,0},{2,3},{3,2},{4,5},{5,4},{6,7},{7,6},{8,9},{9,8},{10,11... | collective-permute-start | bytes 221192 | tf_op jit(solution)/shard_map/ppermute | solution.py:195
  32.6 6.3 %collective-permute-start.6 = (f32[144,128]{1,0:T(8,128)S(1)}, f32[144,128]{1,0:T(8,128)S(1)}, u32[]{:S(2)}, u32[]{:S(2)}) collective-permute-start(f32[144,128]{1,0:T(8,128)S(1)} %get-tuple-element.17), channel_id=1, source_target_pairs={{0,3},{1,2},{2,1},{3,0},{4,7},{5,6},{6,5},{7,4},{8,11},{9,10},{10,... | collective-permute-start | bytes 221192 | tf_op jit(solution)/shard_map/ppermute | solution.py:195
  35.0 6.6 %collective-permute-start.5 = (f32[144,128]{1,0:T(8,128)S(1)}, f32[144,128]{1,0:T(8,128)S(1)}, u32[]{:S(2)}, u32[]{:S(2)}) collective-permute-start(f32[144,128]{1,0:T(8,128)S(1)} %get-tuple-element.18), channel_id=1, source_target_pairs={{0,2},{1,3},{2,0},{3,1},{4,6},{5,7},{6,4},{7,5},{8,10},{9,11},{10,... | collective-permute-start | bytes 221192 | tf_op jit(solution)/shard_map/ppermute | solution.py:195
  42.6 6.3 %collective-permute-start.9 = (f32[144,128]{1,0:T(8,128)S(1)}, f32[144,128]{1,0:T(8,128)S(1)}, u32[]{:S(2)}, u32[]{:S(2)}) collective-permute-start(f32[144,128]{1,0:T(8,128)S(1)} %add_add_fusion.1), channel_id=1, source_target_pairs={{0,3},{1,2},{2,1},{3,0},{4,7},{5,6},{6,5},{7,4},{8,11},{9,10},{10,... | collective-permute-start | bytes 221192 | tf_op jit(solution)/shard_map/ppermute | solution.py:203
  43.8 6.6 %collective-permute-start.8 = (f32[144,128]{1,0:T(8,128)S(1)}, f32[144,128]{1,0:T(8,128)S(1)}, u32[]{:S(2)}, u32[]{:S(2)}) collective-permute-start(f32[144,128]{1,0:T(8,128)S(1)} %add_add_fusion.1), channel_id=1, source_target_pairs={{0,2},{1,3},{2,0},{3,1},{4,6},{5,7},{6,4},{7,5},{8,10},{9,11},{10,... | collective-permute-start | bytes 221192 | tf_op jit(solution)/shard_map/ppermute | solution.py:203
  43.8 6.6 %collective-permute-start.7 = (f32[144,128]{1,0:T(8,128)S(1)}, f32[144,128]{1,0:T(8,128)S(1)}, u32[]{:S(2)}, u32[]{:S(2)}) collective-permute-start(f32[144,128]{1,0:T(8,128)S(1)} %add_add_fusion.1), channel_id=1, source_target_pairs={{0,1},{1,0},{2,3},{3,2},{4,5},{5,4},{6,7},{7,6},{8,9},{9,8},{10,11... | collective-permute-start | bytes 221192 | tf_op jit(solution)/shard_map/ppermute | solution.py:203
  51.2 9.5 %collective-permute-start.11 = (f32[576,128]{1,0:T(8,128)}, f32[576,128]{1,0:T(8,128)S(1)}, u32[]{:S(2)}, u32[]{:S(2)}) collective-permute-start(f32[576,128]{1,0:T(8,128)} %get-tuple-element.11), channel_id=1, source_target_pairs={{0,16},{4,20},{8,24},{12,28},{16,0},{20,4},{24,8},{28,12},{1,17},{... | collective-permute-start | bytes 884744 | tf_op jit(solution)/shard_map/ppermute | solution.py:203
  51.7 9.0 %collective-permute-start.10 = (f32[576,128]{1,0:T(8,128)}, f32[576,128]{1,0:T(8,128)S(1)}, u32[]{:S(2)}, u32[]{:S(2)}) collective-permute-start(f32[576,128]{1,0:T(8,128)} %get-tuple-element.11), channel_id=1, source_target_pairs={{0,8},{4,12},{8,0},{12,4},{16,24},{20,28},{24,16},{28,20},{1,9},{5... | collective-permute-start | bytes 884744 | tf_op jit(solution)/shard_map/ppermute | solution.py:203
  53.2 10.7 %collective-permute-start.12 = (f32[576,128]{1,0:T(8,128)}, f32[576,128]{1,0:T(8,128)S(1)}, u32[]{:S(2)}, u32[]{:S(2)}) collective-permute-start(f32[576,128]{1,0:T(8,128)} %get-tuple-element.11), channel_id=1, source_target_pairs={{0,24},{4,28},{8,16},{12,20},{16,8},{20,12},{24,0},{28,4},{1,25},{... | collective-permute-start | bytes 884744 | tf_op jit(solution)/shard_map/ppermute | solution.py:203
  82.4 2.9 %collective-permute-start.13 = (f32[1280,128]{1,0:T(8,128)S(1)}, f32[1280,128]{1,0:T(8,128)S(1)}, u32[]{:S(2)}, u32[]{:S(2)}) collective-permute-start(f32[1280,128]{1,0:T(8,128)S(1)} %factor.1.wm_ref), channel_id=1, source_target_pairs={{0,4},{4,0},{8,12},{12,8},{16,20},{20,16},{24,28},{28,24},{1,5},{5... | collective-permute-start | bytes 1966088 | tf_op jit(solution)/shard_map/ppermute | solution.py:217
  82.5 2.8 %collective-permute-start.14 = (f32[1024,128]{1,0:T(8,128)S(1)}, f32[1024,128]{1,0:T(8,128)S(1)}, u32[]{:S(2)}, u32[]{:S(2)}) collective-permute-start(f32[1024,128]{1,0:T(8,128)S(1)} %fusion.cm_ref), channel_id=1, source_target_pairs={{0,4},{4,0},{8,12},{12,8},{16,20},{20,16},{24,28},{28,24},{1,5},{5... | collective-permute-start | bytes 1572872 | tf_op jit(solution)/shard_map/ppermute | solution.py:217

commit v2 on v1

--- a/solution.py
+++ b/solution.py
@@ -10,7 +10,7 @@
 NB = 16
 BF = jnp.bfloat16
 F32 = jnp.float32
-VMEM_LIMIT = 48 * 1024 * 1024
+COPIES = 8
 
 
 def dot(a, b, ca=1, cb=0, precision=None):
@@ -85,32 +85,57 @@
     return [(i, j) for i in range(n) for j in range(i + 1)]
 
 
-def gram_kernel(partner, core_ref, x_ref, y_ref, o_ref, a_ref):
-    width = x_ref.shape[1]
-    n = width // B
-    core = core_ref[0]
-    owner = 1 - core if partner else core
-
-    @pl.when(owner == 0)
-    def _():
-        a_ref[...] = x_ref[...]
-
-    @pl.when(owner == 1)
-    def _():
-        a_ref[...] = y_ref[...]
-
+def write_upper(g_ref, o_ref):
+    n = g_ref.shape[1] // B
     row = 0
     for i in range(n):
-        g = dot(a_ref[:, B * i : B * (i + 1)], a_ref[:, B * i :], 0, 0)
+        g = dot(g_ref[:, B * i : B * (i + 1)], g_ref[:, B * i :], 0, 0)
         for j in range(n - i):
             o_ref[row : row + B, :] = g[:, B * j : B * (j + 1)]
             row += B
+
+
+def gram_partner_kernel(core_ref, x_ref, y_ref, o_ref, a_ref, sems):
+    chunk = a_ref.shape[0] // COPIES
+    core = core_ref[0]
+    copies = lambda ref: [
+        pltpu.make_async_copy(ref.at[pl.ds(k * chunk, chunk)], a_ref.at[pl.ds(k * chunk, chunk)], sems.at[k])
+        for k in range(COPIES)
+    ]
+
+    @pl.when(core == 0)
+    def _():
+        for copy in copies(y_ref):
+            copy.start()
+
+    @pl.when(core == 1)
+    def _():
+        for copy in copies(x_ref):
+            copy.start()
+
+    for copy in copies(x_ref):
+        copy.wait()
+    write_upper(a_ref, o_ref)
+
+
+def gram_own_kernel(core_ref, x_ref, y_ref, o_ref, cm_ref, co_ref, a_ref):
+    width = x_ref.shape[1]
     half = width // 2
-    columns = pl.ds(pl.multiple_of(owner * half, half), half)
-    g = dot(x_ref[...], y_ref[:, columns], 0, 0)
-    for j in range(half // B):
-        o_ref[row : row + width, :] = g[:, B * j : B * (j + 1)]
-        row += width
+    core = core_ref[0]
+
+    @pl.when(core == 0)
+    def _():
+        a_ref[...] = x_ref[...]
+
+    @pl.when(core == 1)
+    def _():
+        a_ref[...] = y_ref[...]
+
+    write_upper(a_ref, o_ref)
+    for owner, c_ref in ((1 - core, co_ref), (core, cm_ref)):
+        g = dot(x_ref[...], y_ref[:, pl.ds(pl.multiple_of(owner * half, half), half)], 0, 0)
+        for j in range(half // B):
+            c_ref[width * j : width * (j + 1), :] = g[:, B * j : B * (j + 1)]
 
 
 def factor_kernel(total_rows, n, s_ref, o_ref, f_ref):
@@ -182,27 +207,34 @@
     py_ref[...] = (dot(y_ref[...], high, 1, 1) + dot(y_ref[...], low, 1, 1)).astype(BF)
 
 
-def params():
-    return pltpu.CompilerParams(vmem_limit_bytes=VMEM_LIMIT)
-
-
-def reduce_scatter(v, axis, n, step, index):
+def params(mib):
+    return pltpu.CompilerParams(vmem_limit_bytes=mib * 1024 * 1024)
+
+
+def shift(v, axis, m):
+    return lax.ppermute(v, axis, [(i, i ^ m) for i in range(lax.axis_size(axis))])
+
+
+def scatter_start(v, axis, n, step, index):
     rows = v.shape[0] // n
     block = lambda k: lax.dynamic_slice_in_dim(v, k * rows, rows, 0)
-    total = block(index)
-    for m in range(1, n):
-        pairs = [(i, i ^ (m * step)) for i in range(n * step)]
-        total = total + lax.ppermute(block(index ^ m), axis, pairs)
+    return block(index), [shift(block(index ^ m), axis, m * step) for m in range(1, n)]
+
+
+def scatter_end(state):
+    total, parts = state
+    for part in parts:
+        total = total + part
     return total
 
 
-def all_gather(v, axis, n, step, index):
-    parts = [v]
-    for m in range(1, n):
-        pairs = [(i, i ^ (m * step)) for i in range(n * step)]
-        parts.append(lax.ppermute(v, axis, pairs))
-    parts = jnp.stack(parts)
-    return jnp.concatenate([lax.dynamic_index_in_dim(parts, index ^ k, 0, keepdims=False) for k in range(n)], 0)
+def gather_start(v, axis, n, step):
+    return [v] + [shift(v, axis, m * step) for m in range(1, n)]
+
+
+def gather_end(parts, index):
+    stacked = jnp.stack(parts)
+    return jnp.concatenate([lax.dynamic_index_in_dim(stacked, index ^ k, 0, keepdims=False) for k in range(len(parts))], 0)
 
 
 def on_device(x_states, y_states):
@@ -214,46 +246,67 @@
     core = lax.axis_index("gr") % 2
     chip = lax.axis_index("gr") // 2
     plane = lax.axis_index("gc")
-    swap = lambda v: lax.ppermute(v, "gr", [(i, i ^ 1) for i in range(gr)])
     core_arg = jnp.reshape(core, (1,)).astype(jnp.int32)
     smem = pl.BlockSpec(memory_space=pltpu.SMEM)
     vmem = pl.BlockSpec(memory_space=pltpu.VMEM)
-
+    hbm = pl.BlockSpec(memory_space=pltpu.HBM)
     tri = B * len(upper_blocks(n))
-    packed = tri + width * width // 2 // B
-
-    def gram(partner):
-        return pl.pallas_call(
-            lambda *refs: gram_kernel(partner, *refs),
-            out_shape=jax.ShapeDtypeStruct((packed, B), F32),
-            in_specs=[smem, vmem, vmem],
-            out_specs=vmem,
-            scratch_shapes=[pltpu.VMEM((rows, width), BF)],
-            compiler_params=params(),
-            cost_estimate=pl.CostEstimate(flops=2 * rows * packed * B, bytes_accessed=4 * rows * width, transcendentals=0),
-            name="gram_partner" if partner else "gram_own",
-        )(core_arg, x_states, y_states)
-
-    sums = swap(gram(True))
-    sums = gram(False) + sums
-    sums = reduce_scatter(sums, "gr", chips, 2, chip)
-    sums = reduce_scatter(sums, "gc", gc, 1, plane)
-    sums = all_gather(sums, "gc", gc, 1, plane)
-    sums = all_gather(sums, "gr", chips, 2, chip)
-
-    cov_xy = sums[tri:] / total_rows
-    cov_xy_other = swap(cov_xy)
+    half = width * width // 2 // B
+
+    cov = pl.pallas_call(
+        gram_partner_kernel,
+        out_shape=jax.ShapeDtypeStruct((tri, B), F32),
+        in_specs=[smem, hbm, hbm],
+        out_specs=vmem,
+        scratch_shapes=[pltpu.VMEM((rows, width), BF), pltpu.SemaphoreType.DMA((COPIES,))],
+        compiler_params=params(6),
+        cost_estimate=pl.CostEstimate(flops=2 * rows * tri * B, bytes_accessed=2 * rows * width, transcendentals=0),
+        name="gram_partner",
+    )(core_arg, x_states, y_states)
+    x_again, y_again, cov = lax.optimization_barrier((x_states, y_states, cov))
+    cov_in = shift(cov, "gr", 1)
+    cov, cxy_own, cxy_other = pl.pallas_call(
+        gram_own_kernel,
+        out_shape=(
+            jax.ShapeDtypeStruct((tri, B), F32),
+            jax.ShapeDtypeStruct((half, B), F32),
+            jax.ShapeDtypeStruct((half, B), F32),
+        ),
+        in_specs=[smem, vmem, vmem],
+        out_specs=(vmem,) * 3,
+        scratch_shapes=[pltpu.VMEM((rows, width), BF)],
+        compiler_params=params(10),
+        cost_estimate=pl.CostEstimate(flops=2 * rows * (tri + 2 * half) * B, bytes_accessed=8 * rows * width, transcendentals=0),
+        name="gram_own",
+    )(core_arg, x_again, y_again)
+
+    cxy_in = shift(cxy_other, "gr", 1)
+    cov, cxy_own = cov + cov_in, cxy_own + cxy_in
+    blocks = lambda v: jnp.reshape(v, (chips * gc, -1, B))
+    sums = jnp.reshape(jnp.concatenate([blocks(cov), blocks(cxy_own)], 1), (-1, B))
+    sums = scatter_end(scatter_start(sums, "gr", chips, 2, chip))
+    sums = scatter_end(scatter_start(sums, "gc", gc, 1, plane))
+    sums = gather_end(gather_start(sums, "gc", gc, 1), plane)
+    sums = jnp.reshape(sums, (gc, -1, B))
+    own = tri // (chips * gc)
+    cov = gather_start(jnp.reshape(sums[:, :own], (-1, B)), "gr", chips, 2)
+    cxy = gather_start(jnp.reshape(sums[:, own:], (-1, B)), "gr", chips, 2)
+    cov = gather_end(cov, chip)
+
     white = pl.pallas_call(
         lambda *refs: factor_kernel(float(total_rows), n, *refs),
         out_shape=jax.ShapeDtypeStruct((tri, B), F32),
         in_specs=[vmem],
         out_specs=vmem,
         scratch_shapes=[pltpu.VMEM((width, width), F32)],
-        compiler_params=params(),
+        compiler_params=params(8),
         cost_estimate=pl.CostEstimate(flops=20_000_000_000, bytes_accessed=8 * tri * B, transcendentals=0),
         name="factor",
-    )(sums[:tri])
-    white_other = swap(white)
+    )(cov)
+    cxy, white = lax.optimization_barrier((cxy, white))
+    cxy = gather_end(cxy, chip) / total_rows
+    cxy_other = shift(cxy, "gr", 1)
+    white_other = shift(white, "gr", 1)
 
     return pl.pallas_call(
         project_kernel,
@@ -265,10 +318,10 @@
         in_specs=[smem] + [vmem] * 6,
         out_specs=(vmem,) * 3,
         scratch_shapes=[pltpu.VMEM((width, width), F32)] * 3,
-        compiler_params=params(),
+        compiler_params=params(32),
         cost_estimate=pl.CostEstimate(flops=8 * rows * width * width, bytes_accessed=16 * rows * width, transcendentals=0),
         name="project",
-    )(core_arg, x_states, y_states, white, white_other, cov_xy, cov_xy_other)
+    )(core_arg, x_states, y_states, white, white_other, cxy, cxy_other)
 
 
 def solution(mesh):

time: 94.1 us -> 97.6 us (1.037)
  starting transfers between devices: 17.7 us -> 22.1 us
  waiting for transfers between devices: 37.9 us -> 33.7 us
  Pallas kernels: 28.7 us -> 30.8 us
    ppermute x15 -> x19, starting transfers between devices: 17.7 us -> 22.1 us  [shift(): lax.ppermute(v, axis, [(i, i ^ m) for i in range(lax.axis_size(axis))])]
    ppermute x15 -> x19, waiting for transfers between devices: 37.9 us -> 33.7 us  [shift(): lax.ppermute(v, axis, [(i, i ^ m) for i in range(lax.axis_size(axis))])]
    pallas_call x2, Pallas kernels: 1.9 us -> 4.04 us  [the longest x1 2.03 us: on_device(): pl.pallas_call(gram_partner_kernel, out_shape=jax.ShapeDtypeStruct((tri,...]
    add x3 -> x4, other arithmetic: 3.49 us -> 4.51 us  [the longest x2 2.41 us: on_device(): cov, cxy_own = (cov + cov_in, cxy_own + cxy_in)]
    unnamed x10 -> x12, local copies, waits for them, and re-layouts: 3.22 us -> 3.95 us
  transfers between devices with their start and end apart: 15 -> 19, of which waited for: 12 -> 12; matrix products, arithmetic and copies ran while one was open for 0% -> 2% of each run, Pallas kernels for 1% -> 21%
where the time goes in v2:
time: 97.6 us; the launch traced here: 97.3 us
  waiting for transfers between devices  33.7 us (35%)
  Pallas kernels  30.8 us (32%)
  starting transfers between devices  22.1 us (23%)
  local copies, waits for them, and re-layouts  5.06 us (5%)
  other arithmetic  4.8 us (5%)
    ppermute x19, waiting for transfers between devices, shift(): lax.ppermute(v, axis, [(i, i ^ m) for i in range(lax.axis_size(axis))])  33.7 us
    ppermute x19, starting transfers between devices, shift(): lax.ppermute(v, axis, [(i, i ^ m) for i in range(lax.axis_size(axis))])  22.1 us
    pallas_call x1, Pallas kernels, on_device(): pl.pallas_call(lambda *refs: factor_kernel(float(total_rows), n, *refs),...  18.3 us
    pallas_call x1, Pallas kernels, on_device(): pl.pallas_call(project_kernel, out_shape=(jax.ShapeDtypeStruct((rows, wid...  8.49 us
    unnamed x12, local copies, waits for them, and re-layouts  3.95 us
    add x2, other arithmetic, on_device(): cov, cxy_own = (cov + cov_in, cxy_own + cxy_in)  2.41 us
    add x2, other arithmetic, scatter_end(): total = total + part  2.1 us
    pallas_call x1, Pallas kernels, on_device(): pl.pallas_call(gram_partner_kernel, out_shape=jax.ShapeDtypeStruct((tri,...  2.03 us
  transfers between devices with their start and end apart: 19, of which 12 were waited for; matrix products, arithmetic and copies ran while one was open for 2% of the time, Pallas kernels for 21%

profile of v2, /device:TPU:0, one launch (start us, length us, event | category | flops | bytes accessed | tf_op | source)
XLA Modules:
  0.0 97.3 jit_solution(15637956493188015724)
XLA Ops:
  0.7 1.2 %copy-done = bf16[1024,512]{1,0:T(8,128)(2,1)S(1)} copy-done((bf16[1024,512]{1,0:T(8,128)(2,1)S(1)}, bf16[1024,512]{1,0:T(8,128)(2,1)}, u32[]{:S(2)}) %copy-start) | copy-done | bytes 1048600
  1.9 1.2 %copy-done.2 = bf16[1024,512]{1,0:T(8,128)(2,1)S(1)} copy-done((bf16[1024,512]{1,0:T(8,128)(2,1)S(1)}, bf16[1024,512]{1,0:T(8,128)(2,1)}, u32[]{:S(2)}) %copy-start.2) | copy-done | bytes 1048600
  3.1 2.0 %gram_partner.1 = f32[1280,128]{1,0:T(8,128)S(1)} custom-call(s32[1]{0:T(128)} %bitcast.core_ref, bf16[1024,512]{1,0:T(8,128)(2,1)S(1)} %copy-done, bf16[1024,512]{1,0:T(8,128)(2,1)S(1)} %copy-done.2), custom_call_target="tpu_custom_call" | custom-call | flops 335544320 | bytes 1048576 | tf_op jit(solution)/shard_map/gram_partner/pallas_call | solution.py:256
  5.1 0.5 collective-permute-start
  5.7 2.0 %gram_own.1 = (f32[1280,128]{1,0:T(8,128)S(1)}, f32[1024,128]{1,0:T(8,128)S(1)}, f32[1024,128]{1,0:T(8,128)}) custom-call(s32[1]{0:T(128)} %bitcast.core_ref, bf16[1024,512]{1,0:T(8,128)(2,1)S(1)} %copy-done.1, bf16[1024,512]{1,0:T(8,128)(2,1)S(1)} %copy-done.3), custom_call_target="tpu_custom_call" | custom-call | flops 872415232 | bytes 4194304 | tf_op jit(solution)/shard_map/gram_own/pallas_call | solution.py:268
  7.7 0.8 copy-done.4
  8.5 0.1 collective-permute-start.1
  8.5 2.2 %collective-permute-done.1 = f32[1024,128]{1,0:T(8,128)} collective-permute-done((f32[1024,128]{1,0:T(8,128)}, f32[1024,128]{1,0:T(8,128)}, u32[]{:S(2)}, u32[]{:S(2)}) %collective-permute-start.1) | collective-permute-done | bytes 524320 | tf_op jit(solution)/shard_map/ppermute | solution.py:215
  10.7 1.3 %add.86 = f32[1024,128]{1,0:T(8,128)S(1)} add(f32[1024,128]{1,0:T(8,128)} %copy-done.4, f32[1024,128]{1,0:T(8,128)} %collective-permute-done.1) | non-fusion elementwise | flops 131072 | bytes 1572864 | tf_op jit(solution)/shard_map/add | solution.py:284
  12.0 1.2 %add.85 = f32[1280,128]{1,0:T(8,128)S(1)} add(f32[1280,128]{1,0:T(8,128)S(1)} %get-tuple-element.16, f32[1280,128]{1,0:T(8,128)} %collective-permute-done) | non-fusion elementwise | flops 163840 | bytes 1966080 | tf_op jit(solution)/shard_map/add | solution.py:284
  13.1 0.1 pad_maximum_fusion
  13.2 0.9 constant_dynamic-slice_fusion.5
  14.2 2.7 %collective-permute-start.2 = (f32[576,128]{1,0:T(8,128)}, f32[576,128]{1,0:T(8,128)}, u32[]{:S(2)}, u32[]{:S(2)}) collective-permute-start(f32[576,128]{1,0:T(8,128)} %get-tuple-element.25), channel_id=1, source_target_pairs={{0,8},{4,12},{8,0},{12,4},{16,24},{20,28},{24,16},{28,20},{1,9},{5... | collective-permute-start | bytes 884744 | tf_op jit(solution)/shard_map/ppermute | solution.py:215
  16.8 1.5 %collective-permute-start.4 = (f32[576,128]{1,0:T(8,128)}, f32[576,128]{1,0:T(8,128)}, u32[]{:S(2)}, u32[]{:S(2)}) collective-permute-start(f32[576,128]{1,0:T(8,128)} %get-tuple-element.26), channel_id=1, source_target_pairs={{0,24},{4,28},{8,16},{12,20},{16,8},{20,12},{24,0},{28,4},{1,25},{... | collective-permute-start | bytes 884744 | tf_op jit(solution)/shard_map/ppermute | solution.py:215
  18.3 0.0 collective-permute-start.3
  18.3 6.6 %collective-permute-done.2 = f32[576,128]{1,0:T(8,128)} collective-permute-done((f32[576,128]{1,0:T(8,128)}, f32[576,128]{1,0:T(8,128)}, u32[]{:S(2)}, u32[]{:S(2)}) %collective-permute-start.2) | collective-permute-done | bytes 294944 | tf_op jit(solution)/shard_map/ppermute | solution.py:215
  25.0 7.3 %collective-permute-done.4 = f32[576,128]{1,0:T(8,128)} collective-permute-done((f32[576,128]{1,0:T(8,128)}, f32[576,128]{1,0:T(8,128)}, u32[]{:S(2)}, u32[]{:S(2)}) %collective-permute-start.4) | collective-permute-done | bytes 294944 | tf_op jit(solution)/shard_map/ppermute | solution.py:215
  32.3 1.4 %collective-permute-done.3 = f32[576,128]{1,0:T(8,128)} collective-permute-done((f32[576,128]{1,0:T(8,128)}, f32[576,128]{1,0:T(8,128)}, u32[]{:S(2)}, u32[]{:S(2)}) %collective-permute-start.3) | collective-permute-done | bytes 294944 | tf_op jit(solution)/shard_map/ppermute | solution.py:215
  33.7 1.2 %add_add_fusion = f32[576,128]{1,0:T(8,128)S(1)} fusion(f32[576,128]{1,0:T(8,128)} %collective-permute-done.4, f32[576,128]{1,0:T(8,128)} %collective-permute-done.3, f32[576,128]{1,0:T(8,128)} %collective-permute-done.2, f32[2304,128]{1,0:T(8,128)S(1)} %bitcast.44, s32[]{:T(128)S(6)} %select_n.68), kind=kLoop, calls=%fused_computation.7 | loop fusion | flops 221184 | bytes 1474564 | tf_op jit(solution)/shard_map/add | solution.py:227
  34.9 0.0 copy-start.5
  34.9 0.7 copy-done.5
  35.6 1.6 %collective-permute-start.5 = (f32[144,128]{1,0:T(8,128)S(1)}, f32[144,128]{1,0:T(8,128)S(1)}, u32[]{:S(2)}, u32[]{:S(2)}) collective-permute-start(f32[144,128]{1,0:T(8,128)S(1)} %get-tuple-element.40), channel_id=1, source_target_pairs={{0,1},{1,0},{2,3},{3,2},{4,5},{5,4},{6,7},{7,6},{8,9},{9,8},{10,11... | collective-permute-start | bytes 221192 | tf_op jit(solution)/shard_map/ppermute | solution.py:215
  37.2 2.5 %collective-permute-start.7 = (f32[144,128]{1,0:T(8,128)S(1)}, f32[144,128]{1,0:T(8,128)S(1)}, u32[]{:S(2)}, u32[]{:S(2)}) collective-permute-start(f32[144,128]{1,0:T(8,128)S(1)} %get-tuple-element.41), channel_id=1, source_target_pairs={{0,3},{1,2},{2,1},{3,0},{4,7},{5,6},{6,5},{7,4},{8,11},{9,10},{10,... | collective-permute-start | bytes 221192 | tf_op jit(solution)/shard_map/ppermute | solution.py:215
  39.7 0.1 collective-permute-start.6
  39.8 0.2 collective-permute-done.5
  40.0 3.6 %collective-permute-done.7 = f32[144,128]{1,0:T(8,128)S(1)} collective-permute-done((f32[144,128]{1,0:T(8,128)S(1)}, f32[144,128]{1,0:T(8,128)S(1)}, u32[]{:S(2)}, u32[]{:S(2)}) %collective-permute-start.7) | collective-permute-done | bytes 73760 | tf_op jit(solution)/shard_map/ppermute | solution.py:215
  43.6 2.5 %collective-permute-done.6 = f32[144,128]{1,0:T(8,128)S(1)} collective-permute-done((f32[144,128]{1,0:T(8,128)S(1)}, f32[144,128]{1,0:T(8,128)S(1)}, u32[]{:S(2)}, u32[]{:S(2)}) %collective-permute-start.6) | collective-permute-done | bytes 73760 | tf_op jit(solution)/shard_map/ppermute | solution.py:215
  46.1 0.9 add_add_fusion.1
  47.0 2.4 %collective-permute-start.10 = (f32[144,128]{1,0:T(8,128)S(1)}, f32[144,128]{1,0:T(8,128)S(1)}, u32[]{:S(2)}, u32[]{:S(2)}) collective-permute-start(f32[144,128]{1,0:T(8,128)S(1)} %add_add_fusion.1), channel_id=1, source_target_pairs={{0,3},{1,2},{2,1},{3,0},{4,7},{5,6},{6,5},{7,4},{8,11},{9,10},{10,... | collective-permute-start | bytes 221192 | tf_op jit(solution)/shard_map/ppermute | solution.py:215
  49.4 0.0 collective-permute-start.9
  49.4 2.1 %collective-permute-start.8 = (f32[144,128]{1,0:T(8,128)S(1)}, f32[144,128]{1,0:T(8,128)S(1)}, u32[]{:S(2)}, u32[]{:S(2)}) collective-permute-start(f32[144,128]{1,0:T(8,128)S(1)} %add_add_fusion.1), channel_id=1, source_target_pairs={{0,1},{1,0},{2,3},{3,2},{4,5},{5,4},{6,7},{7,6},{8,9},{9,8},{10,11... | collective-permute-start | bytes 221192 | tf_op jit(solution)/shard_map/ppermute | solution.py:215
  51.5 2.7 %collective-permute-done.10 = f32[144,128]{1,0:T(8,128)S(1)} collective-permute-done((f32[144,128]{1,0:T(8,128)S(1)}, f32[144,128]{1,0:T(8,128)S(1)}, u32[]{:S(2)}, u32[]{:S(2)}) %collective-permute-start.10) | collective-permute-done | bytes 73760 | tf_op jit(solution)/shard_map/ppermute | solution.py:215
  54.2 1.6 %collective-permute-done.9 = f32[144,128]{1,0:T(8,128)S(1)} collective-permute-done((f32[144,128]{1,0:T(8,128)S(1)}, f32[144,128]{1,0:T(8,128)S(1)}, u32[]{:S(2)}, u32[]{:S(2)}) %collective-permute-start.9) | collective-permute-done | bytes 73760 | tf_op jit(solution)/shard_map/ppermute | solution.py:215
  55.8 1.5 %collective-permute-start.16 = (f32[320,128]{1,0:T(8,128)S(1)}, f32[320,128]{1,0:T(8,128)S(1)}, u32[]{:S(2)}, u32[]{:S(2)}) collective-permute-start(f32[320,128]{1,0:T(8,128)S(1)} %bitcast.49), channel_id=1, source_target_pairs={{0,24},{4,28},{8,16},{12,20},{16,8},{20,12},{24,0},{28,4},{1,25},{... | collective-permute-start | bytes 491528 | tf_op jit(solution)/shard_map/ppermute | solution.py:215
  57.3 1.5 %collective-permute-start.15 = (f32[320,128]{1,0:T(8,128)S(1)}, f32[320,128]{1,0:T(8,128)S(1)}, u32[]{:S(2)}, u32[]{:S(2)}) collective-permute-start(f32[320,128]{1,0:T(8,128)S(1)} %bitcast.50), channel_id=1, source_target_pairs={{0,16},{4,20},{8,24},{12,28},{16,0},{20,4},{24,8},{28,12},{1,17},{... | collective-permute-start | bytes 491528 | tf_op jit(solution)/shard_map/ppermute | solution.py:215
  58.9 0.5 collective-permute-start.14
  59.4 1.5 %collective-permute-start.13 = (f32[256,128]{1,0:T(8,128)S(1)}, f32[256,128]{1,0:T(8,128)S(1)}, u32[]{:S(2)}, u32[]{:S(2)}) collective-permute-start(f32[256,128]{1,0:T(8,128)S(1)} %bitcast.53), channel_id=1, source_target_pairs={{0,24},{4,28},{8,16},{12,20},{16,8},{20,12},{24,0},{28,4},{1,25},{... | collective-permute-start | bytes 393224 | tf_op jit(solution)/shard_map/ppermute | solution.py:215
  60.9 1.5 %collective-permute-start.12 = (f32[256,128]{1,0:T(8,128)S(1)}, f32[256,128]{1,0:T(8,128)S(1)}, u32[]{:S(2)}, u32[]{:S(2)}) collective-permute-start(f32[256,128]{1,0:T(8,128)S(1)} %bitcast.54), channel_id=1, source_target_pairs={{0,16},{4,20},{8,24},{12,28},{16,0},{20,4},{24,8},{28,12},{1,17},{... | collective-permute-start | bytes 393224 | tf_op jit(solution)/shard_map/ppermute | solution.py:215
  62.4 1.5 %collective-permute-done.16 = f32[320,128]{1,0:T(8,128)S(1)} collective-permute-done((f32[320,128]{1,0:T(8,128)S(1)}, f32[320,128]{1,0:T(8,128)S(1)}, u32[]{:S(2)}, u32[]{:S(2)}) %collective-permute-start.16) | collective-permute-done | bytes 163872 | tf_op jit(solution)/shard_map/ppermute | solution.py:215
  64.0 1.5 %collective-permute-start.11 = (f32[256,128]{1,0:T(8,128)S(1)}, f32[256,128]{1,0:T(8,128)S(1)}, u32[]{:S(2)}, u32[]{:S(2)}) collective-permute-start(f32[256,128]{1,0:T(8,128)S(1)} %bitcast.55), channel_id=1, source_target_pairs={{0,8},{4,12},{8,0},{12,4},{16,24},{20,28},{24,16},{28,20},{1,9},{5... | collective-permute-start | bytes 393224 | tf_op jit(solution)/shard_map/ppermute | solution.py:215
  65.4 1.9 %collective-permute-done.15 = f32[320,128]{1,0:T(8,128)S(1)} collective-permute-done((f32[320,128]{1,0:T(8,128)S(1)}, f32[320,128]{1,0:T(8,128)S(1)}, u32[]{:S(2)}, u32[]{:S(2)}) %collective-permute-start.15) | collective-permute-done | bytes 163872 | tf_op jit(solution)/shard_map/ppermute | solution.py:215
  67.4 0.1 dynamic-slice_bitcast_fusion.3
  67.5 18.3 %factor.1.wm_ref = f32[1280,128]{1,0:T(8,128)S(1)} custom-call(f32[1280,128]{1,0:T(8,128)S(1)} %pad_maximum_fusion.2.refs_0_), custom_call_target="tpu_custom_call" | custom-call | flops 20000000000 | bytes 1310720 | tf_op jit(solution)/shard_map/factor/pallas_call | solution.py:296
  85.8 0.0 collective-permute-done.13
  85.9 0.1 collective-permute-start.17
  86.1 0.6 collective-permute-start.18
  86.6 2.1 %collective-permute-done.18.co_ref = f32[1024,128]{1,0:T(8,128)S(1)} collective-permute-done((f32[1024,128]{1,0:T(8,128)S(1)}, f32[1024,128]{1,0:T(8,128)S(1)}, u32[]{:S(2)}, u32[]{:S(2)}) %collective-permute-start.18) | collective-permute-done | bytes 524320 | tf_op jit(solution)/shard_map/ppermute | solution.py:215
  88.8 8.5 %project.1 = (bf16[1024,512]{1,0:T(8,128)(2,1)}, bf16[1024,512]{1,0:T(8,128)(2,1)}, f32[512,512]{1,0:T(8,128)}) custom-call(s32[1]{0:T(128)} %bitcast.core_ref, bf16[1024,512]{1,0:T(8,128)(2,1)S(1)} %copy-done.1, bf16[1024,512]{1,0:T(8,128)(2,1)S(1)} %copy-done.3, f32[1280,128]{1,0:T(8,128)S(1)} %factor.1.wm_ref, ...), custom_call_target="tpu_custom_call" | custom-call | flops 2147483648 | bytes 8388608 | tf_op jit(solution)/shard_map/project/pallas_call | solution.py:311
  (24 shorter events, 0.4 us)
Async XLA Ops:
  0.6 1.2 %copy-start = (bf16[1024,512]{1,0:T(8,128)(2,1)S(1)}, bf16[1024,512]{1,0:T(8,128)(2,1)}, u32[]{:S(2)}) copy-start(bf16[1024,512]{1,0:T(8,128)(2,1)} %x_ref.4) | copy-start | bytes 3145732
  1.9 1.2 %copy-start.2 = (bf16[1024,512]{1,0:T(8,128)(2,1)S(1)}, bf16[1024,512]{1,0:T(8,128)(2,1)}, u32[]{:S(2)}) copy-start(bf16[1024,512]{1,0:T(8,128)(2,1)} %y_ref.4) | copy-start | bytes 3145732
  3.1 2.6 %copy-start.1 = (bf16[1024,512]{1,0:T(8,128)(2,1)S(1)}, bf16[1024,512]{1,0:T(8,128)(2,1)}, u32[]{:S(2)}) copy-start(bf16[1024,512]{1,0:T(8,128)(2,1)} %x_ref.4) | copy-start | bytes 3145732
  3.1 2.6 %copy-start.3 = (bf16[1024,512]{1,0:T(8,128)(2,1)S(1)}, bf16[1024,512]{1,0:T(8,128)(2,1)}, u32[]{:S(2)}) copy-start(bf16[1024,512]{1,0:T(8,128)(2,1)} %y_ref.4) | copy-start | bytes 3145732
  5.1 6.8 %collective-permute-start = (f32[1280,128]{1,0:T(8,128)S(1)}, f32[1280,128]{1,0:T(8,128)}, u32[]{:S(2)}, u32[]{:S(2)}) collective-permute-start(f32[1280,128]{1,0:T(8,128)S(1)} %gram_partner.1), channel_id=1, source_target_pairs={{0,4},{4,0},{8,12},{12,8},{16,20},{20,16},{24,28},{28,24},{1,5},{5... | collective-permute-start | bytes 1966088 | tf_op jit(solution)/shard_map/ppermute | solution.py:215
  7.7 0.8 copy-start.4
  8.5 2.3 %collective-permute-start.1 = (f32[1024,128]{1,0:T(8,128)}, f32[1024,128]{1,0:T(8,128)}, u32[]{:S(2)}, u32[]{:S(2)}) collective-permute-start(f32[1024,128]{1,0:T(8,128)} %get-tuple-element.19), channel_id=1, source_target_pairs={{0,4},{4,0},{8,12},{12,8},{16,20},{20,16},{24,28},{28,24},{1,5},{5... | collective-permute-start | bytes 1572872 | tf_op jit(solution)/shard_map/ppermute | solution.py:215
  14.2 10.8 %collective-permute-start.2 = (f32[576,128]{1,0:T(8,128)}, f32[576,128]{1,0:T(8,128)}, u32[]{:S(2)}, u32[]{:S(2)}) collective-permute-start(f32[576,128]{1,0:T(8,128)} %get-tuple-element.25), channel_id=1, source_target_pairs={{0,8},{4,12},{8,0},{12,4},{16,24},{20,28},{24,16},{28,20},{1,9},{5... | collective-permute-start | bytes 884744 | tf_op jit(solution)/shard_map/ppermute | solution.py:215
  16.8 15.5 %collective-permute-start.4 = (f32[576,128]{1,0:T(8,128)}, f32[576,128]{1,0:T(8,128)}, u32[]{:S(2)}, u32[]{:S(2)}) collective-permute-start(f32[576,128]{1,0:T(8,128)} %get-tuple-element.26), channel_id=1, source_target_pairs={{0,24},{4,28},{8,16},{12,20},{16,8},{20,12},{24,0},{28,4},{1,25},{... | collective-permute-start | bytes 884744 | tf_op jit(solution)/shard_map/ppermute | solution.py:215
  18.3 15.3 %collective-permute-start.3 = (f32[576,128]{1,0:T(8,128)}, f32[576,128]{1,0:T(8,128)}, u32[]{:S(2)}, u32[]{:S(2)}) collective-permute-start(f32[576,128]{1,0:T(8,128)} %get-tuple-element.27), channel_id=1, source_target_pairs={{0,16},{4,20},{8,24},{12,28},{16,0},{20,4},{24,8},{28,12},{1,17},{... | collective-permute-start | bytes 884744 | tf_op jit(solution)/shard_map/ppermute | solution.py:215
  34.9 0.7 copy-start.5
  35.6 4.4 %collective-permute-start.5 = (f32[144,128]{1,0:T(8,128)S(1)}, f32[144,128]{1,0:T(8,128)S(1)}, u32[]{:S(2)}, u32[]{:S(2)}) collective-permute-start(f32[144,128]{1,0:T(8,128)S(1)} %get-tuple-element.40), channel_id=1, source_target_pairs={{0,1},{1,0},{2,3},{3,2},{4,5},{5,4},{6,7},{7,6},{8,9},{9,8},{10,11... | collective-permute-start | bytes 221192 | tf_op jit(solution)/shard_map/ppermute | solution.py:215
  37.2 6.4 %collective-permute-start.7 = (f32[144,128]{1,0:T(8,128)S(1)}, f32[144,128]{1,0:T(8,128)S(1)}, u32[]{:S(2)}, u32[]{:S(2)}) collective-permute-start(f32[144,128]{1,0:T(8,128)S(1)} %get-tuple-element.41), channel_id=1, source_target_pairs={{0,3},{1,2},{2,1},{3,0},{4,7},{5,6},{6,5},{7,4},{8,11},{9,10},{10,... | collective-permute-start | bytes 221192 | tf_op jit(solution)/shard_map/ppermute | solution.py:215
  39.7 6.4 %collective-permute-start.6 = (f32[144,128]{1,0:T(8,128)S(1)}, f32[144,128]{1,0:T(8,128)S(1)}, u32[]{:S(2)}, u32[]{:S(2)}) collective-permute-start(f32[144,128]{1,0:T(8,128)S(1)} %get-tuple-element.42), channel_id=1, source_target_pairs={{0,2},{1,3},{2,0},{3,1},{4,6},{5,7},{6,4},{7,5},{8,10},{9,11},{10,... | collective-permute-start | bytes 221192 | tf_op jit(solution)/shard_map/ppermute | solution.py:215
  47.0 7.2 %collective-permute-start.10 = (f32[144,128]{1,0:T(8,128)S(1)}, f32[144,128]{1,0:T(8,128)S(1)}, u32[]{:S(2)}, u32[]{:S(2)}) collective-permute-start(f32[144,128]{1,0:T(8,128)S(1)} %add_add_fusion.1), channel_id=1, source_target_pairs={{0,3},{1,2},{2,1},{3,0},{4,7},{5,6},{6,5},{7,4},{8,11},{9,10},{10,... | collective-permute-start | bytes 221192 | tf_op jit(solution)/shard_map/ppermute | solution.py:215
  49.4 6.4 %collective-permute-start.9 = (f32[144,128]{1,0:T(8,128)S(1)}, f32[144,128]{1,0:T(8,128)S(1)}, u32[]{:S(2)}, u32[]{:S(2)}) collective-permute-start(f32[144,128]{1,0:T(8,128)S(1)} %add_add_fusion.1), channel_id=1, source_target_pairs={{0,2},{1,3},{2,0},{3,1},{4,6},{5,7},{6,4},{7,5},{8,10},{9,11},{10,... | collective-permute-start | bytes 221192 | tf_op jit(solution)/shard_map/ppermute | solution.py:215
  49.4 6.4 %collective-permute-start.8 = (f32[144,128]{1,0:T(8,128)S(1)}, f32[144,128]{1,0:T(8,128)S(1)}, u32[]{:S(2)}, u32[]{:S(2)}) collective-permute-start(f32[144,128]{1,0:T(8,128)S(1)} %add_add_fusion.1), channel_id=1, source_target_pairs={{0,1},{1,0},{2,3},{3,2},{4,5},{5,4},{6,7},{7,6},{8,9},{9,8},{10,11... | collective-permute-start | bytes 221192 | tf_op jit(solution)/shard_map/ppermute | solution.py:215
  55.8 8.1 %collective-permute-start.16 = (f32[320,128]{1,0:T(8,128)S(1)}, f32[320,128]{1,0:T(8,128)S(1)}, u32[]{:S(2)}, u32[]{:S(2)}) collective-permute-start(f32[320,128]{1,0:T(8,128)S(1)} %bitcast.49), channel_id=1, source_target_pairs={{0,24},{4,28},{8,16},{12,20},{16,8},{20,12},{24,0},{28,4},{1,25},{... | collective-permute-start | bytes 491528 | tf_op jit(solution)/shard_map/ppermute | solution.py:215
  57.3 10.0 %collective-permute-start.15 = (f32[320,128]{1,0:T(8,128)S(1)}, f32[320,128]{1,0:T(8,128)S(1)}, u32[]{:S(2)}, u32[]{:S(2)}) collective-permute-start(f32[320,128]{1,0:T(8,128)S(1)} %bitcast.50), channel_id=1, source_target_pairs={{0,16},{4,20},{8,24},{12,28},{16,0},{20,4},{24,8},{28,12},{1,17},{... | collective-permute-start | bytes 491528 | tf_op jit(solution)/shard_map/ppermute | solution.py:215
  58.9 8.5 %collective-permute-start.14 = (f32[320,128]{1,0:T(8,128)S(1)}, f32[320,128]{1,0:T(8,128)S(1)}, u32[]{:S(2)}, u32[]{:S(2)}) collective-permute-start(f32[320,128]{1,0:T(8,128)S(1)} %bitcast.51), channel_id=1, source_target_pairs={{0,8},{4,12},{8,0},{12,4},{16,24},{20,28},{24,16},{28,20},{1,9},{5... | collective-permute-start | bytes 491528 | tf_op jit(solution)/shard_map/ppermute | solution.py:215
  59.4 26.4 %collective-permute-start.13 = (f32[256,128]{1,0:T(8,128)S(1)}, f32[256,128]{1,0:T(8,128)S(1)}, u32[]{:S(2)}, u32[]{:S(2)}) collective-permute-start(f32[256,128]{1,0:T(8,128)S(1)} %bitcast.53), channel_id=1, source_target_pairs={{0,24},{4,28},{8,16},{12,20},{16,8},{20,12},{24,0},{28,4},{1,25},{... | collective-permute-start | bytes 393224 | tf_op jit(solution)/shard_map/ppermute | solution.py:215
  60.9 24.9 %collective-permute-start.12 = (f32[256,128]{1,0:T(8,128)S(1)}, f32[256,128]{1,0:T(8,128)S(1)}, u32[]{:S(2)}, u32[]{:S(2)}) collective-permute-start(f32[256,128]{1,0:T(8,128)S(1)} %bitcast.54), channel_id=1, source_target_pairs={{0,16},{4,20},{8,24},{12,28},{16,0},{20,4},{24,8},{28,12},{1,17},{... | collective-permute-start | bytes 393224 | tf_op jit(solution)/shard_map/ppermute | solution.py:215
  64.0 21.9 %collective-permute-start.11 = (f32[256,128]{1,0:T(8,128)S(1)}, f32[256,128]{1,0:T(8,128)S(1)}, u32[]{:S(2)}, u32[]{:S(2)}) collective-permute-start(f32[256,128]{1,0:T(8,128)S(1)} %bitcast.55), channel_id=1, source_target_pairs={{0,8},{4,12},{8,0},{12,4},{16,24},{20,28},{24,16},{28,20},{1,9},{5... | collective-permute-start | bytes 393224 | tf_op jit(solution)/shard_map/ppermute | solution.py:215
  85.9 2.9 %collective-permute-start.17 = (f32[1280,128]{1,0:T(8,128)S(1)}, f32[1280,128]{1,0:T(8,128)S(1)}, u32[]{:S(2)}, u32[]{:S(2)}) collective-permute-start(f32[1280,128]{1,0:T(8,128)S(1)} %factor.1.wm_ref), channel_id=1, source_target_pairs={{0,4},{4,0},{8,12},{12,8},{16,20},{20,16},{24,28},{28,24},{1,5},{5... | collective-permute-start | bytes 1966088 | tf_op jit(solution)/shard_map/ppermute | solution.py:215
  86.1 2.7 %collective-permute-start.18 = (f32[1024,128]{1,0:T(8,128)S(1)}, f32[1024,128]{1,0:T(8,128)S(1)}, u32[]{:S(2)}, u32[]{:S(2)}) collective-permute-start(f32[1024,128]{1,0:T(8,128)S(1)} %maximum_multiply_fusion.cm_ref), channel_id=1, source_target_pairs={{0,4},{4,0},{8,12},{12,8},{16,20},{20,16},{24,28},{28,24},{1,5},{5... | collective-permute-start | bytes 1572872 | tf_op jit(solution)/shard_map/ppermute | solution.py:215

commit v3 on v2

v3 whole, which is shorter than its diff:
```python
import jax
import jax.numpy as jnp
from jax import lax
from jax.experimental import pallas as pl
from jax.experimental.pallas import tpu as pltpu
from jax.sharding import PartitionSpec as P

RIDGE = 0.1
B = 128
NB = 16
TILE = 8
BF = jnp.bfloat16
F32 = jnp.float32
CHUNKS = 2


def dot(a, b, ca=1, cb=0, precision=None):
    return lax.dot_general(a, b, (((ca,), (cb,)), ((), ())), preferred_element_type=F32, precision=precision)


def dot_f32(a, b, ca=1, cb=0):
    return dot(a, b, ca, cb, lax.Precision.HIGHEST)


def split2(a):
    high = a.astype(BF)
    return high, (a - high.astype(F32)).astype(BF)


def split3(a):
    high = a.astype(BF)
    rest = a - high.astype(F32)
    mid = rest.astype(BF)
    return high, mid, (rest - mid.astype(F32)).astype(BF)


def dot_x3(a, b, ca=1, cb=0):
    ah, al = a
    bh, bl = b
    return dot(jnp.concatenate([ah, ah, al], ca), jnp.concatenate([bh, bl, bh], cb), ca, cb)


def outer_sum(u, v):
    uh, um, ul = split3(u)
    vh, vm, vl = split3(v)
    a = jnp.concatenate([uh, uh, um, uh, ul, um], 0)
    b = jnp.concatenate([vh, vm, vh, vl, vh, vm], 0)
    return dot(a, b, 0, 0)


def inverse_factor(a, beside=()):
    beside = list(beside)
    n = a.shape[0]
    panels = n // NB
    r = lax.broadcasted_iota(jnp.int32, (n, n), 0)
    c = lax.broadcasted_iota(jnp.int32, (n, n), 1)
    z = jnp.where(r == c, 1.0, 0.0).astype(F32)
    sublane = lax.broadcasted_iota(jnp.int32, (TILE, n), 0)
    tiles = lambda a, z: [(a[k : k + TILE], z[k : k + TILE]) for k in range(0, NB, TILE)]
    now, later, rest = tiles(a[:NB], z[:NB]), tiles(a[NB : 2 * NB], z[NB : 2 * NB]), (a[2 * NB :], z[2 * NB :])
    out = []
    for s in range(panels):
        last = s == panels - 1
        groups = now if last else now + later
        left = [g[0] for g in groups]
        right = [g[1] for g in groups]
        cols = [[jnp.broadcast_to(g[:, NB * s + q : NB * s + q + 1], (TILE, n)) for q in range(NB)] for g in left]
        pivots = [jnp.ones((TILE, n), F32) for _ in now]
        for k in range(NB):
            tile, sub = divmod(k, TILE)
            row = lambda v: v[sub : sub + 1, :]
            d = row(cols[tile][k])
            pivots[tile] = jnp.where(sublane == sub, d, pivots[tile])
            inverse = 1.0 / d
            left_row, right_row = row(left[tile]), row(right[tile])
            entries = {q: row(cols[tile][q]) for q in range(k + 1, NB)}
            for g in range(tile, len(groups)):
                if g == tile and sub == TILE - 1:
                    continue
                m = cols[g][k] * inverse
                if g == tile:
                    m = jnp.where(sublane > sub, m, 0.0)
                for q in range(k + 1, NB):
                    cols[g][q] = cols[g][q] - m * entries[q]
                left[g] = left[g] - m * left_row
                right[g] = right[g] - m * right_row
        scales = [lax.rsqrt(p) for p in pivots]
        u = jnp.concatenate([v * scale for v, scale in zip(left, scales)], 0)
        v = jnp.concatenate([v * scale for v, scale in zip(right, scales)], 0)
        out.append(v)
        now = list(zip(left, right))[len(now) :]
        if s < panels - 2:
            update = outer_sum(u[:, NB * (s + 2) :], jnp.concatenate([u, v], 1))
            a, z = rest[0] - update[:, :n], rest[1] - update[:, n:]
            later, rest = tiles(a[:NB], z[:NB]), (a[NB:], z[NB:])
        if beside:
            beside.pop(0)()
    for work in beside:
        work()
    return jnp.concatenate(out, 0)


def upper_blocks(n):
    return [(i, j) for i in range(n) for j in range(i, n)]


def lower_blocks(n):
    return [(i, j) for i in range(n) for j in range(i + 1)]


def gram_kernel(core_ref, x_ref, y_ref, other_ref, own_ref, a_ref):
    width = x_ref.shape[1]
    half = width // 2
    n = width // B
    core = core_ref[0]
    for owner, o_ref in ((1 - core, other_ref), (core, own_ref)):

        @pl.when(owner == 0)
        def _():
            a_ref[...] = x_ref[...]

        @pl.when(owner == 1)
        def _():
            a_ref[...] = y_ref[...]

        row = 0
        for i in range(n):
            g = dot(a_ref[:, B * i : B * (i + 1)], a_ref[:, B * i :], 0, 0)
            for j in range(n - i):
                o_ref[row : row + B, :] = g[:, B * j : B * (j + 1)]
                row += B
        g = dot(x_ref[...], y_ref[:, pl.ds(pl.multiple_of(owner * half, half), half)], 0, 0)
        for j in range(half // B):
            o_ref[row : row + width, :] = g[:, B * j : B * (j + 1)]
            row += width


def factor_kernel(total_rows, n, s_ref, o_ref, f_ref):
    r = lax.broadcasted_iota(jnp.int32, (B, B), 0)
    c = lax.broadcasted_iota(jnp.int32, (B, B), 1)
    ridge = jnp.where(r == c, RIDGE, 0.0).astype(F32)
    at = lambda i: slice(B * i, B * (i + 1))
    for k, (i, j) in enumerate(upper_blocks(n)):
        block = s_ref[at(k), :] / total_rows
        f_ref[at(i), at(j)] = block + ridge if i == j else block
    beside = []
    a = f_ref[at(0), at(0)]
    for b in range(n):
        w = inverse_factor(a, beside)
        f_ref[at(b), at(b)] = w
        if b == n - 1:
            f_ref[at(b), : B * b] = dot_f32(w, f_ref[at(b), : B * b])
            break
        u = dot_f32(w, f_ref[at(b), at(b + 1)])
        f_ref[at(b), at(b + 1)] = u
        a = f_ref[at(b + 1), at(b + 1)] - dot_f32(u, u, 0, 0)

        def rows(b=b, w=w):
            if b > 0:
                f_ref[at(b), : B * b] = dot_f32(w, f_ref[at(b), : B * b])
            if b + 2 < n:
                f_ref[at(b), B * (b + 2) :] = dot_f32(w, f_ref[at(b), B * (b + 2) :])

        def below(i, b=b, w=w):
            u = f_ref[at(b), at(i)]
            first = B * i if i > b + 1 else B * (i + 1)
            if first < B * n:
                f_ref[at(i), first:] -= dot_f32(u, f_ref[at(b), first:], 0, 0)
            if b > 0:
                f_ref[at(i), : B * b] -= dot_f32(u, f_ref[at(b), : B * b], 0, 0)
            f_ref[at(i), at(b)] = -dot_f32(u, w, 0, 0)

        beside = [rows] + [lambda i=i, below=below: below(i) for i in range(b + 1, n)]
    for k, (i, j) in enumerate(lower_blocks(n)):
        o_ref[at(k), :] = f_ref[at(i), at(j)]


def project_kernel(
    core_ref, x_ref, y_ref, wm_ref, wo_ref, cm_ref, co_ref, px_hbm, py_hbm, cross_hbm,
    px_ref, py_ref, cross_ref, wx_ref, wy_ref, c_ref, sems,
):
    rows, width = x_ref.shape
    n = width // B
    half = width // 2
    core = core_ref[0]
    at = lambda i: slice(B * i, B * (i + 1))

    def unpack(w_x, w_y, c_0, c_1):
        for k, (i, j) in enumerate(lower_blocks(n)):
            wx_ref[at(i), at(j)] = w_x[at(k), :]
            wy_ref[at(i), at(j)] = w_y[at(k), :]
        for j in range(half // B):
            c_ref[:, B * j : B * (j + 1)] = c_0[width * j : width * (j + 1), :]
            c_ref[:, half + B * j : half + B * (j + 1)] = c_1[width * j : width * (j + 1), :]

    @pl.when(core == 0)
    def _():
        unpack(wm_ref, wo_ref, cm_ref, co_ref)

    @pl.when(core == 1)
    def _():
        unpack(wo_ref, wm_ref, co_ref, cm_ref)

    c_hl = split2(c_ref[...])
    left = []
    for i in range(n):
        k = B * (i + 1)
        left.append(dot_x3(split2(wx_ref[at(i), :k]), [e[:k] for e in c_hl]))
    left = split2(jnp.concatenate(left, 0))
    for j in range(n):
        k = B * (j + 1)
        cross_ref[:, at(j)] = dot_x3([e[:, :k] for e in left], split2(wy_ref[at(j), :k]), 1, 1)
    copies = [pltpu.make_async_copy(cross_ref, cross_hbm, sems.at[0])]
    copies[0].start()
    cross = split2(cross_ref[...])
    map_x, map_y = [], []
    for i in range(n):
        k = B * i
        map_x.append(dot_x3(split2(wx_ref[k:, at(i)]), [e[k:] for e in cross], 0, 0))
        map_y.append(dot_x3([e[:, k:] for e in cross], split2(wy_ref[k:, at(i)])))
    map_x, map_y = jnp.concatenate(map_x, 0), jnp.concatenate(map_y, 1)
    step = rows // CHUNKS
    for ref, p_ref, p_hbm, m, cb in ((x_ref, px_ref, px_hbm, map_x, 0), (y_ref, py_ref, py_hbm, map_y, 1)):
        m = jnp.concatenate(split2(m), cb)
        for k in range(CHUNKS):
            part = pl.ds(k * step, step)
            v = ref[part, :]
            p_ref[part, :] = dot(jnp.concatenate([v, v], 1), m, 1, cb).astype(BF)
            copies.append(pltpu.make_async_copy(p_ref.at[part], p_hbm.at[part], sems.at[len(copies)]))
            copies[-1].start()
    for copy in copies:
        copy.wait()


def params(mib):
    return pltpu.CompilerParams(vmem_limit_bytes=mib * 1024 * 1024)


def shift(v, axis, m):
    return lax.ppermute(v, axis, [(i, i ^ m) for i in range(lax.axis_size(axis))])


def scatter_start(v, axis, n, step, index):
    rows = v.shape[0] // n
    block = lambda k: lax.dynamic_slice_in_dim(v, k * rows, rows, 0)
    return block(index), [shift(block(index ^ m), axis, m * step) for m in range(1, n)]


def scatter_end(state):
    total, parts = state
    for part in parts:
        total = total + part
    return total


def gather_start(v, axis, n, step):
    return [v] + [shift(v, axis, m * step) for m in range(1, n)]


def gather_end(parts, place):
    stacked = jnp.stack(parts)
    return jnp.concatenate([lax.dynamic_index_in_dim(stacked, p, 0, keepdims=False) for p in place], 0)


def plane_scatter(v, chips, core, chip):
    bits = chips.bit_length() - 1
    for s in range(bits):
        masks = 1 << s, 1 << (bits - 1 - s)
        mask = jnp.where(core == 0, *masks)
        bit = (chip & mask) // mask
        rows = v.shape[0] // 2
        half = lambda k: lax.dynamic_slice_in_dim(v, k * rows, rows, 0)
        pairs = [(i, i ^ (2 * masks[i % 2])) for i in range(2 * chips)]
        v = half(bit) + lax.ppermute(half(1 - bit), "gr", pairs)
    reverse = lambda k: sum(((k >> b) & 1) << (bits - 1 - b) for b in range(bits))
    return v, [chip ^ jnp.where(core == 0, reverse(k), k) for k in range(chips)]


def on_device(x_states, y_states):
    rows, width = x_states.shape
    n = width // B
    gr, gc = lax.axis_size("gr"), lax.axis_size("gc")
    chips = gr // 2
    total_rows = rows * gr * gc
    core = lax.axis_index("gr") % 2
    chip = lax.axis_index("gr") // 2
    plane = lax.axis_index("gc")
    core_arg = jnp.reshape(core, (1,)).astype(jnp.int32)
    smem = pl.BlockSpec(memory_space=pltpu.SMEM)
    vmem = pl.BlockSpec(memory_space=pltpu.VMEM)
    hbm = pl.BlockSpec(memory_space=pltpu.HBM)
    tri = B * len(upper_blocks(n))
    half = width * width // 2 // B

    panel = pltpu.VMEM((rows, width), BF)

    other, own = pl.pallas_call(
        gram_kernel,
        out_shape=(jax.ShapeDtypeStruct((tri + half, B), F32),) * 2,
        in_specs=[smem, vmem, vmem],
        out_specs=(vmem,) * 2,
        scratch_shapes=[panel],
        compiler_params=params(10),
        cost_estimate=pl.CostEstimate(flops=4 * rows * (tri + half) * B, bytes_accessed=8 * rows * width, transcendentals=0),
        name="gram",
    )(core_arg, x_states, y_states)
    sums = own + shift(other, "gr", 1)
    cov, cxy = sums[:tri], sums[tri:]
    blocks = lambda v: jnp.reshape(v, (chips * gc, -1, B))
    sums = jnp.reshape(jnp.concatenate([blocks(cov), blocks(cxy)], 1), (-1, B))
    sums, place = plane_scatter(sums, chips, core, chip)
    sums = scatter_end(scatter_start(sums, "gc", gc, 1, plane))
    sums = gather_end(gather_start(sums, "gc", gc, 1), [plane ^ k for k in range(gc)])
    sums = jnp.reshape(sums, (gc, -1, B))
    own = tri // (chips * gc)
    cov = gather_start(jnp.reshape(sums[:, :own], (-1, B)), "gr", chips, 2)
    cxy = gather_start(jnp.reshape(sums[:, own:], (-1, B)), "gr", chips, 2)
    cov = gather_end(cov, place)

    white = pl.pallas_call(
        lambda *refs: factor_kernel(float(total_rows), n, *refs),
        out_shape=jax.ShapeDtypeStruct((tri, B), F32),
        in_specs=[vmem],
        out_specs=vmem,
        scratch_shapes=[pltpu.VMEM((width, width), F32)],
        compiler_params=params(8),
        cost_estimate=pl.CostEstimate(flops=20_000_000_000, bytes_accessed=8 * tri * B, transcendentals=0),
        name="factor",
    )(cov)
    cxy, white = lax.optimization_barrier((cxy, white))
    cxy = gather_end(cxy, place) / total_rows
    cxy_other = shift(cxy, "gr", 1)
    white_other = shift(white, "gr", 1)

    return pl.pallas_call(
        project_kernel,
        out_shape=(
            jax.ShapeDtypeStruct((rows, width), BF),
            jax.ShapeDtypeStruct((rows, width), BF),
            jax.ShapeDtypeStruct((width, width), F32),
        ),
        in_specs=[smem] + [vmem] * 6,
        out_specs=(hbm,) * 3,
        scratch_shapes=[panel] * 2 + [pltpu.VMEM((width, width), F32)] * 4 + [pltpu.SemaphoreType.DMA((1 + 2 * CHUNKS,))],
        compiler_params=params(24),
        cost_estimate=pl.CostEstimate(flops=8 * rows * width * width, bytes_accessed=16 * rows * width, transcendentals=0),
        name="project",
    )(core_arg, x_states, y_states, white, white_other, cxy, cxy_other)


def solution(mesh):
    return jax.shard_map(
        on_device,
        mesh=mesh,
        in_specs=(P(("gr", "gc"), None), P(("gr", "gc"), None)),
        out_specs=(P(("gr", "gc"), None), P(("gr", "gc"), None), P()),
        check_vma=False,
    )
```

time: 97.6 us -> 79.7 us (0.82)
  Pallas kernels: 30.8 us -> 23 us
  waiting for transfers between devices: 33.7 us -> 29.2 us
  other arithmetic: 4.8 us -> 0.52 us
  local copies, waits for them, and re-layouts: 5.06 us -> 2.8 us
    ppermute x19 -> x15, waiting for transfers between devices: 33.7 us -> 16.6 us  [shift(): lax.ppermute(v, axis, [(i, i ^ m) for i in range(lax.axis_size(axis))])]
    ppermute x0 -> x2, waiting for transfers between devices: none -> 12.6 us  [plane_scatter(): v = half(bit) + lax.ppermute(half(1 - bit), 'gr', pairs)]
    ppermute x0 -> x2, starting transfers between devices: none -> 5.04 us  [plane_scatter(): v = half(bit) + lax.ppermute(half(1 - bit), 'gr', pairs)]
    pallas_call x1, Pallas kernels: 18.3 us -> 13.7 us  [on_device(): pl.pallas_call(lambda *refs: factor_kernel(float(total_rows), n, *refs),...]
    ppermute x19 -> x15, starting transfers between devices: 22.1 us -> 17.9 us  [shift(): lax.ppermute(v, axis, [(i, i ^ m) for i in range(lax.axis_size(axis))])]
    add x2 -> x3, other arithmetic: 2.41 us -> 0.21 us  [the longest x1 0.12 us: on_device(): sums = own + shift(other, 'gr', 1)]
    pallas_call x2 -> x1, Pallas kernels: 4.04 us -> 1.92 us  [on_device(): pl.pallas_call(gram_kernel, out_shape=(jax.ShapeDtypeStruct((tri + half,...]
    add x2 -> x1, other arithmetic: 2.1 us -> 0.02 us  [scatter_end(): total = total + part]
  transfers between devices with their start and end apart: 19 -> 17, of which waited for: 12 -> 10; matrix products, arithmetic and copies ran while one was open for 2% -> 0% of each run, Pallas kernels for 21% -> 17%
where the time goes in v3:
time: 79.7 us; the launch traced here: 79.5 us
  waiting for transfers between devices  29.2 us (37%)
  Pallas kernels  23 us (29%)
  starting transfers between devices  23 us (29%)
  local copies, waits for them, and re-layouts  2.8 us (4%)
  between operations  1.03 us (1%)
    ppermute x15, starting transfers between devices, shift(): lax.ppermute(v, axis, [(i, i ^ m) for i in range(lax.axis_size(axis))])  17.9 us
    ppermute x15, waiting for transfers between devices, shift(): lax.ppermute(v, axis, [(i, i ^ m) for i in range(lax.axis_size(axis))])  16.6 us
    pallas_call x1, Pallas kernels, on_device(): pl.pallas_call(lambda *refs: factor_kernel(float(total_rows), n, *refs),...  13.7 us
    ppermute x2, waiting for transfers between devices, plane_scatter(): v = half(bit) + lax.ppermute(half(1 - bit), 'gr', pairs)  12.6 us
    pallas_call x1, Pallas kernels, on_device(): pl.pallas_call(project_kernel, out_shape=(jax.ShapeDtypeStruct((rows, wid...  7.36 us
    ppermute x2, starting transfers between devices, plane_scatter(): v = half(bit) + lax.ppermute(half(1 - bit), 'gr', pairs)  5.04 us
    unnamed x8, local copies, waits for them, and re-layouts  2.46 us
    pallas_call x1, Pallas kernels, on_device(): pl.pallas_call(gram_kernel, out_shape=(jax.ShapeDtypeStruct((tri + half,...  1.92 us
  transfers between devices with their start and end apart: 17, of which 10 were waited for; matrix products, arithmetic and copies ran while one was open for 0% of the time, Pallas kernels for 17%

profile of v3, /device:TPU:0, one launch (start us, length us, event | category | flops | bytes accessed | tf_op | source)
XLA Modules:
  0.0 79.5 jit_solution(17339047317566845376)
XLA Ops:
  0.6 0.0 copy-start
  0.7 1.2 %copy-done = bf16[1024,512]{1,0:T(8,128)(2,1)S(1)} copy-done((bf16[1024,512]{1,0:T(8,128)(2,1)S(1)}, bf16[1024,512]{1,0:T(8,128)(2,1)}, u32[]{:S(2)}) %copy-start) | copy-done | bytes 1048600
  1.9 1.2 %copy-done.2 = bf16[1024,512]{1,0:T(8,128)(2,1)S(1)} copy-done((bf16[1024,512]{1,0:T(8,128)(2,1)S(1)}, bf16[1024,512]{1,0:T(8,128)(2,1)}, u32[]{:S(2)}) %copy-start.2) | copy-done | bytes 1048600
  3.1 1.9 %gram.1 = (f32[2304,128]{1,0:T(8,128)S(1)}, f32[2304,128]{1,0:T(8,128)S(1)}) custom-call(s32[1]{0:T(128)} %bitcast.core_ref, bf16[1024,512]{1,0:T(8,128)(2,1)S(1)} %copy-done, bf16[1024,512]{1,0:T(8,128)(2,1)S(1)} %copy-done.2), custom_call_target="tpu_custom_call" | custom-call | flops 1207959552 | bytes 4194304 | tf_op jit(solution)/shard_map/gram/pallas_call | solution.py:297
  5.0 0.5 collective-permute-start
  5.5 2.5 %collective-permute-done = f32[2304,128]{1,0:T(8,128)S(1)} collective-permute-done((f32[2304,128]{1,0:T(8,128)S(1)}, f32[2304,128]{1,0:T(8,128)S(1)}, u32[]{:S(2)}, u32[]{:S(2)}) %collective-permute-start) | collective-permute-done | bytes 1179680 | tf_op jit(solution)/shard_map/ppermute | solution.py:240
  8.0 0.1 add.81
  8.2 0.1 pad_maximum_fusion
  8.4 2.9 %collective-permute-start.1 = (f32[1152,128]{1,0:T(8,128)S(1)}, f32[1152,128]{1,0:T(8,128)S(1)}, u32[]{:S(2)}, u32[]{:S(2)}) collective-permute-start(f32[1152,128]{1,0:T(8,128)S(1)} %constant_dynamic-slice_fusion.4), channel_id=1, source_target_pairs={{0,8},{4,20},{8,0},{12,28},{16,24},{20,4},{24,16},{28,12},{1,9},{5... | collective-permute-start | bytes 1769480 | tf_op jit(solution)/shard_map/ppermute | solution.py:274
  11.3 7.9 %collective-permute-done.1 = f32[1152,128]{1,0:T(8,128)S(1)} collective-permute-done((f32[1152,128]{1,0:T(8,128)S(1)}, f32[1152,128]{1,0:T(8,128)S(1)}, u32[]{:S(2)}, u32[]{:S(2)}) %collective-permute-start.1) | collective-permute-done | bytes 589856 | tf_op jit(solution)/shard_map/ppermute | solution.py:274
  19.2 0.1 dynamic-slice_add_fusion
  19.3 2.1 %collective-permute-start.2 = (f32[576,128]{1,0:T(8,128)S(1)}, f32[576,128]{1,0:T(8,128)S(1)}, u32[]{:S(2)}, u32[]{:S(2)}) collective-permute-start(f32[576,128]{1,0:T(8,128)S(1)} %constant_dynamic-slice_fusion.3), channel_id=1, source_target_pairs={{0,16},{4,12},{8,24},{12,4},{16,0},{20,28},{24,8},{28,20},{1,17},{... | collective-permute-start | bytes 884744 | tf_op jit(solution)/shard_map/ppermute | solution.py:274
  21.4 4.7 %collective-permute-done.2 = f32[576,128]{1,0:T(8,128)S(1)} collective-permute-done((f32[576,128]{1,0:T(8,128)S(1)}, f32[576,128]{1,0:T(8,128)S(1)}, u32[]{:S(2)}, u32[]{:S(2)}) %collective-permute-start.2) | collective-permute-done | bytes 294944 | tf_op jit(solution)/shard_map/ppermute | solution.py:274
  26.1 2.1 %collective-permute-start.3 = (f32[144,128]{1,0:T(8,128)S(1)}, f32[144,128]{1,0:T(8,128)S(1)}, u32[]{:S(2)}, u32[]{:S(2)}) collective-permute-start(f32[144,128]{1,0:T(8,128)S(1)} %get-tuple-element.29), channel_id=1, source_target_pairs={{0,1},{1,0},{2,3},{3,2},{4,5},{5,4},{6,7},{7,6},{8,9},{9,8},{10,11... | collective-permute-start | bytes 221192 | tf_op jit(solution)/shard_map/ppermute | solution.py:240
  28.3 2.5 %collective-permute-start.5 = (f32[144,128]{1,0:T(8,128)S(1)}, f32[144,128]{1,0:T(8,128)S(1)}, u32[]{:S(2)}, u32[]{:S(2)}) collective-permute-start(f32[144,128]{1,0:T(8,128)S(1)} %get-tuple-element.30), channel_id=1, source_target_pairs={{0,3},{1,2},{2,1},{3,0},{4,7},{5,6},{6,5},{7,4},{8,11},{9,10},{10,... | collective-permute-start | bytes 221192 | tf_op jit(solution)/shard_map/ppermute | solution.py:240
  30.8 0.1 collective-permute-start.4
  30.9 0.0 collective-permute-done.3
  30.9 3.7 %collective-permute-done.5 = f32[144,128]{1,0:T(8,128)S(1)} collective-permute-done((f32[144,128]{1,0:T(8,128)S(1)}, f32[144,128]{1,0:T(8,128)S(1)}, u32[]{:S(2)}, u32[]{:S(2)}) %collective-permute-start.5) | collective-permute-done | bytes 73760 | tf_op jit(solution)/shard_map/ppermute | solution.py:240
  34.6 2.8 %collective-permute-done.4 = f32[144,128]{1,0:T(8,128)S(1)} collective-permute-done((f32[144,128]{1,0:T(8,128)S(1)}, f32[144,128]{1,0:T(8,128)S(1)}, u32[]{:S(2)}, u32[]{:S(2)}) %collective-permute-start.4) | collective-permute-done | bytes 73760 | tf_op jit(solution)/shard_map/ppermute | solution.py:240
  37.4 2.1 %collective-permute-start.8 = (f32[144,128]{1,0:T(8,128)S(1)}, f32[144,128]{1,0:T(8,128)S(1)}, u32[]{:S(2)}, u32[]{:S(2)}) collective-permute-start(f32[144,128]{1,0:T(8,128)S(1)} %add_add_fusion), channel_id=1, source_target_pairs={{0,3},{1,2},{2,1},{3,0},{4,7},{5,6},{6,5},{7,4},{8,11},{9,10},{10,... | collective-permute-start | bytes 221192 | tf_op jit(solution)/shard_map/ppermute | solution.py:240
  39.5 0.0 collective-permute-start.7
  39.5 2.4 %collective-permute-start.6 = (f32[144,128]{1,0:T(8,128)S(1)}, f32[144,128]{1,0:T(8,128)S(1)}, u32[]{:S(2)}, u32[]{:S(2)}) collective-permute-start(f32[144,128]{1,0:T(8,128)S(1)} %add_add_fusion), channel_id=1, source_target_pairs={{0,1},{1,0},{2,3},{3,2},{4,5},{5,4},{6,7},{7,6},{8,9},{9,8},{10,11... | collective-permute-start | bytes 221192 | tf_op jit(solution)/shard_map/ppermute | solution.py:240
  41.9 1.8 %collective-permute-done.8 = f32[144,128]{1,0:T(8,128)S(1)} collective-permute-done((f32[144,128]{1,0:T(8,128)S(1)}, f32[144,128]{1,0:T(8,128)S(1)}, u32[]{:S(2)}, u32[]{:S(2)}) %collective-permute-start.8) | collective-permute-done | bytes 73760 | tf_op jit(solution)/shard_map/ppermute | solution.py:240
  43.7 1.6 %collective-permute-done.7 = f32[144,128]{1,0:T(8,128)S(1)} collective-permute-done((f32[144,128]{1,0:T(8,128)S(1)}, f32[144,128]{1,0:T(8,128)S(1)}, u32[]{:S(2)}, u32[]{:S(2)}) %collective-permute-start.7) | collective-permute-done | bytes 73760 | tf_op jit(solution)/shard_map/ppermute | solution.py:240
  45.2 0.0 collective-permute-done.6
  45.3 2.5 %collective-permute-start.14 = (f32[320,128]{1,0:T(8,128)S(1)}, f32[320,128]{1,0:T(8,128)S(1)}, u32[]{:S(2)}, u32[]{:S(2)}) collective-permute-start(f32[320,128]{1,0:T(8,128)S(1)} %bitcast.49), channel_id=1, source_target_pairs={{0,24},{4,28},{8,16},{12,20},{16,8},{20,12},{24,0},{28,4},{1,25},{... | collective-permute-start | bytes 491528 | tf_op jit(solution)/shard_map/ppermute | solution.py:240
  47.9 0.5 collective-permute-start.13
  48.4 0.5 collective-permute-start.12
  48.9 2.5 %collective-permute-start.11 = (f32[256,128]{1,0:T(8,128)S(1)}, f32[256,128]{1,0:T(8,128)S(1)}, u32[]{:S(2)}, u32[]{:S(2)}) collective-permute-start(f32[256,128]{1,0:T(8,128)S(1)} %bitcast.53), channel_id=1, source_target_pairs={{0,24},{4,28},{8,16},{12,20},{16,8},{20,12},{24,0},{28,4},{1,25},{... | collective-permute-start | bytes 393224 | tf_op jit(solution)/shard_map/ppermute | solution.py:240
  51.4 0.5 collective-permute-start.10
  51.9 1.6 %collective-permute-done.14 = f32[320,128]{1,0:T(8,128)S(1)} collective-permute-done((f32[320,128]{1,0:T(8,128)S(1)}, f32[320,128]{1,0:T(8,128)S(1)}, u32[]{:S(2)}, u32[]{:S(2)}) %collective-permute-start.14) | collective-permute-done | bytes 163872 | tf_op jit(solution)/shard_map/ppermute | solution.py:240
  53.5 1.0 %collective-permute-start.9 = (f32[256,128]{1,0:T(8,128)S(1)}, f32[256,128]{1,0:T(8,128)S(1)}, u32[]{:S(2)}, u32[]{:S(2)}) collective-permute-start(f32[256,128]{1,0:T(8,128)S(1)} %bitcast.55), channel_id=1, source_target_pairs={{0,8},{4,12},{8,0},{12,4},{16,24},{20,28},{24,16},{28,20},{1,9},{5... | collective-permute-start | bytes 393224 | tf_op jit(solution)/shard_map/ppermute | solution.py:240
  54.5 0.6 collective-permute-done.13
  55.1 0.0 collective-permute-done.12
  55.1 0.1 dynamic-slice_bitcast_fusion.3
  55.3 13.7 %factor.1.wm_ref = f32[1280,128]{1,0:T(8,128)S(1)} custom-call(f32[1280,128]{1,0:T(8,128)S(1)} %pad_maximum_fusion.2.refs_0_), custom_call_target="tpu_custom_call" | custom-call | flops 20000000000 | bytes 1310720 | tf_op jit(solution)/shard_map/factor/pallas_call | solution.py:320
  69.0 0.0 collective-permute-done.11
  69.0 0.0 collective-permute-done.10
  69.0 0.0 collective-permute-done.9
  69.0 0.1 collective-permute-start.15
  69.2 0.0 copy-start.1
  69.2 0.0 copy-start.3
  69.3 0.6 collective-permute-start.16
  69.8 2.1 %collective-permute-done.16.co_ref = f32[1024,128]{1,0:T(8,128)S(1)} collective-permute-done((f32[1024,128]{1,0:T(8,128)S(1)}, f32[1024,128]{1,0:T(8,128)S(1)}, u32[]{:S(2)}, u32[]{:S(2)}) %collective-permute-start.16) | collective-permute-done | bytes 524320 | tf_op jit(solution)/shard_map/ppermute | solution.py:240
  72.0 0.0 collective-permute-done.15.wo_ref
  72.0 0.0 copy-done.1
  72.0 0.0 copy-done.3
  72.0 7.4 %project.1 = (bf16[1024,512]{1,0:T(8,128)(2,1)}, bf16[1024,512]{1,0:T(8,128)(2,1)}, f32[512,512]{1,0:T(8,128)}) custom-call(s32[1]{0:T(128)} %bitcast.core_ref, bf16[1024,512]{1,0:T(8,128)(2,1)S(1)} %copy-done.1, bf16[1024,512]{1,0:T(8,128)(2,1)S(1)} %copy-done.3, f32[1280,128]{1,0:T(8,128)S(1)} %factor.1.wm_ref, ...), custom_call_target="tpu_custom_call" | custom-call | flops 2147483648 | bytes 8388608 | tf_op jit(solution)/shard_map/project/pallas_call | solution.py:335
  (18 shorter events, 0.5 us)
Async XLA Ops:
  0.6 1.2 %copy-start = (bf16[1024,512]{1,0:T(8,128)(2,1)S(1)}, bf16[1024,512]{1,0:T(8,128)(2,1)}, u32[]{:S(2)}) copy-start(bf16[1024,512]{1,0:T(8,128)(2,1)} %x_ref.3) | copy-start | bytes 3145732
  1.9 1.2 %copy-start.2 = (bf16[1024,512]{1,0:T(8,128)(2,1)S(1)}, bf16[1024,512]{1,0:T(8,128)(2,1)}, u32[]{:S(2)}) copy-start(bf16[1024,512]{1,0:T(8,128)(2,1)} %y_ref.3) | copy-start | bytes 3145732
  5.0 3.0 %collective-permute-start = (f32[2304,128]{1,0:T(8,128)S(1)}, f32[2304,128]{1,0:T(8,128)S(1)}, u32[]{:S(2)}, u32[]{:S(2)}) collective-permute-start(f32[2304,128]{1,0:T(8,128)S(1)} %get-tuple-element.11), channel_id=1, source_target_pairs={{0,4},{4,0},{8,12},{12,8},{16,20},{20,16},{24,28},{28,24},{1,5},{5... | collective-permute-start | bytes 3538952 | tf_op jit(solution)/shard_map/ppermute | solution.py:240
  8.4 10.8 %collective-permute-start.1 = (f32[1152,128]{1,0:T(8,128)S(1)}, f32[1152,128]{1,0:T(8,128)S(1)}, u32[]{:S(2)}, u32[]{:S(2)}) collective-permute-start(f32[1152,128]{1,0:T(8,128)S(1)} %constant_dynamic-slice_fusion.4), channel_id=1, source_target_pairs={{0,8},{4,20},{8,0},{12,28},{16,24},{20,4},{24,16},{28,12},{1,9},{5... | collective-permute-start | bytes 1769480 | tf_op jit(solution)/shard_map/ppermute | solution.py:274
  19.3 6.8 %collective-permute-start.2 = (f32[576,128]{1,0:T(8,128)S(1)}, f32[576,128]{1,0:T(8,128)S(1)}, u32[]{:S(2)}, u32[]{:S(2)}) collective-permute-start(f32[576,128]{1,0:T(8,128)S(1)} %constant_dynamic-slice_fusion.3), channel_id=1, source_target_pairs={{0,16},{4,12},{8,24},{12,4},{16,0},{20,28},{24,8},{28,20},{1,17},{... | collective-permute-start | bytes 884744 | tf_op jit(solution)/shard_map/ppermute | solution.py:274
  26.1 4.7 %collective-permute-start.3 = (f32[144,128]{1,0:T(8,128)S(1)}, f32[144,128]{1,0:T(8,128)S(1)}, u32[]{:S(2)}, u32[]{:S(2)}) collective-permute-start(f32[144,128]{1,0:T(8,128)S(1)} %get-tuple-element.29), channel_id=1, source_target_pairs={{0,1},{1,0},{2,3},{3,2},{4,5},{5,4},{6,7},{7,6},{8,9},{9,8},{10,11... | collective-permute-start | bytes 221192 | tf_op jit(solution)/shard_map/ppermute | solution.py:240
  28.3 6.3 %collective-permute-start.5 = (f32[144,128]{1,0:T(8,128)S(1)}, f32[144,128]{1,0:T(8,128)S(1)}, u32[]{:S(2)}, u32[]{:S(2)}) collective-permute-start(f32[144,128]{1,0:T(8,128)S(1)} %get-tuple-element.30), channel_id=1, source_target_pairs={{0,3},{1,2},{2,1},{3,0},{4,7},{5,6},{6,5},{7,4},{8,11},{9,10},{10,... | collective-permute-start | bytes 221192 | tf_op jit(solution)/shard_map/ppermute | solution.py:240
  30.8 6.6 %collective-permute-start.4 = (f32[144,128]{1,0:T(8,128)S(1)}, f32[144,128]{1,0:T(8,128)S(1)}, u32[]{:S(2)}, u32[]{:S(2)}) collective-permute-start(f32[144,128]{1,0:T(8,128)S(1)} %get-tuple-element.31), channel_id=1, source_target_pairs={{0,2},{1,3},{2,0},{3,1},{4,6},{5,7},{6,4},{7,5},{8,10},{9,11},{10,... | collective-permute-start | bytes 221192 | tf_op jit(solution)/shard_map/ppermute | solution.py:240
  37.4 6.2 %collective-permute-start.8 = (f32[144,128]{1,0:T(8,128)S(1)}, f32[144,128]{1,0:T(8,128)S(1)}, u32[]{:S(2)}, u32[]{:S(2)}) collective-permute-start(f32[144,128]{1,0:T(8,128)S(1)} %add_add_fusion), channel_id=1, source_target_pairs={{0,3},{1,2},{2,1},{3,0},{4,7},{5,6},{6,5},{7,4},{8,11},{9,10},{10,... | collective-permute-start | bytes 221192 | tf_op jit(solution)/shard_map/ppermute | solution.py:240
  39.5 5.7 %collective-permute-start.7 = (f32[144,128]{1,0:T(8,128)S(1)}, f32[144,128]{1,0:T(8,128)S(1)}, u32[]{:S(2)}, u32[]{:S(2)}) collective-permute-start(f32[144,128]{1,0:T(8,128)S(1)} %add_add_fusion), channel_id=1, source_target_pairs={{0,2},{1,3},{2,0},{3,1},{4,6},{5,7},{6,4},{7,5},{8,10},{9,11},{10,... | collective-permute-start | bytes 221192 | tf_op jit(solution)/shard_map/ppermute | solution.py:240
  39.5 5.7 %collective-permute-start.6 = (f32[144,128]{1,0:T(8,128)S(1)}, f32[144,128]{1,0:T(8,128)S(1)}, u32[]{:S(2)}, u32[]{:S(2)}) collective-permute-start(f32[144,128]{1,0:T(8,128)S(1)} %add_add_fusion), channel_id=1, source_target_pairs={{0,1},{1,0},{2,3},{3,2},{4,5},{5,4},{6,7},{7,6},{8,9},{9,8},{10,11... | collective-permute-start | bytes 221192 | tf_op jit(solution)/shard_map/ppermute | solution.py:240
  45.3 8.1 %collective-permute-start.14 = (f32[320,128]{1,0:T(8,128)S(1)}, f32[320,128]{1,0:T(8,128)S(1)}, u32[]{:S(2)}, u32[]{:S(2)}) collective-permute-start(f32[320,128]{1,0:T(8,128)S(1)} %bitcast.49), channel_id=1, source_target_pairs={{0,24},{4,28},{8,16},{12,20},{16,8},{20,12},{24,0},{28,4},{1,25},{... | collective-permute-start | bytes 491528 | tf_op jit(solution)/shard_map/ppermute | solution.py:240
  47.9 7.2 %collective-permute-start.13 = (f32[320,128]{1,0:T(8,128)S(1)}, f32[320,128]{1,0:T(8,128)S(1)}, u32[]{:S(2)}, u32[]{:S(2)}) collective-permute-start(f32[320,128]{1,0:T(8,128)S(1)} %bitcast.50), channel_id=1, source_target_pairs={{0,16},{4,20},{8,24},{12,28},{16,0},{20,4},{24,8},{28,12},{1,17},{... | collective-permute-start | bytes 491528 | tf_op jit(solution)/shard_map/ppermute | solution.py:240
  48.4 6.7 %collective-permute-start.12 = (f32[320,128]{1,0:T(8,128)S(1)}, f32[320,128]{1,0:T(8,128)S(1)}, u32[]{:S(2)}, u32[]{:S(2)}) collective-permute-start(f32[320,128]{1,0:T(8,128)S(1)} %bitcast.51), channel_id=1, source_target_pairs={{0,8},{4,12},{8,0},{12,4},{16,24},{20,28},{24,16},{28,20},{1,9},{5... | collective-permute-start | bytes 491528 | tf_op jit(solution)/shard_map/ppermute | solution.py:240
  48.9 20.1 %collective-permute-start.11 = (f32[256,128]{1,0:T(8,128)S(1)}, f32[256,128]{1,0:T(8,128)S(1)}, u32[]{:S(2)}, u32[]{:S(2)}) collective-permute-start(f32[256,128]{1,0:T(8,128)S(1)} %bitcast.53), channel_id=1, source_target_pairs={{0,24},{4,28},{8,16},{12,20},{16,8},{20,12},{24,0},{28,4},{1,25},{... | collective-permute-start | bytes 393224 | tf_op jit(solution)/shard_map/ppermute | solution.py:240
  51.4 17.6 %collective-permute-start.10 = (f32[256,128]{1,0:T(8,128)S(1)}, f32[256,128]{1,0:T(8,128)S(1)}, u32[]{:S(2)}, u32[]{:S(2)}) collective-permute-start(f32[256,128]{1,0:T(8,128)S(1)} %bitcast.54), channel_id=1, source_target_pairs={{0,16},{4,20},{8,24},{12,28},{16,0},{20,4},{24,8},{28,12},{1,17},{... | collective-permute-start | bytes 393224 | tf_op jit(solution)/shard_map/ppermute | solution.py:240
  53.5 15.5 %collective-permute-start.9 = (f32[256,128]{1,0:T(8,128)S(1)}, f32[256,128]{1,0:T(8,128)S(1)}, u32[]{:S(2)}, u32[]{:S(2)}) collective-permute-start(f32[256,128]{1,0:T(8,128)S(1)} %bitcast.55), channel_id=1, source_target_pairs={{0,8},{4,12},{8,0},{12,4},{16,24},{20,28},{24,16},{28,20},{1,9},{5... | collective-permute-start | bytes 393224 | tf_op jit(solution)/shard_map/ppermute | solution.py:240
  69.0 2.9 %collective-permute-start.15 = (f32[1280,128]{1,0:T(8,128)S(1)}, f32[1280,128]{1,0:T(8,128)S(1)}, u32[]{:S(2)}, u32[]{:S(2)}) collective-permute-start(f32[1280,128]{1,0:T(8,128)S(1)} %factor.1.wm_ref), channel_id=1, source_target_pairs={{0,4},{4,0},{8,12},{12,8},{16,20},{20,16},{24,28},{28,24},{1,5},{5... | collective-permute-start | bytes 1966088 | tf_op jit(solution)/shard_map/ppermute | solution.py:240
  69.2 2.8 %copy-start.1 = (bf16[1024,512]{1,0:T(8,128)(2,1)S(1)}, bf16[1024,512]{1,0:T(8,128)(2,1)}, u32[]{:S(2)}) copy-start(bf16[1024,512]{1,0:T(8,128)(2,1)} %x_ref.3) | copy-start | bytes 3145732
  69.2 2.8 %copy-start.3 = (bf16[1024,512]{1,0:T(8,128)(2,1)S(1)}, bf16[1024,512]{1,0:T(8,128)(2,1)}, u32[]{:S(2)}) copy-start(bf16[1024,512]{1,0:T(8,128)(2,1)} %y_ref.3) | copy-start | bytes 3145732
  69.3 2.7 %collective-permute-start.16 = (f32[1024,128]{1,0:T(8,128)S(1)}, f32[1024,128]{1,0:T(8,128)S(1)}, u32[]{:S(2)}, u32[]{:S(2)}) collective-permute-start(f32[1024,128]{1,0:T(8,128)S(1)} %maximum_multiply_fusion.cm_ref), channel_id=1, source_target_pairs={{0,4},{4,0},{8,12},{12,8},{16,20},{20,16},{24,28},{28,24},{1,5},{5... | collective-permute-start | bytes 1572872 | tf_op jit(solution)/shard_map/ppermute | solution.py:240

commit v4 on v3

--- a/solution.py
+++ b/solution.py
@@ -52,97 +52,131 @@
     beside = list(beside)
     n = a.shape[0]
     panels = n // NB
-    r = lax.broadcasted_iota(jnp.int32, (n, n), 0)
-    c = lax.broadcasted_iota(jnp.int32, (n, n), 1)
-    z = jnp.where(r == c, 1.0, 0.0).astype(F32)
     sublane = lax.broadcasted_iota(jnp.int32, (TILE, n), 0)
-    tiles = lambda a, z: [(a[k : k + TILE], z[k : k + TILE]) for k in range(0, NB, TILE)]
-    now, later, rest = tiles(a[:NB], z[:NB]), tiles(a[NB : 2 * NB], z[NB : 2 * NB]), (a[2 * NB :], z[2 * NB :])
+    lane = lax.broadcasted_iota(jnp.int32, (TILE, n), 1)
+    tiles = lambda a: [a[k : k + TILE] for k in range(0, NB, TILE)]
+    row = lambda v, k: v[k : k + 1, :]
+    now, later, rest = tiles(a[:NB]), tiles(a[NB : 2 * NB]), a[2 * NB :]
     out = []
     for s in range(panels):
-        last = s == panels - 1
-        groups = now if last else now + later
-        left = [g[0] for g in groups]
-        right = [g[1] for g in groups]
-        cols = [[jnp.broadcast_to(g[:, NB * s + q : NB * s + q + 1], (TILE, n)) for q in range(NB)] for g in left]
+        base = NB * s
+        groups = now if s == panels - 1 else now + later
+        cols = [
+            {q: jnp.broadcast_to(v[:, base + q : base + q + 1], (TILE, n)) for q in range(min(NB, TILE * (g + 1)))}
+            for g, v in enumerate(groups)
+        ]
+        inside = (lane >= base) & (lane < base + NB)
+        start = lambda g: jnp.where(lane - base - TILE * g == sublane, 1.0, 0.0) if g < len(now) else 0.0
+        values = [jnp.where(inside, start(g), v) for g, v in enumerate(groups)]
         pivots = [jnp.ones((TILE, n), F32) for _ in now]
         for k in range(NB):
             tile, sub = divmod(k, TILE)
-            row = lambda v: v[sub : sub + 1, :]
-            d = row(cols[tile][k])
+            d = row(cols[tile][k], sub)
             pivots[tile] = jnp.where(sublane == sub, d, pivots[tile])
             inverse = 1.0 / d
-            left_row, right_row = row(left[tile]), row(right[tile])
-            entries = {q: row(cols[tile][q]) for q in range(k + 1, NB)}
+            pivot_row = row(values[tile], sub)
+            entries = {q: row(cols[q // TILE][k], q % TILE) for q in range(k + 1, NB)}
             for g in range(tile, len(groups)):
                 if g == tile and sub == TILE - 1:
                     continue
                 m = cols[g][k] * inverse
+                for q in range(k + 1, NB):
+                    if q in cols[g]:
+                        cols[g][q] = cols[g][q] - m * entries[q]
                 if g == tile:
                     m = jnp.where(sublane > sub, m, 0.0)
-                for q in range(k + 1, NB):
-                    cols[g][q] = cols[g][q] - m * entries[q]
-                left[g] = left[g] - m * left_row
-                right[g] = right[g] - m * right_row
-        scales = [lax.rsqrt(p) for p in pivots]
-        u = jnp.concatenate([v * scale for v, scale in zip(left, scales)], 0)
-        v = jnp.concatenate([v * scale for v, scale in zip(right, scales)], 0)
-        out.append(v)
-        now = list(zip(left, right))[len(now) :]
+                values[g] = values[g] - m * pivot_row
+        u = jnp.concatenate([v * lax.rsqrt(p) for v, p in zip(values, pivots)], 0)
+        out.append(u)
+        now = values[len(now) :]
         if s < panels - 2:
-            update = outer_sum(u[:, NB * (s + 2) :], jnp.concatenate([u, v], 1))
-            a, z = rest[0] - update[:, :n], rest[1] - update[:, n:]
-            later, rest = tiles(a[:NB], z[:NB]), (a[NB:], z[NB:])
+            rest = jnp.where(inside[:1], 0.0, rest) - outer_sum(u[:, base + 2 * NB :], u)
+            later, rest = tiles(rest[:NB]), rest[NB:]
         if beside:
             beside.pop(0)()
     for work in beside:
         work()
-    return jnp.concatenate(out, 0)
-
-
-def upper_blocks(n):
-    return [(i, j) for i in range(n) for j in range(i, n)]
+    r = lax.broadcasted_iota(jnp.int32, (n, n), 0)
+    c = lax.broadcasted_iota(jnp.int32, (n, n), 1)
+    return jnp.where(r >= c, jnp.concatenate(out, 0), 0.0)
+
+
+def off_diagonal(n):
+    return [(i, j) for i in range(n) for j in range(i + 1, n)]
 
 
 def lower_blocks(n):
     return [(i, j) for i in range(n) for j in range(i + 1)]
 
 
-def gram_kernel(core_ref, x_ref, y_ref, other_ref, own_ref, a_ref):
+def block_iotas():
+    return lax.broadcasted_iota(jnp.int32, (B, B), 0), lax.broadcasted_iota(jnp.int32, (B, B), 1)
+
+
+def folded_rows(n):
+    return B * (n // 2 + n * (n - 1) // 2)
+
+
+def fold(v_ref, o_ref, e_ref):
+    n = v_ref.shape[1] // B
+    r, c = block_iotas()
+    diagonals = []
+    for i in range(n):
+        g = dot(v_ref[:, B * i : B * (i + 1)], v_ref[:, B * i :], 0, 0)
+        diagonals.append(g[:, :B])
+        for j in range(i + 1, n):
+            k = n // 2 + off_diagonal(n).index((i, j))
+            o_ref[B * k : B * (k + 1), :] = g[:, B * (j - i) : B * (j - i + 1)]
+    extra = jnp.zeros((TILE, B), F32)
+    for p in range(n // 2):
+        low, high = diagonals[2 * p], diagonals[2 * p + 1]
+        o_ref[B * p : B * (p + 1), :] = jnp.where(r >= c, low, high)
+        diagonal = jnp.sum(jnp.where(r == c, high, 0.0), 0, keepdims=True)
+        extra = jnp.where(lax.broadcasted_iota(jnp.int32, (TILE, B), 0) == p, diagonal, extra)
+    e_ref[...] = jnp.zeros_like(e_ref)
+    e_ref[:TILE, :] = extra
+
+
+def gram_kernel(core_ref, x_ref, y_ref, other_ref, own_ref, gx_ref, ex_ref, gy_ref, ey_ref):
     width = x_ref.shape[1]
     half = width // 2
-    n = width // B
     core = core_ref[0]
+    rows = gx_ref.shape[0]
+    fold(x_ref, gx_ref, ex_ref)
+    fold(y_ref, gy_ref, ey_ref)
+
+    def write(o_ref, g_ref, e_ref):
+        o_ref[:rows, :] = g_ref[...]
+        o_ref[o_ref.shape[0] - B :, :] = e_ref[...]
+
+    @pl.when(core == 0)
+    def _():
+        write(own_ref, gx_ref, ex_ref)
+        write(other_ref, gy_ref, ey_ref)
+
+    @pl.when(core == 1)
+    def _():
+        write(own_ref, gy_ref, ey_ref)
+        write(other_ref, gx_ref, ex_ref)
+
     for owner, o_ref in ((1 - core, other_ref), (core, own_ref)):
-
-        @pl.when(owner == 0)
-        def _():
-            a_ref[...] = x_ref[...]
-
-        @pl.when(owner == 1)
-        def _():
-            a_ref[...] = y_ref[...]
-
-        row = 0
-        for i in range(n):
-            g = dot(a_ref[:, B * i : B * (i + 1)], a_ref[:, B * i :], 0, 0)
-            for j in range(n - i):
-                o_ref[row : row + B, :] = g[:, B * j : B * (j + 1)]
-                row += B
         g = dot(x_ref[...], y_ref[:, pl.ds(pl.multiple_of(owner * half, half), half)], 0, 0)
         for j in range(half // B):
-            o_ref[row : row + width, :] = g[:, B * j : B * (j + 1)]
-            row += width
-
-
-def factor_kernel(total_rows, n, s_ref, o_ref, f_ref):
-    r = lax.broadcasted_iota(jnp.int32, (B, B), 0)
-    c = lax.broadcasted_iota(jnp.int32, (B, B), 1)
-    ridge = jnp.where(r == c, RIDGE, 0.0).astype(F32)
+            o_ref[rows + width * j : rows + width * (j + 1), :] = g[:, B * j : B * (j + 1)]
+
+
+def factor_kernel(total_rows, n, s_ref, e_ref, o_ref, f_ref):
+    r, c = block_iotas()
     at = lambda i: slice(B * i, B * (i + 1))
-    for k, (i, j) in enumerate(upper_blocks(n)):
-        block = s_ref[at(k), :] / total_rows
-        f_ref[at(i), at(j)] = block + ridge if i == j else block
+    finish = lambda sums: sums / total_rows + jnp.where(r == c, RIDGE, 0.0)
+    for p in range(n // 2):
+        pair = s_ref[at(p), :]
+        turned = pair.T
+        f_ref[at(2 * p), at(2 * p)] = finish(jnp.where(r >= c, pair, turned))
+        high = jnp.where(r == c, e_ref[p : p + 1, :], jnp.where(r < c, pair, turned))
+        f_ref[at(2 * p + 1), at(2 * p + 1)] = finish(high)
+    for k, (i, j) in enumerate(off_diagonal(n)):
+        f_ref[at(i), at(j)] = s_ref[at(n // 2 + k), :] / total_rows
     beside = []
     a = f_ref[at(0), at(0)]
     for b in range(n):
@@ -186,11 +220,13 @@
     at = lambda i: slice(B * i, B * (i + 1))
 
     def unpack(w_x, w_y, c_0, c_1):
-        for k, (i, j) in enumerate(lower_blocks(n)):
-            wx_ref[at(i), at(j)] = w_x[at(k), :]
-            wy_ref[at(i), at(j)] = w_y[at(k), :]
+        for w_ref, w in ((wx_ref, w_x), (wy_ref, w_y)):
+            for i in range(0, n, 2):
+                w_ref[at(i), at(i + 1)] = jnp.zeros((B, B), F32)
+            for k, (i, j) in enumerate(lower_blocks(n)):
+                w_ref[at(i), at(j)] = w[at(k), :]
         for j in range(half // B):
-            c_ref[:, B * j : B * (j + 1)] = c_0[width * j : width * (j + 1), :]
+            c_ref[:, at(j)] = c_0[width * j : width * (j + 1), :]
             c_ref[:, half + B * j : half + B * (j + 1)] = c_1[width * j : width * (j + 1), :]
 
     @pl.when(core == 0)
@@ -201,23 +237,24 @@
     def _():
         unpack(wo_ref, wm_ref, co_ref, cm_ref)
 
+    ends = range(0, width, 2 * B)
     c_hl = split2(c_ref[...])
     left = []
-    for i in range(n):
-        k = B * (i + 1)
-        left.append(dot_x3(split2(wx_ref[at(i), :k]), [e[:k] for e in c_hl]))
+    for i in ends:
+        k = i + 2 * B
+        left.append(dot_x3(split2(wx_ref[i:k, :k]), [e[:k] for e in c_hl]))
     left = split2(jnp.concatenate(left, 0))
-    for j in range(n):
-        k = B * (j + 1)
-        cross_ref[:, at(j)] = dot_x3([e[:, :k] for e in left], split2(wy_ref[at(j), :k]), 1, 1)
+    for i in ends:
+        k = i + 2 * B
+        cross_ref[:, i:k] = dot_x3([e[:, :k] for e in left], split2(wy_ref[i:k, :k]), 1, 1)
     copies = [pltpu.make_async_copy(cross_ref, cross_hbm, sems.at[0])]
     copies[0].start()
     cross = split2(cross_ref[...])
     map_x, map_y = [], []
-    for i in range(n):
-        k = B * i
-        map_x.append(dot_x3(split2(wx_ref[k:, at(i)]), [e[k:] for e in cross], 0, 0))
-        map_y.append(dot_x3([e[:, k:] for e in cross], split2(wy_ref[k:, at(i)])))
+    for i in ends:
+        columns = slice(i, i + 2 * B)
+        map_x.append(dot_x3(split2(wx_ref[i:, columns]), [e[i:] for e in cross], 0, 0))
+        map_y.append(dot_x3([e[:, i:] for e in cross], split2(wy_ref[i:, columns])))
     map_x, map_y = jnp.concatenate(map_x, 0), jnp.concatenate(map_y, 1)
     step = rows // CHUNKS
     for ref, p_ref, p_hbm, m, cb in ((x_ref, px_ref, px_hbm, map_x, 0), (y_ref, py_ref, py_hbm, map_y, 1)):
@@ -273,7 +310,7 @@
         pairs = [(i, i ^ (2 * masks[i % 2])) for i in range(2 * chips)]
         v = half(bit) + lax.ppermute(half(1 - bit), "gr", pairs)
     reverse = lambda k: sum(((k >> b) & 1) << (bits - 1 - b) for b in range(bits))
-    return v, [chip ^ jnp.where(core == 0, reverse(k), k) for k in range(chips)]
+    return v, [(k, reverse(k)) for k in range(chips)]
 
 
 def on_device(x_states, y_states):
@@ -289,47 +326,56 @@
     smem = pl.BlockSpec(memory_space=pltpu.SMEM)
     vmem = pl.BlockSpec(memory_space=pltpu.VMEM)
     hbm = pl.BlockSpec(memory_space=pltpu.HBM)
-    tri = B * len(upper_blocks(n))
+    folded = folded_rows(n)
     half = width * width // 2 // B
-
     panel = pltpu.VMEM((rows, width), BF)
+    gram = pltpu.VMEM((folded, B), F32)
+    extra = pltpu.VMEM((B, B), F32)
+    packed = jax.ShapeDtypeStruct((folded + half + B, B), F32)
 
     other, own = pl.pallas_call(
         gram_kernel,
-        out_shape=(jax.ShapeDtypeStruct((tri + half, B), F32),) * 2,
+        out_shape=(packed,) * 2,
         in_specs=[smem, vmem, vmem],
         out_specs=(vmem,) * 2,
-        scratch_shapes=[panel],
+        scratch_shapes=[gram, extra] * 2,
         compiler_params=params(10),
-        cost_estimate=pl.CostEstimate(flops=4 * rows * (tri + half) * B, bytes_accessed=8 * rows * width, transcendentals=0),
+        cost_estimate=pl.CostEstimate(flops=4 * rows * (folded + half) * B, bytes_accessed=8 * rows * width, transcendentals=0),
         name="gram",
     )(core_arg, x_states, y_states)
     sums = own + shift(other, "gr", 1)
-    cov, cxy = sums[:tri], sums[tri:]
-    blocks = lambda v: jnp.reshape(v, (chips * gc, -1, B))
-    sums = jnp.reshape(jnp.concatenate([blocks(cov), blocks(cxy)], 1), (-1, B))
+    shards = chips * gc
+    blocks = lambda v: jnp.reshape(v, (shards, -1, B))
+    flat = lambda v: jnp.reshape(v, (-1, B))
+    parts = sums[:folded], sums[folded + half :], sums[folded : folded + half]
+    sums = flat(jnp.concatenate([blocks(v) for v in parts], 1))
     sums, place = plane_scatter(sums, chips, core, chip)
+    place_other = [chip ^ jnp.where(core == 0, a, b) for a, b in place]
+    place = [chip ^ jnp.where(core == 0, b, a) for a, b in place]
     sums = scatter_end(scatter_start(sums, "gc", gc, 1, plane))
     sums = gather_end(gather_start(sums, "gc", gc, 1), [plane ^ k for k in range(gc)])
     sums = jnp.reshape(sums, (gc, -1, B))
-    own = tri // (chips * gc)
-    cov = gather_start(jnp.reshape(sums[:, :own], (-1, B)), "gr", chips, 2)
-    cxy = gather_start(jnp.reshape(sums[:, own:], (-1, B)), "gr", chips, 2)
-    cov = gather_end(cov, place)
-
+    sizes = folded // shards, (folded + B) // shards
+    cov = gather_start(flat(sums[:, : sizes[1]]), "gr", chips, 2)
+    cxy = flat(sums[:, sizes[1] :])
+    cxy = gather_start(jnp.stack([cxy, shift(cxy, "gr", 1)]), "gr", chips, 2)
+    cov = jnp.reshape(gather_end(cov, place), (shards, -1, B))
+    cov, extra = flat(cov[:, : sizes[0]]), flat(cov[:, sizes[0] :])
+
+    tri = B * len(lower_blocks(n))
     white = pl.pallas_call(
         lambda *refs: factor_kernel(float(total_rows), n, *refs),
         out_shape=jax.ShapeDtypeStruct((tri, B), F32),
-        in_specs=[vmem],
+        in_specs=[vmem] * 2,
         out_specs=vmem,
         scratch_shapes=[pltpu.VMEM((width, width), F32)],
         compiler_params=params(8),
         cost_estimate=pl.CostEstimate(flops=20_000_000_000, bytes_accessed=8 * tri * B, transcendentals=0),
         name="factor",
-    )(cov)
+    )(cov, extra)
     cxy, white = lax.optimization_barrier((cxy, white))
-    cxy = gather_end(cxy, place) / total_rows
-    cxy_other = shift(cxy, "gr", 1)
+    cxy_other = gather_end([v[1] for v in cxy], place_other) / total_rows
+    cxy = gather_end([v[0] for v in cxy], place) / total_rows
     white_other = shift(white, "gr", 1)
 
     return pl.pallas_call(

time: 79.7 us -> 77.3 us (0.970)
  Pallas kernels: 23 us -> 21 us
    pallas_call x1, Pallas kernels: 13.7 us -> 12.7 us  [on_device(): pl.pallas_call(lambda *refs: factor_kernel(float(total_rows), n, *refs),...]
    pallas_call x1, Pallas kernels: 7.36 us -> 6.43 us  [on_device(): pl.pallas_call(project_kernel, out_shape=(jax.ShapeDtypeStruct((rows, wid...]
  transfers between devices with their start and end apart: 17 -> 17, of which waited for: 10 -> 10; matrix products, arithmetic and copies ran while one was open for 0% -> 1% of each run, Pallas kernels for 17% -> 16%
where the time goes in v4:
time: 77.3 us; the launch traced here: 77.1 us
  waiting for transfers between devices  28.5 us (37%)
  starting transfers between devices  23 us (30%)
  Pallas kernels  21 us (27%)
  local copies, waits for them, and re-layouts  2.95 us (4%)
  between operations  1.1 us (1%)
    ppermute x15, starting transfers between devices, shift(): lax.ppermute(v, axis, [(i, i ^ m) for i in range(lax.axis_size(axis))])  18 us
    ppermute x15, waiting for transfers between devices, shift(): lax.ppermute(v, axis, [(i, i ^ m) for i in range(lax.axis_size(axis))])  16.5 us
    pallas_call x1, Pallas kernels, on_device(): pl.pallas_call(lambda *refs: factor_kernel(float(total_rows), n, *refs),...  12.7 us
    ppermute x2, waiting for transfers between devices, plane_scatter(): v = half(bit) + lax.ppermute(half(1 - bit), 'gr', pairs)  12 us
    pallas_call x1, Pallas kernels, on_device(): pl.pallas_call(project_kernel, out_shape=(jax.ShapeDtypeStruct((rows, wid...  6.43 us
    ppermute x2, starting transfers between devices, plane_scatter(): v = half(bit) + lax.ppermute(half(1 - bit), 'gr', pairs)  5.02 us
    unnamed x8, local copies, waits for them, and re-layouts  2.46 us
    pallas_call x1, Pallas kernels, on_device(): pl.pallas_call(gram_kernel, out_shape=(packed,) * 2, in_specs=[smem, vmem...  1.84 us
  transfers between devices with their start and end apart: 17, of which 10 were waited for; matrix products, arithmetic and copies ran while one was open for 1% of the time, Pallas kernels for 16%

profile of v4, /device:TPU:0, one launch (start us, length us, event | category | flops | bytes accessed | tf_op | source)
XLA Modules:
  0.0 77.1 jit_solution(5605208589920873794)
XLA Ops:
  0.6 0.0 copy-start
  0.7 1.2 %copy-done = bf16[1024,512]{1,0:T(8,128)(2,1)S(1)} copy-done((bf16[1024,512]{1,0:T(8,128)(2,1)S(1)}, bf16[1024,512]{1,0:T(8,128)(2,1)}, u32[]{:S(2)}) %copy-start) | copy-done | bytes 1048600
  1.9 1.2 %copy-done.2 = bf16[1024,512]{1,0:T(8,128)(2,1)S(1)} copy-done((bf16[1024,512]{1,0:T(8,128)(2,1)S(1)}, bf16[1024,512]{1,0:T(8,128)(2,1)}, u32[]{:S(2)}) %copy-start.2) | copy-done | bytes 1048600
  3.1 1.8 %gram.1 = (f32[2176,128]{1,0:T(8,128)S(1)}, f32[2176,128]{1,0:T(8,128)S(1)}) custom-call(s32[1]{0:T(128)} %bitcast.core_ref, bf16[1024,512]{1,0:T(8,128)(2,1)S(1)} %copy-done, bf16[1024,512]{1,0:T(8,128)(2,1)S(1)} %copy-done.2), custom_call_target="tpu_custom_call" | custom-call | flops 1073741824 | bytes 4194304 | tf_op jit(solution)/shard_map/gram/pallas_call | solution.py:336
  4.9 0.5 collective-permute-start
  5.5 2.4 %collective-permute-done = f32[2176,128]{1,0:T(8,128)S(1)} collective-permute-done((f32[2176,128]{1,0:T(8,128)S(1)}, f32[2176,128]{1,0:T(8,128)S(1)}, u32[]{:S(2)}, u32[]{:S(2)}) %collective-permute-start) | collective-permute-done | bytes 1114144 | tf_op jit(solution)/shard_map/ppermute | solution.py:277
  7.9 0.1 add.85
  8.0 0.1 fusion
  8.1 0.1 pad_maximum_fusion
  8.2 2.9 %collective-permute-start.1 = (f32[1088,128]{1,0:T(8,128)S(1)}, f32[1088,128]{1,0:T(8,128)S(1)}, u32[]{:S(2)}, u32[]{:S(2)}) collective-permute-start(f32[1088,128]{1,0:T(8,128)S(1)} %constant_dynamic-slice_fusion.4), channel_id=1, source_target_pairs={{0,8},{4,20},{8,0},{12,28},{16,24},{20,4},{24,16},{28,12},{1,9},{5... | collective-permute-start | bytes 1671176 | tf_op jit(solution)/shard_map/ppermute | solution.py:311
  11.1 7.5 %collective-permute-done.1 = f32[1088,128]{1,0:T(8,128)S(1)} collective-permute-done((f32[1088,128]{1,0:T(8,128)S(1)}, f32[1088,128]{1,0:T(8,128)S(1)}, u32[]{:S(2)}, u32[]{:S(2)}) %collective-permute-start.1) | collective-permute-done | bytes 557088 | tf_op jit(solution)/shard_map/ppermute | solution.py:311
  18.6 0.1 dynamic-slice_add_fusion
  18.7 2.1 %collective-permute-start.2 = (f32[544,128]{1,0:T(8,128)S(1)}, f32[544,128]{1,0:T(8,128)S(1)}, u32[]{:S(2)}, u32[]{:S(2)}) collective-permute-start(f32[544,128]{1,0:T(8,128)S(1)} %constant_dynamic-slice_fusion.3), channel_id=1, source_target_pairs={{0,16},{4,12},{8,24},{12,4},{16,0},{20,28},{24,8},{28,20},{1,17},{... | collective-permute-start | bytes 835592 | tf_op jit(solution)/shard_map/ppermute | solution.py:311
  20.8 4.5 %collective-permute-done.2 = f32[544,128]{1,0:T(8,128)S(1)} collective-permute-done((f32[544,128]{1,0:T(8,128)S(1)}, f32[544,128]{1,0:T(8,128)S(1)}, u32[]{:S(2)}, u32[]{:S(2)}) %collective-permute-start.2) | collective-permute-done | bytes 278560 | tf_op jit(solution)/shard_map/ppermute | solution.py:311
  25.4 2.1 %collective-permute-start.3 = (f32[136,128]{1,0:T(8,128)S(1)}, f32[136,128]{1,0:T(8,128)S(1)}, u32[]{:S(2)}, u32[]{:S(2)}) collective-permute-start(f32[136,128]{1,0:T(8,128)S(1)} %get-tuple-element.35), channel_id=1, source_target_pairs={{0,1},{1,0},{2,3},{3,2},{4,5},{5,4},{6,7},{7,6},{8,9},{9,8},{10,11... | collective-permute-start | bytes 208904 | tf_op jit(solution)/shard_map/ppermute | solution.py:277
  27.6 2.5 %collective-permute-start.5 = (f32[136,128]{1,0:T(8,128)S(1)}, f32[136,128]{1,0:T(8,128)S(1)}, u32[]{:S(2)}, u32[]{:S(2)}) collective-permute-start(f32[136,128]{1,0:T(8,128)S(1)} %get-tuple-element.36), channel_id=1, source_target_pairs={{0,3},{1,2},{2,1},{3,0},{4,7},{5,6},{6,5},{7,4},{8,11},{9,10},{10,... | collective-permute-start | bytes 208904 | tf_op jit(solution)/shard_map/ppermute | solution.py:277
  30.1 0.1 collective-permute-start.4
  30.2 0.0 collective-permute-done.3
  30.2 3.6 %collective-permute-done.5 = f32[136,128]{1,0:T(8,128)S(1)} collective-permute-done((f32[136,128]{1,0:T(8,128)S(1)}, f32[136,128]{1,0:T(8,128)S(1)}, u32[]{:S(2)}, u32[]{:S(2)}) %collective-permute-start.5) | collective-permute-done | bytes 69664 | tf_op jit(solution)/shard_map/ppermute | solution.py:277
  33.8 2.8 %collective-permute-done.4 = f32[136,128]{1,0:T(8,128)S(1)} collective-permute-done((f32[136,128]{1,0:T(8,128)S(1)}, f32[136,128]{1,0:T(8,128)S(1)}, u32[]{:S(2)}, u32[]{:S(2)}) %collective-permute-start.4) | collective-permute-done | bytes 69664 | tf_op jit(solution)/shard_map/ppermute | solution.py:277
  36.6 1.7 %collective-permute-start.8 = (f32[136,128]{1,0:T(8,128)S(1)}, f32[136,128]{1,0:T(8,128)S(1)}, u32[]{:S(2)}, u32[]{:S(2)}) collective-permute-start(f32[136,128]{1,0:T(8,128)S(1)} %add_add_fusion), channel_id=1, source_target_pairs={{0,3},{1,2},{2,1},{3,0},{4,7},{5,6},{6,5},{7,4},{8,11},{9,10},{10,... | collective-permute-start | bytes 208904 | tf_op jit(solution)/shard_map/ppermute | solution.py:277
  38.3 0.0 collective-permute-start.7
  38.3 2.7 %collective-permute-start.6 = (f32[136,128]{1,0:T(8,128)S(1)}, f32[136,128]{1,0:T(8,128)S(1)}, u32[]{:S(2)}, u32[]{:S(2)}) collective-permute-start(f32[136,128]{1,0:T(8,128)S(1)} %add_add_fusion), channel_id=1, source_target_pairs={{0,1},{1,0},{2,3},{3,2},{4,5},{5,4},{6,7},{7,6},{8,9},{9,8},{10,11... | collective-permute-start | bytes 208904 | tf_op jit(solution)/shard_map/ppermute | solution.py:277
  41.0 1.7 %collective-permute-done.8 = f32[136,128]{1,0:T(8,128)S(1)} collective-permute-done((f32[136,128]{1,0:T(8,128)S(1)}, f32[136,128]{1,0:T(8,128)S(1)}, u32[]{:S(2)}, u32[]{:S(2)}) %collective-permute-start.8) | collective-permute-done | bytes 69664 | tf_op jit(solution)/shard_map/ppermute | solution.py:277
  42.8 1.5 %collective-permute-done.7 = f32[136,128]{1,0:T(8,128)S(1)} collective-permute-done((f32[136,128]{1,0:T(8,128)S(1)}, f32[136,128]{1,0:T(8,128)S(1)}, u32[]{:S(2)}, u32[]{:S(2)}) %collective-permute-start.7) | collective-permute-done | bytes 69664 | tf_op jit(solution)/shard_map/ppermute | solution.py:277
  44.2 0.0 collective-permute-done.6
  44.3 0.1 collective-permute-start.9
  44.4 2.5 %collective-permute-start.15 = (f32[288,128]{1,0:T(8,128)S(1)}, f32[288,128]{1,0:T(8,128)S(1)}, u32[]{:S(2)}, u32[]{:S(2)}) collective-permute-start(f32[288,128]{1,0:T(8,128)S(1)} %bitcast.64), channel_id=1, source_target_pairs={{0,24},{4,28},{8,16},{12,20},{16,8},{20,12},{24,0},{28,4},{1,25},{... | collective-permute-start | bytes 442376 | tf_op jit(solution)/shard_map/ppermute | solution.py:277
  47.0 0.5 collective-permute-start.14
  47.5 0.5 collective-permute-start.13
  48.0 0.0 collective-permute-done.9
  48.0 2.5 %collective-permute-start.12 = (f32[2,256,128]{2,1,0:T(8,128)S(1)}, f32[2,256,128]{2,1,0:T(8,128)S(1)}, u32[]{:S(2)}, u32[]{:S(2)}) collective-permute-start(f32[2,256,128]{2,1,0:T(8,128)S(1)} %pad_maximum_fusion.7), channel_id=1, source_target_pairs={{0,24},{4,28},{8,16},{12,20},{16,8},{20,12},{24,0},{28,4},{1,25},{... | collective-permute-start | bytes 786440 | tf_op jit(solution)/shard_map/ppermute | solution.py:277
  50.5 0.5 collective-permute-start.11
  51.0 1.0 %collective-permute-done.15 = f32[288,128]{1,0:T(8,128)S(1)} collective-permute-done((f32[288,128]{1,0:T(8,128)S(1)}, f32[288,128]{1,0:T(8,128)S(1)}, u32[]{:S(2)}, u32[]{:S(2)}) %collective-permute-start.15) | collective-permute-done | bytes 147488 | tf_op jit(solution)/shard_map/ppermute | solution.py:277
  52.0 1.5 %collective-permute-start.10 = (f32[2,256,128]{2,1,0:T(8,128)S(1)}, f32[2,256,128]{2,1,0:T(8,128)S(1)}, u32[]{:S(2)}, u32[]{:S(2)}) collective-permute-start(f32[2,256,128]{2,1,0:T(8,128)S(1)} %pad_maximum_fusion.7), channel_id=1, source_target_pairs={{0,8},{4,12},{8,0},{12,4},{16,24},{20,28},{24,16},{28,20},{1,9},{5... | collective-permute-start | bytes 786440 | tf_op jit(solution)/shard_map/ppermute | solution.py:277
  53.6 1.7 %collective-permute-done.14 = f32[288,128]{1,0:T(8,128)S(1)} collective-permute-done((f32[288,128]{1,0:T(8,128)S(1)}, f32[288,128]{1,0:T(8,128)S(1)}, u32[]{:S(2)}, u32[]{:S(2)}) %collective-permute-start.14) | collective-permute-done | bytes 147488 | tf_op jit(solution)/shard_map/ppermute | solution.py:277
  55.3 0.0 collective-permute-done.13
  55.3 0.1 dynamic-slice_bitcast_fusion.3
  55.5 12.7 %factor.1.wm_ref = f32[1280,128]{1,0:T(8,128)S(1)} custom-call(f32[1024,128]{1,0:T(8,128)S(1)} %bitcast.55, f32[128,128]{1,0:T(8,128)S(1)} %slice_bitcast_fusion.refs_1_), custom_call_target="tpu_custom_call" | custom-call | flops 20000000000 | bytes 1310720 | tf_op jit(solution)/shard_map/factor/pallas_call | solution.py:366
  68.2 0.0 collective-permute-done.12
  68.3 0.0 collective-permute-done.11
  68.3 0.0 collective-permute-done.10
  68.4 0.1 collective-permute-start.16
  68.6 0.1 dynamic-slice_bitcast_fusion.7
  68.6 0.0 copy-start.1
  68.7 0.0 copy-start.3
  68.8 1.8 %collective-permute-done.16.wo_ref = f32[1280,128]{1,0:T(8,128)S(1)} collective-permute-done((f32[1280,128]{1,0:T(8,128)S(1)}, f32[1280,128]{1,0:T(8,128)S(1)}, u32[]{:S(2)}, u32[]{:S(2)}) %collective-permute-start.16) | collective-permute-done | bytes 655392 | tf_op jit(solution)/shard_map/ppermute | solution.py:277
  70.5 6.4 %project.1 = (bf16[1024,512]{1,0:T(8,128)(2,1)}, bf16[1024,512]{1,0:T(8,128)(2,1)}, f32[512,512]{1,0:T(8,128)}) custom-call(s32[1]{0:T(128)} %bitcast.core_ref, bf16[1024,512]{1,0:T(8,128)(2,1)S(1)} %copy-done.1, bf16[1024,512]{1,0:T(8,128)(2,1)S(1)} %copy-done.3, f32[1280,128]{1,0:T(8,128)S(1)} %factor.1.wm_ref, ...), custom_call_target="tpu_custom_call" | custom-call | flops 2147483648 | bytes 8388608 | tf_op jit(solution)/shard_map/project/pallas_call | solution.py:381
  (27 shorter events, 0.6 us)
Async XLA Ops:
  0.6 1.2 %copy-start = (bf16[1024,512]{1,0:T(8,128)(2,1)S(1)}, bf16[1024,512]{1,0:T(8,128)(2,1)}, u32[]{:S(2)}) copy-start(bf16[1024,512]{1,0:T(8,128)(2,1)} %x_ref.3) | copy-start | bytes 3145732
  1.9 1.2 %copy-start.2 = (bf16[1024,512]{1,0:T(8,128)(2,1)S(1)}, bf16[1024,512]{1,0:T(8,128)(2,1)}, u32[]{:S(2)}) copy-start(bf16[1024,512]{1,0:T(8,128)(2,1)} %y_ref.3) | copy-start | bytes 3145732
  4.9 2.9 %collective-permute-start = (f32[2176,128]{1,0:T(8,128)S(1)}, f32[2176,128]{1,0:T(8,128)S(1)}, u32[]{:S(2)}, u32[]{:S(2)}) collective-permute-start(f32[2176,128]{1,0:T(8,128)S(1)} %get-tuple-element.11), channel_id=1, source_target_pairs={{0,4},{4,0},{8,12},{12,8},{16,20},{20,16},{24,28},{28,24},{1,5},{5... | collective-permute-start | bytes 3342344 | tf_op jit(solution)/shard_map/ppermute | solution.py:277
  8.2 10.4 %collective-permute-start.1 = (f32[1088,128]{1,0:T(8,128)S(1)}, f32[1088,128]{1,0:T(8,128)S(1)}, u32[]{:S(2)}, u32[]{:S(2)}) collective-permute-start(f32[1088,128]{1,0:T(8,128)S(1)} %constant_dynamic-slice_fusion.4), channel_id=1, source_target_pairs={{0,8},{4,20},{8,0},{12,28},{16,24},{20,4},{24,16},{28,12},{1,9},{5... | collective-permute-start | bytes 1671176 | tf_op jit(solution)/shard_map/ppermute | solution.py:311
  18.7 6.6 %collective-permute-start.2 = (f32[544,128]{1,0:T(8,128)S(1)}, f32[544,128]{1,0:T(8,128)S(1)}, u32[]{:S(2)}, u32[]{:S(2)}) collective-permute-start(f32[544,128]{1,0:T(8,128)S(1)} %constant_dynamic-slice_fusion.3), channel_id=1, source_target_pairs={{0,16},{4,12},{8,24},{12,4},{16,0},{20,28},{24,8},{28,20},{1,17},{... | collective-permute-start | bytes 835592 | tf_op jit(solution)/shard_map/ppermute | solution.py:311
  25.4 4.7 %collective-permute-start.3 = (f32[136,128]{1,0:T(8,128)S(1)}, f32[136,128]{1,0:T(8,128)S(1)}, u32[]{:S(2)}, u32[]{:S(2)}) collective-permute-start(f32[136,128]{1,0:T(8,128)S(1)} %get-tuple-element.35), channel_id=1, source_target_pairs={{0,1},{1,0},{2,3},{3,2},{4,5},{5,4},{6,7},{7,6},{8,9},{9,8},{10,11... | collective-permute-start | bytes 208904 | tf_op jit(solution)/shard_map/ppermute | solution.py:277
  27.6 6.2 %collective-permute-start.5 = (f32[136,128]{1,0:T(8,128)S(1)}, f32[136,128]{1,0:T(8,128)S(1)}, u32[]{:S(2)}, u32[]{:S(2)}) collective-permute-start(f32[136,128]{1,0:T(8,128)S(1)} %get-tuple-element.36), channel_id=1, source_target_pairs={{0,3},{1,2},{2,1},{3,0},{4,7},{5,6},{6,5},{7,4},{8,11},{9,10},{10,... | collective-permute-start | bytes 208904 | tf_op jit(solution)/shard_map/ppermute | solution.py:277
  30.1 6.5 %collective-permute-start.4 = (f32[136,128]{1,0:T(8,128)S(1)}, f32[136,128]{1,0:T(8,128)S(1)}, u32[]{:S(2)}, u32[]{:S(2)}) collective-permute-start(f32[136,128]{1,0:T(8,128)S(1)} %get-tuple-element.37), channel_id=1, source_target_pairs={{0,2},{1,3},{2,0},{3,1},{4,6},{5,7},{6,4},{7,5},{8,10},{9,11},{10,... | collective-permute-start | bytes 208904 | tf_op jit(solution)/shard_map/ppermute | solution.py:277
  36.6 6.2 %collective-permute-start.8 = (f32[136,128]{1,0:T(8,128)S(1)}, f32[136,128]{1,0:T(8,128)S(1)}, u32[]{:S(2)}, u32[]{:S(2)}) collective-permute-start(f32[136,128]{1,0:T(8,128)S(1)} %add_add_fusion), channel_id=1, source_target_pairs={{0,3},{1,2},{2,1},{3,0},{4,7},{5,6},{6,5},{7,4},{8,11},{9,10},{10,... | collective-permute-start | bytes 208904 | tf_op jit(solution)/shard_map/ppermute | solution.py:277
  38.3 5.9 %collective-permute-start.7 = (f32[136,128]{1,0:T(8,128)S(1)}, f32[136,128]{1,0:T(8,128)S(1)}, u32[]{:S(2)}, u32[]{:S(2)}) collective-permute-start(f32[136,128]{1,0:T(8,128)S(1)} %add_add_fusion), channel_id=1, source_target_pairs={{0,2},{1,3},{2,0},{3,1},{4,6},{5,7},{6,4},{7,5},{8,10},{9,11},{10,... | collective-permute-start | bytes 208904 | tf_op jit(solution)/shard_map/ppermute | solution.py:277
  38.3 5.9 %collective-permute-start.6 = (f32[136,128]{1,0:T(8,128)S(1)}, f32[136,128]{1,0:T(8,128)S(1)}, u32[]{:S(2)}, u32[]{:S(2)}) collective-permute-start(f32[136,128]{1,0:T(8,128)S(1)} %add_add_fusion), channel_id=1, source_target_pairs={{0,1},{1,0},{2,3},{3,2},{4,5},{5,4},{6,7},{7,6},{8,9},{9,8},{10,11... | collective-permute-start | bytes 208904 | tf_op jit(solution)/shard_map/ppermute | solution.py:277
  44.3 3.7 %collective-permute-start.9 = (f32[256,128]{1,0:T(8,128)S(1)}, f32[256,128]{1,0:T(8,128)S(1)}, u32[]{:S(2)}, u32[]{:S(2)}) collective-permute-start(f32[256,128]{1,0:T(8,128)S(1)} %bitcast.68), channel_id=1, source_target_pairs={{0,4},{4,0},{8,12},{12,8},{16,20},{20,16},{24,28},{28,24},{1,5},{5... | collective-permute-start | bytes 393224 | tf_op jit(solution)/shard_map/ppermute | solution.py:277
  44.4 7.6 %collective-permute-start.15 = (f32[288,128]{1,0:T(8,128)S(1)}, f32[288,128]{1,0:T(8,128)S(1)}, u32[]{:S(2)}, u32[]{:S(2)}) collective-permute-start(f32[288,128]{1,0:T(8,128)S(1)} %bitcast.64), channel_id=1, source_target_pairs={{0,24},{4,28},{8,16},{12,20},{16,8},{20,12},{24,0},{28,4},{1,25},{... | collective-permute-start | bytes 442376 | tf_op jit(solution)/shard_map/ppermute | solution.py:277
  47.0 8.3 %collective-permute-start.14 = (f32[288,128]{1,0:T(8,128)S(1)}, f32[288,128]{1,0:T(8,128)S(1)}, u32[]{:S(2)}, u32[]{:S(2)}) collective-permute-start(f32[288,128]{1,0:T(8,128)S(1)} %bitcast.65), channel_id=1, source_target_pairs={{0,16},{4,20},{8,24},{12,28},{16,0},{20,4},{24,8},{28,12},{1,17},{... | collective-permute-start | bytes 442376 | tf_op jit(solution)/shard_map/ppermute | solution.py:277
  47.5 7.8 %collective-permute-start.13 = (f32[288,128]{1,0:T(8,128)S(1)}, f32[288,128]{1,0:T(8,128)S(1)}, u32[]{:S(2)}, u32[]{:S(2)}) collective-permute-start(f32[288,128]{1,0:T(8,128)S(1)} %bitcast.66), channel_id=1, source_target_pairs={{0,8},{4,12},{8,0},{12,4},{16,24},{20,28},{24,16},{28,20},{1,9},{5... | collective-permute-start | bytes 442376 | tf_op jit(solution)/shard_map/ppermute | solution.py:277
  48.0 20.2 %collective-permute-start.12 = (f32[2,256,128]{2,1,0:T(8,128)S(1)}, f32[2,256,128]{2,1,0:T(8,128)S(1)}, u32[]{:S(2)}, u32[]{:S(2)}) collective-permute-start(f32[2,256,128]{2,1,0:T(8,128)S(1)} %pad_maximum_fusion.7), channel_id=1, source_target_pairs={{0,24},{4,28},{8,16},{12,20},{16,8},{20,12},{24,0},{28,4},{1,25},{... | collective-permute-start | bytes 786440 | tf_op jit(solution)/shard_map/ppermute | solution.py:277
  50.5 17.7 %collective-permute-start.11 = (f32[2,256,128]{2,1,0:T(8,128)S(1)}, f32[2,256,128]{2,1,0:T(8,128)S(1)}, u32[]{:S(2)}, u32[]{:S(2)}) collective-permute-start(f32[2,256,128]{2,1,0:T(8,128)S(1)} %pad_maximum_fusion.7), channel_id=1, source_target_pairs={{0,16},{4,20},{8,24},{12,28},{16,0},{20,4},{24,8},{28,12},{1,17},{... | collective-permute-start | bytes 786440 | tf_op jit(solution)/shard_map/ppermute | solution.py:277
  52.0 16.2 %collective-permute-start.10 = (f32[2,256,128]{2,1,0:T(8,128)S(1)}, f32[2,256,128]{2,1,0:T(8,128)S(1)}, u32[]{:S(2)}, u32[]{:S(2)}) collective-permute-start(f32[2,256,128]{2,1,0:T(8,128)S(1)} %pad_maximum_fusion.7), channel_id=1, source_target_pairs={{0,8},{4,12},{8,0},{12,4},{16,24},{20,28},{24,16},{28,20},{1,9},{5... | collective-permute-start | bytes 786440 | tf_op jit(solution)/shard_map/ppermute | solution.py:277
  68.4 2.2 %collective-permute-start.16 = (f32[1280,128]{1,0:T(8,128)S(1)}, f32[1280,128]{1,0:T(8,128)S(1)}, u32[]{:S(2)}, u32[]{:S(2)}) collective-permute-start(f32[1280,128]{1,0:T(8,128)S(1)} %factor.1.wm_ref), channel_id=1, source_target_pairs={{0,4},{4,0},{8,12},{12,8},{16,20},{20,16},{24,28},{28,24},{1,5},{5... | collective-permute-start | bytes 1966088 | tf_op jit(solution)/shard_map/ppermute | solution.py:277
  68.6 1.9 %copy-start.1 = (bf16[1024,512]{1,0:T(8,128)(2,1)S(1)}, bf16[1024,512]{1,0:T(8,128)(2,1)}, u32[]{:S(2)}) copy-start(bf16[1024,512]{1,0:T(8,128)(2,1)} %x_ref.3) | copy-start | bytes 3145732
  68.7 1.9 %copy-start.3 = (bf16[1024,512]{1,0:T(8,128)(2,1)S(1)}, bf16[1024,512]{1,0:T(8,128)(2,1)}, u32[]{:S(2)}) copy-start(bf16[1024,512]{1,0:T(8,128)(2,1)} %y_ref.3) | copy-start | bytes 3145732

commit v5 on v4

--- a/solution.py
+++ b/solution.py
@@ -11,7 +11,7 @@
 TILE = 8
 BF = jnp.bfloat16
 F32 = jnp.float32
-CHUNKS = 2
+CHUNKS = 4
 
 
 def dot(a, b, ca=1, cb=0, precision=None):
@@ -350,15 +350,13 @@
     parts = sums[:folded], sums[folded + half :], sums[folded : folded + half]
     sums = flat(jnp.concatenate([blocks(v) for v in parts], 1))
     sums, place = plane_scatter(sums, chips, core, chip)
-    place_other = [chip ^ jnp.where(core == 0, a, b) for a, b in place]
     place = [chip ^ jnp.where(core == 0, b, a) for a, b in place]
     sums = scatter_end(scatter_start(sums, "gc", gc, 1, plane))
     sums = gather_end(gather_start(sums, "gc", gc, 1), [plane ^ k for k in range(gc)])
     sums = jnp.reshape(sums, (gc, -1, B))
     sizes = folded // shards, (folded + B) // shards
     cov = gather_start(flat(sums[:, : sizes[1]]), "gr", chips, 2)
-    cxy = flat(sums[:, sizes[1] :])
-    cxy = gather_start(jnp.stack([cxy, shift(cxy, "gr", 1)]), "gr", chips, 2)
+    cxy = gather_start(flat(sums[:, sizes[1] :]), "gr", chips, 2)
     cov = jnp.reshape(gather_end(cov, place), (shards, -1, B))
     cov, extra = flat(cov[:, : sizes[0]]), flat(cov[:, sizes[0] :])
 
@@ -374,8 +372,8 @@
         name="factor",
     )(cov, extra)
     cxy, white = lax.optimization_barrier((cxy, white))
-    cxy_other = gather_end([v[1] for v in cxy], place_other) / total_rows
-    cxy = gather_end([v[0] for v in cxy], place) / total_rows
+    cxy = gather_end(cxy, place) / total_rows
+    cxy_other = shift(cxy, "gr", 1)
     white_other = shift(white, "gr", 1)
 
     return pl.pallas_call(

time: 77.3 us -> 75.8 us (0.981)
  waiting for transfers between devices: 28.5 us -> 27.5 us
    ppermute x15, waiting for transfers between devices: 16.5 us -> 15.5 us  [shift(): lax.ppermute(v, axis, [(i, i ^ m) for i in range(lax.axis_size(axis))])]
  transfers between devices with their start and end apart: 17 -> 17, of which waited for: 10 -> 10; matrix products, arithmetic and copies ran while one was open for 1% -> 0% of each run, Pallas kernels for 16% -> 17%
where the time goes in v5:
time: 75.8 us; the launch traced here: 75.6 us
  waiting for transfers between devices  27.5 us (36%)
  starting transfers between devices  23 us (30%)
  Pallas kernels  20.6 us (27%)
  local copies, waits for them, and re-layouts  2.84 us (4%)
  between operations  1.04 us (1%)
    ppermute x15, starting transfers between devices, shift(): lax.ppermute(v, axis, [(i, i ^ m) for i in range(lax.axis_size(axis))])  18 us
    ppermute x15, waiting for transfers between devices, shift(): lax.ppermute(v, axis, [(i, i ^ m) for i in range(lax.axis_size(axis))])  15.5 us
    pallas_call x1, Pallas kernels, on_device(): pl.pallas_call(lambda *refs: factor_kernel(float(total_rows), n, *refs),...  12.7 us
    ppermute x2, waiting for transfers between devices, plane_scatter(): v = half(bit) + lax.ppermute(half(1 - bit), 'gr', pairs)  12 us
    pallas_call x1, Pallas kernels, on_device(): pl.pallas_call(project_kernel, out_shape=(jax.ShapeDtypeStruct((rows, wid...  6.08 us
    ppermute x2, starting transfers between devices, plane_scatter(): v = half(bit) + lax.ppermute(half(1 - bit), 'gr', pairs)  5.02 us
    unnamed x8, local copies, waits for them, and re-layouts  2.46 us
    pallas_call x1, Pallas kernels, on_device(): pl.pallas_call(gram_kernel, out_shape=(packed,) * 2, in_specs=[smem, vmem...  1.84 us
  transfers between devices with their start and end apart: 17, of which 10 were waited for; matrix products, arithmetic and copies ran while one was open for 0% of the time, Pallas kernels for 17%

profile of v5, /device:TPU:0, one launch (start us, length us, event | category | flops | bytes accessed | tf_op | source)
XLA Modules:
  0.0 75.6 jit_solution(11838209075027891853)
XLA Ops:
  0.6 0.0 copy-start
  0.7 1.2 %copy-done = bf16[1024,512]{1,0:T(8,128)(2,1)S(1)} copy-done((bf16[1024,512]{1,0:T(8,128)(2,1)S(1)}, bf16[1024,512]{1,0:T(8,128)(2,1)}, u32[]{:S(2)}) %copy-start) | copy-done | bytes 1048600
  1.9 1.2 %copy-done.2 = bf16[1024,512]{1,0:T(8,128)(2,1)S(1)} copy-done((bf16[1024,512]{1,0:T(8,128)(2,1)S(1)}, bf16[1024,512]{1,0:T(8,128)(2,1)}, u32[]{:S(2)}) %copy-start.2) | copy-done | bytes 1048600
  3.1 1.8 %gram.1 = (f32[2176,128]{1,0:T(8,128)S(1)}, f32[2176,128]{1,0:T(8,128)S(1)}) custom-call(s32[1]{0:T(128)} %bitcast.core_ref, bf16[1024,512]{1,0:T(8,128)(2,1)S(1)} %copy-done, bf16[1024,512]{1,0:T(8,128)(2,1)S(1)} %copy-done.2), custom_call_target="tpu_custom_call" | custom-call | flops 1073741824 | bytes 4194304 | tf_op jit(solution)/shard_map/gram/pallas_call | solution.py:336
  4.9 0.5 collective-permute-start
  5.5 2.4 %collective-permute-done = f32[2176,128]{1,0:T(8,128)S(1)} collective-permute-done((f32[2176,128]{1,0:T(8,128)S(1)}, f32[2176,128]{1,0:T(8,128)S(1)}, u32[]{:S(2)}, u32[]{:S(2)}) %collective-permute-start) | collective-permute-done | bytes 1114144 | tf_op jit(solution)/shard_map/ppermute | solution.py:277
  7.9 0.1 add.81
  8.0 0.1 fusion
  8.1 0.1 pad_maximum_fusion
  8.2 2.9 %collective-permute-start.1 = (f32[1088,128]{1,0:T(8,128)S(1)}, f32[1088,128]{1,0:T(8,128)S(1)}, u32[]{:S(2)}, u32[]{:S(2)}) collective-permute-start(f32[1088,128]{1,0:T(8,128)S(1)} %constant_dynamic-slice_fusion.4), channel_id=1, source_target_pairs={{0,8},{4,20},{8,0},{12,28},{16,24},{20,4},{24,16},{28,12},{1,9},{5... | collective-permute-start | bytes 1671176 | tf_op jit(solution)/shard_map/ppermute | solution.py:311
  11.1 7.5 %collective-permute-done.1 = f32[1088,128]{1,0:T(8,128)S(1)} collective-permute-done((f32[1088,128]{1,0:T(8,128)S(1)}, f32[1088,128]{1,0:T(8,128)S(1)}, u32[]{:S(2)}, u32[]{:S(2)}) %collective-permute-start.1) | collective-permute-done | bytes 557088 | tf_op jit(solution)/shard_map/ppermute | solution.py:311
  18.6 0.1 dynamic-slice_add_fusion
  18.7 2.1 %collective-permute-start.2 = (f32[544,128]{1,0:T(8,128)S(1)}, f32[544,128]{1,0:T(8,128)S(1)}, u32[]{:S(2)}, u32[]{:S(2)}) collective-permute-start(f32[544,128]{1,0:T(8,128)S(1)} %constant_dynamic-slice_fusion.3), channel_id=1, source_target_pairs={{0,16},{4,12},{8,24},{12,4},{16,0},{20,28},{24,8},{28,20},{1,17},{... | collective-permute-start | bytes 835592 | tf_op jit(solution)/shard_map/ppermute | solution.py:311
  20.8 4.5 %collective-permute-done.2 = f32[544,128]{1,0:T(8,128)S(1)} collective-permute-done((f32[544,128]{1,0:T(8,128)S(1)}, f32[544,128]{1,0:T(8,128)S(1)}, u32[]{:S(2)}, u32[]{:S(2)}) %collective-permute-start.2) | collective-permute-done | bytes 278560 | tf_op jit(solution)/shard_map/ppermute | solution.py:311
  25.4 2.1 %collective-permute-start.3 = (f32[136,128]{1,0:T(8,128)S(1)}, f32[136,128]{1,0:T(8,128)S(1)}, u32[]{:S(2)}, u32[]{:S(2)}) collective-permute-start(f32[136,128]{1,0:T(8,128)S(1)} %get-tuple-element.31), channel_id=1, source_target_pairs={{0,1},{1,0},{2,3},{3,2},{4,5},{5,4},{6,7},{7,6},{8,9},{9,8},{10,11... | collective-permute-start | bytes 208904 | tf_op jit(solution)/shard_map/ppermute | solution.py:277
  27.6 2.5 %collective-permute-start.5 = (f32[136,128]{1,0:T(8,128)S(1)}, f32[136,128]{1,0:T(8,128)S(1)}, u32[]{:S(2)}, u32[]{:S(2)}) collective-permute-start(f32[136,128]{1,0:T(8,128)S(1)} %get-tuple-element.32), channel_id=1, source_target_pairs={{0,3},{1,2},{2,1},{3,0},{4,7},{5,6},{6,5},{7,4},{8,11},{9,10},{10,... | collective-permute-start | bytes 208904 | tf_op jit(solution)/shard_map/ppermute | solution.py:277
  30.1 0.1 collective-permute-start.4
  30.2 0.0 collective-permute-done.3
  30.2 3.6 %collective-permute-done.5 = f32[136,128]{1,0:T(8,128)S(1)} collective-permute-done((f32[136,128]{1,0:T(8,128)S(1)}, f32[136,128]{1,0:T(8,128)S(1)}, u32[]{:S(2)}, u32[]{:S(2)}) %collective-permute-start.5) | collective-permute-done | bytes 69664 | tf_op jit(solution)/shard_map/ppermute | solution.py:277
  33.8 2.8 %collective-permute-done.4 = f32[136,128]{1,0:T(8,128)S(1)} collective-permute-done((f32[136,128]{1,0:T(8,128)S(1)}, f32[136,128]{1,0:T(8,128)S(1)}, u32[]{:S(2)}, u32[]{:S(2)}) %collective-permute-start.4) | collective-permute-done | bytes 69664 | tf_op jit(solution)/shard_map/ppermute | solution.py:277
  36.6 1.7 %collective-permute-start.8 = (f32[136,128]{1,0:T(8,128)S(1)}, f32[136,128]{1,0:T(8,128)S(1)}, u32[]{:S(2)}, u32[]{:S(2)}) collective-permute-start(f32[136,128]{1,0:T(8,128)S(1)} %add_add_fusion), channel_id=1, source_target_pairs={{0,3},{1,2},{2,1},{3,0},{4,7},{5,6},{6,5},{7,4},{8,11},{9,10},{10,... | collective-permute-start | bytes 208904 | tf_op jit(solution)/shard_map/ppermute | solution.py:277
  38.3 0.0 collective-permute-start.7
  38.3 2.7 %collective-permute-start.6 = (f32[136,128]{1,0:T(8,128)S(1)}, f32[136,128]{1,0:T(8,128)S(1)}, u32[]{:S(2)}, u32[]{:S(2)}) collective-permute-start(f32[136,128]{1,0:T(8,128)S(1)} %add_add_fusion), channel_id=1, source_target_pairs={{0,1},{1,0},{2,3},{3,2},{4,5},{5,4},{6,7},{7,6},{8,9},{9,8},{10,11... | collective-permute-start | bytes 208904 | tf_op jit(solution)/shard_map/ppermute | solution.py:277
  41.0 1.7 %collective-permute-done.8 = f32[136,128]{1,0:T(8,128)S(1)} collective-permute-done((f32[136,128]{1,0:T(8,128)S(1)}, f32[136,128]{1,0:T(8,128)S(1)}, u32[]{:S(2)}, u32[]{:S(2)}) %collective-permute-start.8) | collective-permute-done | bytes 69664 | tf_op jit(solution)/shard_map/ppermute | solution.py:277
  42.8 1.5 %collective-permute-done.7 = f32[136,128]{1,0:T(8,128)S(1)} collective-permute-done((f32[136,128]{1,0:T(8,128)S(1)}, f32[136,128]{1,0:T(8,128)S(1)}, u32[]{:S(2)}, u32[]{:S(2)}) %collective-permute-start.7) | collective-permute-done | bytes 69664 | tf_op jit(solution)/shard_map/ppermute | solution.py:277
  44.2 0.0 collective-permute-done.6
  44.3 2.5 %collective-permute-start.14 = (f32[288,128]{1,0:T(8,128)S(1)}, f32[288,128]{1,0:T(8,128)S(1)}, u32[]{:S(2)}, u32[]{:S(2)}) collective-permute-start(f32[288,128]{1,0:T(8,128)S(1)} %bitcast.58), channel_id=1, source_target_pairs={{0,24},{4,28},{8,16},{12,20},{16,8},{20,12},{24,0},{28,4},{1,25},{... | collective-permute-start | bytes 442376 | tf_op jit(solution)/shard_map/ppermute | solution.py:277
  46.9 0.5 collective-permute-start.13
  47.4 0.5 collective-permute-start.12
  47.9 2.5 %collective-permute-start.11 = (f32[256,128]{1,0:T(8,128)S(1)}, f32[256,128]{1,0:T(8,128)S(1)}, u32[]{:S(2)}, u32[]{:S(2)}) collective-permute-start(f32[256,128]{1,0:T(8,128)S(1)} %bitcast.62), channel_id=1, source_target_pairs={{0,24},{4,28},{8,16},{12,20},{16,8},{20,12},{24,0},{28,4},{1,25},{... | collective-permute-start | bytes 393224 | tf_op jit(solution)/shard_map/ppermute | solution.py:277
  50.4 0.5 collective-permute-start.10
  50.9 1.0 %collective-permute-done.14 = f32[288,128]{1,0:T(8,128)S(1)} collective-permute-done((f32[288,128]{1,0:T(8,128)S(1)}, f32[288,128]{1,0:T(8,128)S(1)}, u32[]{:S(2)}, u32[]{:S(2)}) %collective-permute-start.14) | collective-permute-done | bytes 147488 | tf_op jit(solution)/shard_map/ppermute | solution.py:277
  51.9 1.1 %collective-permute-start.9 = (f32[256,128]{1,0:T(8,128)S(1)}, f32[256,128]{1,0:T(8,128)S(1)}, u32[]{:S(2)}, u32[]{:S(2)}) collective-permute-start(f32[256,128]{1,0:T(8,128)S(1)} %bitcast.64), channel_id=1, source_target_pairs={{0,8},{4,12},{8,0},{12,4},{16,24},{20,28},{24,16},{28,20},{1,9},{5... | collective-permute-start | bytes 393224 | tf_op jit(solution)/shard_map/ppermute | solution.py:277
  53.0 0.4 collective-permute-done.13
  53.4 0.0 collective-permute-done.12
  53.5 0.1 dynamic-slice_bitcast_fusion.3
  53.7 12.7 %factor.1.wm_ref = f32[1280,128]{1,0:T(8,128)S(1)} custom-call(f32[1024,128]{1,0:T(8,128)S(1)} %bitcast.49, f32[128,128]{1,0:T(8,128)S(1)} %slice_bitcast_fusion.refs_1_), custom_call_target="tpu_custom_call" | custom-call | flops 20000000000 | bytes 1310720 | tf_op jit(solution)/shard_map/factor/pallas_call | solution.py:364
  66.4 0.0 collective-permute-done.11
  66.4 0.0 collective-permute-done.10
  66.4 0.0 collective-permute-done.9
  66.4 0.1 collective-permute-start.15
  66.5 0.0 copy-start.1
  66.5 0.0 copy-start.3
  66.7 0.6 collective-permute-start.16
  67.2 2.1 %collective-permute-done.16.co_ref = f32[1024,128]{1,0:T(8,128)S(1)} collective-permute-done((f32[1024,128]{1,0:T(8,128)S(1)}, f32[1024,128]{1,0:T(8,128)S(1)}, u32[]{:S(2)}, u32[]{:S(2)}) %collective-permute-start.16) | collective-permute-done | bytes 524320 | tf_op jit(solution)/shard_map/ppermute | solution.py:277
  69.3 0.0 collective-permute-done.15.wo_ref
  69.3 0.0 copy-done.3
  69.3 6.1 %project.1 = (bf16[1024,512]{1,0:T(8,128)(2,1)}, bf16[1024,512]{1,0:T(8,128)(2,1)}, f32[512,512]{1,0:T(8,128)}) custom-call(s32[1]{0:T(128)} %bitcast.core_ref, bf16[1024,512]{1,0:T(8,128)(2,1)S(1)} %copy-done.1, bf16[1024,512]{1,0:T(8,128)(2,1)S(1)} %copy-done.3, f32[1280,128]{1,0:T(8,128)S(1)} %factor.1.wm_ref, ...), custom_call_target="tpu_custom_call" | custom-call | flops 2147483648 | bytes 8388608 | tf_op jit(solution)/shard_map/project/pallas_call | solution.py:379
  (20 shorter events, 0.5 us)
Async XLA Ops:
  0.6 1.2 %copy-start = (bf16[1024,512]{1,0:T(8,128)(2,1)S(1)}, bf16[1024,512]{1,0:T(8,128)(2,1)}, u32[]{:S(2)}) copy-start(bf16[1024,512]{1,0:T(8,128)(2,1)} %x_ref.3) | copy-start | bytes 3145732
  1.9 1.2 %copy-start.2 = (bf16[1024,512]{1,0:T(8,128)(2,1)S(1)}, bf16[1024,512]{1,0:T(8,128)(2,1)}, u32[]{:S(2)}) copy-start(bf16[1024,512]{1,0:T(8,128)(2,1)} %y_ref.3) | copy-start | bytes 3145732
  4.9 2.9 %collective-permute-start = (f32[2176,128]{1,0:T(8,128)S(1)}, f32[2176,128]{1,0:T(8,128)S(1)}, u32[]{:S(2)}, u32[]{:S(2)}) collective-permute-start(f32[2176,128]{1,0:T(8,128)S(1)} %get-tuple-element.11), channel_id=1, source_target_pairs={{0,4},{4,0},{8,12},{12,8},{16,20},{20,16},{24,28},{28,24},{1,5},{5... | collective-permute-start | bytes 3342344 | tf_op jit(solution)/shard_map/ppermute | solution.py:277
  8.2 10.4 %collective-permute-start.1 = (f32[1088,128]{1,0:T(8,128)S(1)}, f32[1088,128]{1,0:T(8,128)S(1)}, u32[]{:S(2)}, u32[]{:S(2)}) collective-permute-start(f32[1088,128]{1,0:T(8,128)S(1)} %constant_dynamic-slice_fusion.4), channel_id=1, source_target_pairs={{0,8},{4,20},{8,0},{12,28},{16,24},{20,4},{24,16},{28,12},{1,9},{5... | collective-permute-start | bytes 1671176 | tf_op jit(solution)/shard_map/ppermute | solution.py:311
  18.7 6.6 %collective-permute-start.2 = (f32[544,128]{1,0:T(8,128)S(1)}, f32[544,128]{1,0:T(8,128)S(1)}, u32[]{:S(2)}, u32[]{:S(2)}) collective-permute-start(f32[544,128]{1,0:T(8,128)S(1)} %constant_dynamic-slice_fusion.3), channel_id=1, source_target_pairs={{0,16},{4,12},{8,24},{12,4},{16,0},{20,28},{24,8},{28,20},{1,17},{... | collective-permute-start | bytes 835592 | tf_op jit(solution)/shard_map/ppermute | solution.py:311
  25.4 4.7 %collective-permute-start.3 = (f32[136,128]{1,0:T(8,128)S(1)}, f32[136,128]{1,0:T(8,128)S(1)}, u32[]{:S(2)}, u32[]{:S(2)}) collective-permute-start(f32[136,128]{1,0:T(8,128)S(1)} %get-tuple-element.31), channel_id=1, source_target_pairs={{0,1},{1,0},{2,3},{3,2},{4,5},{5,4},{6,7},{7,6},{8,9},{9,8},{10,11... | collective-permute-start | bytes 208904 | tf_op jit(solution)/shard_map/ppermute | solution.py:277
  27.6 6.2 %collective-permute-start.5 = (f32[136,128]{1,0:T(8,128)S(1)}, f32[136,128]{1,0:T(8,128)S(1)}, u32[]{:S(2)}, u32[]{:S(2)}) collective-permute-start(f32[136,128]{1,0:T(8,128)S(1)} %get-tuple-element.32), channel_id=1, source_target_pairs={{0,3},{1,2},{2,1},{3,0},{4,7},{5,6},{6,5},{7,4},{8,11},{9,10},{10,... | collective-permute-start | bytes 208904 | tf_op jit(solution)/shard_map/ppermute | solution.py:277
  30.1 6.5 %collective-permute-start.4 = (f32[136,128]{1,0:T(8,128)S(1)}, f32[136,128]{1,0:T(8,128)S(1)}, u32[]{:S(2)}, u32[]{:S(2)}) collective-permute-start(f32[136,128]{1,0:T(8,128)S(1)} %get-tuple-element.33), channel_id=1, source_target_pairs={{0,2},{1,3},{2,0},{3,1},{4,6},{5,7},{6,4},{7,5},{8,10},{9,11},{10,... | collective-permute-start | bytes 208904 | tf_op jit(solution)/shard_map/ppermute | solution.py:277
  36.6 6.2 %collective-permute-start.8 = (f32[136,128]{1,0:T(8,128)S(1)}, f32[136,128]{1,0:T(8,128)S(1)}, u32[]{:S(2)}, u32[]{:S(2)}) collective-permute-start(f32[136,128]{1,0:T(8,128)S(1)} %add_add_fusion), channel_id=1, source_target_pairs={{0,3},{1,2},{2,1},{3,0},{4,7},{5,6},{6,5},{7,4},{8,11},{9,10},{10,... | collective-permute-start | bytes 208904 | tf_op jit(solution)/shard_map/ppermute | solution.py:277
  38.3 5.9 %collective-permute-start.7 = (f32[136,128]{1,0:T(8,128)S(1)}, f32[136,128]{1,0:T(8,128)S(1)}, u32[]{:S(2)}, u32[]{:S(2)}) collective-permute-start(f32[136,128]{1,0:T(8,128)S(1)} %add_add_fusion), channel_id=1, source_target_pairs={{0,2},{1,3},{2,0},{3,1},{4,6},{5,7},{6,4},{7,5},{8,10},{9,11},{10,... | collective-permute-start | bytes 208904 | tf_op jit(solution)/shard_map/ppermute | solution.py:277
  38.3 5.9 %collective-permute-start.6 = (f32[136,128]{1,0:T(8,128)S(1)}, f32[136,128]{1,0:T(8,128)S(1)}, u32[]{:S(2)}, u32[]{:S(2)}) collective-permute-start(f32[136,128]{1,0:T(8,128)S(1)} %add_add_fusion), channel_id=1, source_target_pairs={{0,1},{1,0},{2,3},{3,2},{4,5},{5,4},{6,7},{7,6},{8,9},{9,8},{10,11... | collective-permute-start | bytes 208904 | tf_op jit(solution)/shard_map/ppermute | solution.py:277
  44.3 7.6 %collective-permute-start.14 = (f32[288,128]{1,0:T(8,128)S(1)}, f32[288,128]{1,0:T(8,128)S(1)}, u32[]{:S(2)}, u32[]{:S(2)}) collective-permute-start(f32[288,128]{1,0:T(8,128)S(1)} %bitcast.58), channel_id=1, source_target_pairs={{0,24},{4,28},{8,16},{12,20},{16,8},{20,12},{24,0},{28,4},{1,25},{... | collective-permute-start | bytes 442376 | tf_op jit(solution)/shard_map/ppermute | solution.py:277
  46.9 6.6 %collective-permute-start.13 = (f32[288,128]{1,0:T(8,128)S(1)}, f32[288,128]{1,0:T(8,128)S(1)}, u32[]{:S(2)}, u32[]{:S(2)}) collective-permute-start(f32[288,128]{1,0:T(8,128)S(1)} %bitcast.59), channel_id=1, source_target_pairs={{0,16},{4,20},{8,24},{12,28},{16,0},{20,4},{24,8},{28,12},{1,17},{... | collective-permute-start | bytes 442376 | tf_op jit(solution)/shard_map/ppermute | solution.py:277
  47.4 6.1 %collective-permute-start.12 = (f32[288,128]{1,0:T(8,128)S(1)}, f32[288,128]{1,0:T(8,128)S(1)}, u32[]{:S(2)}, u32[]{:S(2)}) collective-permute-start(f32[288,128]{1,0:T(8,128)S(1)} %bitcast.60), channel_id=1, source_target_pairs={{0,8},{4,12},{8,0},{12,4},{16,24},{20,28},{24,16},{28,20},{1,9},{5... | collective-permute-start | bytes 442376 | tf_op jit(solution)/shard_map/ppermute | solution.py:277
  47.9 18.5 %collective-permute-start.11 = (f32[256,128]{1,0:T(8,128)S(1)}, f32[256,128]{1,0:T(8,128)S(1)}, u32[]{:S(2)}, u32[]{:S(2)}) collective-permute-start(f32[256,128]{1,0:T(8,128)S(1)} %bitcast.62), channel_id=1, source_target_pairs={{0,24},{4,28},{8,16},{12,20},{16,8},{20,12},{24,0},{28,4},{1,25},{... | collective-permute-start | bytes 393224 | tf_op jit(solution)/shard_map/ppermute | solution.py:277
  50.4 16.0 %collective-permute-start.10 = (f32[256,128]{1,0:T(8,128)S(1)}, f32[256,128]{1,0:T(8,128)S(1)}, u32[]{:S(2)}, u32[]{:S(2)}) collective-permute-start(f32[256,128]{1,0:T(8,128)S(1)} %bitcast.63), channel_id=1, source_target_pairs={{0,16},{4,20},{8,24},{12,28},{16,0},{20,4},{24,8},{28,12},{1,17},{... | collective-permute-start | bytes 393224 | tf_op jit(solution)/shard_map/ppermute | solution.py:277
  51.9 14.5 %collective-permute-start.9 = (f32[256,128]{1,0:T(8,128)S(1)}, f32[256,128]{1,0:T(8,128)S(1)}, u32[]{:S(2)}, u32[]{:S(2)}) collective-permute-start(f32[256,128]{1,0:T(8,128)S(1)} %bitcast.64), channel_id=1, source_target_pairs={{0,8},{4,12},{8,0},{12,4},{16,24},{20,28},{24,16},{28,20},{1,9},{5... | collective-permute-start | bytes 393224 | tf_op jit(solution)/shard_map/ppermute | solution.py:277
  66.4 2.9 %collective-permute-start.15 = (f32[1280,128]{1,0:T(8,128)S(1)}, f32[1280,128]{1,0:T(8,128)S(1)}, u32[]{:S(2)}, u32[]{:S(2)}) collective-permute-start(f32[1280,128]{1,0:T(8,128)S(1)} %factor.1.wm_ref), channel_id=1, source_target_pairs={{0,4},{4,0},{8,12},{12,8},{16,20},{20,16},{24,28},{28,24},{1,5},{5... | collective-permute-start | bytes 1966088 | tf_op jit(solution)/shard_map/ppermute | solution.py:277
  66.5 2.8 %copy-start.1 = (bf16[1024,512]{1,0:T(8,128)(2,1)S(1)}, bf16[1024,512]{1,0:T(8,128)(2,1)}, u32[]{:S(2)}) copy-start(bf16[1024,512]{1,0:T(8,128)(2,1)} %x_ref.3) | copy-start | bytes 3145732
  66.5 2.8 %copy-start.3 = (bf16[1024,512]{1,0:T(8,128)(2,1)S(1)}, bf16[1024,512]{1,0:T(8,128)(2,1)}, u32[]{:S(2)}) copy-start(bf16[1024,512]{1,0:T(8,128)(2,1)} %y_ref.3) | copy-start | bytes 3145732
  66.7 2.7 %collective-permute-start.16 = (f32[1024,128]{1,0:T(8,128)S(1)}, f32[1024,128]{1,0:T(8,128)S(1)}, u32[]{:S(2)}, u32[]{:S(2)}) collective-permute-start(f32[1024,128]{1,0:T(8,128)S(1)} %maximum_multiply_fusion.cm_ref), channel_id=1, source_target_pairs={{0,4},{4,0},{8,12},{12,8},{16,20},{20,16},{24,28},{28,24},{1,5},{5... | collective-permute-start | bytes 1572872 | tf_op jit(solution)/shard_map/ppermute | solution.py:277

commit v6 on v5

--- a/solution.py
+++ b/solution.py
@@ -145,24 +145,23 @@
     fold(x_ref, gx_ref, ex_ref)
     fold(y_ref, gy_ref, ey_ref)
 
-    def write(o_ref, g_ref, e_ref):
+    cxy = dot(x_ref[...], y_ref[...], 0, 0)
+
+    def write(o_ref, g_ref, e_ref, first):
         o_ref[:rows, :] = g_ref[...]
         o_ref[o_ref.shape[0] - B :, :] = e_ref[...]
+        for j in range(half // B):
+            o_ref[rows + width * j : rows + width * (j + 1), :] = cxy[:, first + B * j : first + B * (j + 1)]
 
     @pl.when(core == 0)
     def _():
-        write(own_ref, gx_ref, ex_ref)
-        write(other_ref, gy_ref, ey_ref)
+        write(own_ref, gx_ref, ex_ref, 0)
+        write(other_ref, gy_ref, ey_ref, half)
 
     @pl.when(core == 1)
     def _():
-        write(own_ref, gy_ref, ey_ref)
-        write(other_ref, gx_ref, ex_ref)
-
-    for owner, o_ref in ((1 - core, other_ref), (core, own_ref)):
-        g = dot(x_ref[...], y_ref[:, pl.ds(pl.multiple_of(owner * half, half), half)], 0, 0)
-        for j in range(half // B):
-            o_ref[rows + width * j : rows + width * (j + 1), :] = g[:, B * j : B * (j + 1)]
+        write(own_ref, gy_ref, ey_ref, half)
+        write(other_ref, gx_ref, ex_ref, 0)
 
 
 def factor_kernel(total_rows, n, s_ref, e_ref, o_ref, f_ref):
@@ -238,11 +237,10 @@
         unpack(wo_ref, wm_ref, co_ref, cm_ref)
 
     ends = range(0, width, 2 * B)
-    c_hl = split2(c_ref[...])
     left = []
     for i in ends:
         k = i + 2 * B
-        left.append(dot_x3(split2(wx_ref[i:k, :k]), [e[:k] for e in c_hl]))
+        left.append(dot_f32(wx_ref[i:k, :k], c_ref[:k, :]))
     left = split2(jnp.concatenate(left, 0))
     for i in ends:
         k = i + 2 * B
@@ -302,7 +300,7 @@
 def plane_scatter(v, chips, core, chip):
     bits = chips.bit_length() - 1
     for s in range(bits):
-        masks = 1 << s, 1 << (bits - 1 - s)
+        masks = 1 << (bits - 1 - s), 1 << s
         mask = jnp.where(core == 0, *masks)
         bit = (chip & mask) // mask
         rows = v.shape[0] // 2
@@ -310,7 +308,7 @@
         pairs = [(i, i ^ (2 * masks[i % 2])) for i in range(2 * chips)]
         v = half(bit) + lax.ppermute(half(1 - bit), "gr", pairs)
     reverse = lambda k: sum(((k >> b) & 1) << (bits - 1 - b) for b in range(bits))
-    return v, [(k, reverse(k)) for k in range(chips)]
+    return v, [(reverse(k), k) for k in range(chips)]
 
 
 def on_device(x_states, y_states):

time: 75.8 us -> 76.3 us (level)
  no operation moved by 1% of the time
where the time goes in v6:
time: 76.3 us; the launch traced here: 76.1 us
  waiting for transfers between devices  27.5 us (36%)
  starting transfers between devices  23 us (30%)
  Pallas kernels  21.2 us (28%)
  local copies, waits for them, and re-layouts  2.84 us (4%)
  between operations  1.04 us (1%)
    ppermute x15, starting transfers between devices, shift(): lax.ppermute(v, axis, [(i, i ^ m) for i in range(lax.axis_size(axis))])  18 us
    ppermute x15, waiting for transfers between devices, shift(): lax.ppermute(v, axis, [(i, i ^ m) for i in range(lax.axis_size(axis))])  15.5 us
    pallas_call x1, Pallas kernels, on_device(): pl.pallas_call(lambda *refs: factor_kernel(float(total_rows), n, *refs),...  12.7 us
    ppermute x2, waiting for transfers between devices, plane_scatter(): v = half(bit) + lax.ppermute(half(1 - bit), 'gr', pairs)  12.1 us
    pallas_call x1, Pallas kernels, on_device(): pl.pallas_call(project_kernel, out_shape=(jax.ShapeDtypeStruct((rows, wid...  6.78 us
    ppermute x2, starting transfers between devices, plane_scatter(): v = half(bit) + lax.ppermute(half(1 - bit), 'gr', pairs)  5 us
    unnamed x8, local copies, waits for them, and re-layouts  2.46 us
    pallas_call x1, Pallas kernels, on_device(): pl.pallas_call(gram_kernel, out_shape=(packed,) * 2, in_specs=[smem, vmem...  1.7 us
  transfers between devices with their start and end apart: 17, of which 10 were waited for; matrix products, arithmetic and copies ran while one was open for 0% of the time, Pallas kernels for 17%

profile of v6, /device:TPU:0, one launch (start us, length us, event | category | flops | bytes accessed | tf_op | source)
XLA Modules:
  0.0 76.1 jit_solution(8841775025220503974)
XLA Ops:
  0.6 0.0 copy-start
  0.7 1.2 %copy-done = bf16[1024,512]{1,0:T(8,128)(2,1)S(1)} copy-done((bf16[1024,512]{1,0:T(8,128)(2,1)S(1)}, bf16[1024,512]{1,0:T(8,128)(2,1)}, u32[]{:S(2)}) %copy-start) | copy-done | bytes 1048600
  1.9 1.2 %copy-done.2 = bf16[1024,512]{1,0:T(8,128)(2,1)S(1)} copy-done((bf16[1024,512]{1,0:T(8,128)(2,1)S(1)}, bf16[1024,512]{1,0:T(8,128)(2,1)}, u32[]{:S(2)}) %copy-start.2) | copy-done | bytes 1048600
  3.1 1.7 %gram.1 = (f32[2176,128]{1,0:T(8,128)S(1)}, f32[2176,128]{1,0:T(8,128)S(1)}) custom-call(s32[1]{0:T(128)} %bitcast.core_ref, bf16[1024,512]{1,0:T(8,128)(2,1)S(1)} %copy-done, bf16[1024,512]{1,0:T(8,128)(2,1)S(1)} %copy-done.2), custom_call_target="tpu_custom_call" | custom-call | flops 1073741824 | bytes 4194304 | tf_op jit(solution)/shard_map/gram/pallas_call | solution.py:334
  4.8 0.5 collective-permute-start
  5.3 2.4 %collective-permute-done = f32[2176,128]{1,0:T(8,128)S(1)} collective-permute-done((f32[2176,128]{1,0:T(8,128)S(1)}, f32[2176,128]{1,0:T(8,128)S(1)}, u32[]{:S(2)}, u32[]{:S(2)}) %collective-permute-start) | collective-permute-done | bytes 1114144 | tf_op jit(solution)/shard_map/ppermute | solution.py:275
  7.7 0.1 add.81
  7.8 0.1 fusion
  7.9 0.1 pad_maximum_fusion
  8.1 2.9 %collective-permute-start.1 = (f32[1088,128]{1,0:T(8,128)S(1)}, f32[1088,128]{1,0:T(8,128)S(1)}, u32[]{:S(2)}, u32[]{:S(2)}) collective-permute-start(f32[1088,128]{1,0:T(8,128)S(1)} %constant_dynamic-slice_fusion.4), channel_id=1, source_target_pairs={{0,16},{4,12},{8,24},{12,4},{16,0},{20,28},{24,8},{28,20},{1,17},{... | collective-permute-start | bytes 1671176 | tf_op jit(solution)/shard_map/ppermute | solution.py:309
  11.0 7.5 %collective-permute-done.1 = f32[1088,128]{1,0:T(8,128)S(1)} collective-permute-done((f32[1088,128]{1,0:T(8,128)S(1)}, f32[1088,128]{1,0:T(8,128)S(1)}, u32[]{:S(2)}, u32[]{:S(2)}) %collective-permute-start.1) | collective-permute-done | bytes 557088 | tf_op jit(solution)/shard_map/ppermute | solution.py:309
  18.5 0.1 dynamic-slice_add_fusion
  18.6 2.1 %collective-permute-start.2 = (f32[544,128]{1,0:T(8,128)S(1)}, f32[544,128]{1,0:T(8,128)S(1)}, u32[]{:S(2)}, u32[]{:S(2)}) collective-permute-start(f32[544,128]{1,0:T(8,128)S(1)} %constant_dynamic-slice_fusion.3), channel_id=1, source_target_pairs={{0,8},{4,20},{8,0},{12,28},{16,24},{20,4},{24,16},{28,12},{1,9},{5... | collective-permute-start | bytes 835592 | tf_op jit(solution)/shard_map/ppermute | solution.py:309
  20.7 4.6 %collective-permute-done.2 = f32[544,128]{1,0:T(8,128)S(1)} collective-permute-done((f32[544,128]{1,0:T(8,128)S(1)}, f32[544,128]{1,0:T(8,128)S(1)}, u32[]{:S(2)}, u32[]{:S(2)}) %collective-permute-start.2) | collective-permute-done | bytes 278560 | tf_op jit(solution)/shard_map/ppermute | solution.py:309
  25.3 2.1 %collective-permute-start.3 = (f32[136,128]{1,0:T(8,128)S(1)}, f32[136,128]{1,0:T(8,128)S(1)}, u32[]{:S(2)}, u32[]{:S(2)}) collective-permute-start(f32[136,128]{1,0:T(8,128)S(1)} %get-tuple-element.31), channel_id=1, source_target_pairs={{0,1},{1,0},{2,3},{3,2},{4,5},{5,4},{6,7},{7,6},{8,9},{9,8},{10,11... | collective-permute-start | bytes 208904 | tf_op jit(solution)/shard_map/ppermute | solution.py:275
  27.4 2.5 %collective-permute-start.5 = (f32[136,128]{1,0:T(8,128)S(1)}, f32[136,128]{1,0:T(8,128)S(1)}, u32[]{:S(2)}, u32[]{:S(2)}) collective-permute-start(f32[136,128]{1,0:T(8,128)S(1)} %get-tuple-element.32), channel_id=1, source_target_pairs={{0,3},{1,2},{2,1},{3,0},{4,7},{5,6},{6,5},{7,4},{8,11},{9,10},{10,... | collective-permute-start | bytes 208904 | tf_op jit(solution)/shard_map/ppermute | solution.py:275
  29.9 0.1 collective-permute-start.4
  30.0 0.0 collective-permute-done.3
  30.0 3.6 %collective-permute-done.5 = f32[136,128]{1,0:T(8,128)S(1)} collective-permute-done((f32[136,128]{1,0:T(8,128)S(1)}, f32[136,128]{1,0:T(8,128)S(1)}, u32[]{:S(2)}, u32[]{:S(2)}) %collective-permute-start.5) | collective-permute-done | bytes 69664 | tf_op jit(solution)/shard_map/ppermute | solution.py:275
  33.6 2.8 %collective-permute-done.4 = f32[136,128]{1,0:T(8,128)S(1)} collective-permute-done((f32[136,128]{1,0:T(8,128)S(1)}, f32[136,128]{1,0:T(8,128)S(1)}, u32[]{:S(2)}, u32[]{:S(2)}) %collective-permute-start.4) | collective-permute-done | bytes 69664 | tf_op jit(solution)/shard_map/ppermute | solution.py:275
  36.4 1.7 %collective-permute-start.8 = (f32[136,128]{1,0:T(8,128)S(1)}, f32[136,128]{1,0:T(8,128)S(1)}, u32[]{:S(2)}, u32[]{:S(2)}) collective-permute-start(f32[136,128]{1,0:T(8,128)S(1)} %add_add_fusion), channel_id=1, source_target_pairs={{0,3},{1,2},{2,1},{3,0},{4,7},{5,6},{6,5},{7,4},{8,11},{9,10},{10,... | collective-permute-start | bytes 208904 | tf_op jit(solution)/shard_map/ppermute | solution.py:275
  38.2 0.0 collective-permute-start.7
  38.2 2.7 %collective-permute-start.6 = (f32[136,128]{1,0:T(8,128)S(1)}, f32[136,128]{1,0:T(8,128)S(1)}, u32[]{:S(2)}, u32[]{:S(2)}) collective-permute-start(f32[136,128]{1,0:T(8,128)S(1)} %add_add_fusion), channel_id=1, source_target_pairs={{0,1},{1,0},{2,3},{3,2},{4,5},{5,4},{6,7},{7,6},{8,9},{9,8},{10,11... | collective-permute-start | bytes 208904 | tf_op jit(solution)/shard_map/ppermute | solution.py:275
  40.9 1.7 %collective-permute-done.8 = f32[136,128]{1,0:T(8,128)S(1)} collective-permute-done((f32[136,128]{1,0:T(8,128)S(1)}, f32[136,128]{1,0:T(8,128)S(1)}, u32[]{:S(2)}, u32[]{:S(2)}) %collective-permute-start.8) | collective-permute-done | bytes 69664 | tf_op jit(solution)/shard_map/ppermute | solution.py:275
  42.6 1.5 %collective-permute-done.7 = f32[136,128]{1,0:T(8,128)S(1)} collective-permute-done((f32[136,128]{1,0:T(8,128)S(1)}, f32[136,128]{1,0:T(8,128)S(1)}, u32[]{:S(2)}, u32[]{:S(2)}) %collective-permute-start.7) | collective-permute-done | bytes 69664 | tf_op jit(solution)/shard_map/ppermute | solution.py:275
  44.1 0.0 collective-permute-done.6
  44.2 2.5 %collective-permute-start.14 = (f32[288,128]{1,0:T(8,128)S(1)}, f32[288,128]{1,0:T(8,128)S(1)}, u32[]{:S(2)}, u32[]{:S(2)}) collective-permute-start(f32[288,128]{1,0:T(8,128)S(1)} %bitcast.58), channel_id=1, source_target_pairs={{0,24},{4,28},{8,16},{12,20},{16,8},{20,12},{24,0},{28,4},{1,25},{... | collective-permute-start | bytes 442376 | tf_op jit(solution)/shard_map/ppermute | solution.py:275
  46.7 0.5 collective-permute-start.13
  47.2 0.5 collective-permute-start.12
  47.8 2.5 %collective-permute-start.11 = (f32[256,128]{1,0:T(8,128)S(1)}, f32[256,128]{1,0:T(8,128)S(1)}, u32[]{:S(2)}, u32[]{:S(2)}) collective-permute-start(f32[256,128]{1,0:T(8,128)S(1)} %bitcast.62), channel_id=1, source_target_pairs={{0,24},{4,28},{8,16},{12,20},{16,8},{20,12},{24,0},{28,4},{1,25},{... | collective-permute-start | bytes 393224 | tf_op jit(solution)/shard_map/ppermute | solution.py:275
  50.3 0.5 collective-permute-start.10
  50.8 1.0 %collective-permute-done.14 = f32[288,128]{1,0:T(8,128)S(1)} collective-permute-done((f32[288,128]{1,0:T(8,128)S(1)}, f32[288,128]{1,0:T(8,128)S(1)}, u32[]{:S(2)}, u32[]{:S(2)}) %collective-permute-start.14) | collective-permute-done | bytes 147488 | tf_op jit(solution)/shard_map/ppermute | solution.py:275
  51.8 1.1 %collective-permute-start.9 = (f32[256,128]{1,0:T(8,128)S(1)}, f32[256,128]{1,0:T(8,128)S(1)}, u32[]{:S(2)}, u32[]{:S(2)}) collective-permute-start(f32[256,128]{1,0:T(8,128)S(1)} %bitcast.64), channel_id=1, source_target_pairs={{0,8},{4,12},{8,0},{12,4},{16,24},{20,28},{24,16},{28,20},{1,9},{5... | collective-permute-start | bytes 393224 | tf_op jit(solution)/shard_map/ppermute | solution.py:275
  52.9 0.4 collective-permute-done.13
  53.3 0.0 collective-permute-done.12
  53.3 0.1 dynamic-slice_bitcast_fusion.3
  53.5 12.7 %factor.1.wm_ref = f32[1280,128]{1,0:T(8,128)S(1)} custom-call(f32[1024,128]{1,0:T(8,128)S(1)} %bitcast.49, f32[128,128]{1,0:T(8,128)S(1)} %slice_bitcast_fusion.refs_1_), custom_call_target="tpu_custom_call" | custom-call | flops 20000000000 | bytes 1310720 | tf_op jit(solution)/shard_map/factor/pallas_call | solution.py:362
  66.2 0.0 collective-permute-done.11
  66.3 0.0 collective-permute-done.10
  66.3 0.0 collective-permute-done.9
  66.3 0.1 collective-permute-start.15
  66.4 0.0 copy-start.1
  66.4 0.0 copy-start.3
  66.5 0.6 collective-permute-start.16
  67.1 2.1 %collective-permute-done.16.co_ref = f32[1024,128]{1,0:T(8,128)S(1)} collective-permute-done((f32[1024,128]{1,0:T(8,128)S(1)}, f32[1024,128]{1,0:T(8,128)S(1)}, u32[]{:S(2)}, u32[]{:S(2)}) %collective-permute-start.16) | collective-permute-done | bytes 524320 | tf_op jit(solution)/shard_map/ppermute | solution.py:275
  69.2 0.0 collective-permute-done.15.wo_ref
  69.2 0.0 copy-done.1
  69.2 6.8 %project.1 = (bf16[1024,512]{1,0:T(8,128)(2,1)}, bf16[1024,512]{1,0:T(8,128)(2,1)}, f32[512,512]{1,0:T(8,128)}) custom-call(s32[1]{0:T(128)} %bitcast.core_ref, bf16[1024,512]{1,0:T(8,128)(2,1)S(1)} %copy-done.1, bf16[1024,512]{1,0:T(8,128)(2,1)S(1)} %copy-done.3, f32[1280,128]{1,0:T(8,128)S(1)} %factor.1.wm_ref, ...), custom_call_target="tpu_custom_call" | custom-call | flops 2147483648 | bytes 8388608 | tf_op jit(solution)/shard_map/project/pallas_call | solution.py:377
  (20 shorter events, 0.5 us)
Async XLA Ops:
  0.6 1.2 %copy-start = (bf16[1024,512]{1,0:T(8,128)(2,1)S(1)}, bf16[1024,512]{1,0:T(8,128)(2,1)}, u32[]{:S(2)}) copy-start(bf16[1024,512]{1,0:T(8,128)(2,1)} %x_ref.3) | copy-start | bytes 3145732
  1.9 1.2 %copy-start.2 = (bf16[1024,512]{1,0:T(8,128)(2,1)S(1)}, bf16[1024,512]{1,0:T(8,128)(2,1)}, u32[]{:S(2)}) copy-start(bf16[1024,512]{1,0:T(8,128)(2,1)} %y_ref.3) | copy-start | bytes 3145732
  4.8 2.9 %collective-permute-start = (f32[2176,128]{1,0:T(8,128)S(1)}, f32[2176,128]{1,0:T(8,128)S(1)}, u32[]{:S(2)}, u32[]{:S(2)}) collective-permute-start(f32[2176,128]{1,0:T(8,128)S(1)} %get-tuple-element.11), channel_id=1, source_target_pairs={{0,4},{4,0},{8,12},{12,8},{16,20},{20,16},{24,28},{28,24},{1,5},{5... | collective-permute-start | bytes 3342344 | tf_op jit(solution)/shard_map/ppermute | solution.py:275
  8.1 10.5 %collective-permute-start.1 = (f32[1088,128]{1,0:T(8,128)S(1)}, f32[1088,128]{1,0:T(8,128)S(1)}, u32[]{:S(2)}, u32[]{:S(2)}) collective-permute-start(f32[1088,128]{1,0:T(8,128)S(1)} %constant_dynamic-slice_fusion.4), channel_id=1, source_target_pairs={{0,16},{4,12},{8,24},{12,4},{16,0},{20,28},{24,8},{28,20},{1,17},{... | collective-permute-start | bytes 1671176 | tf_op jit(solution)/shard_map/ppermute | solution.py:309
  18.6 6.6 %collective-permute-start.2 = (f32[544,128]{1,0:T(8,128)S(1)}, f32[544,128]{1,0:T(8,128)S(1)}, u32[]{:S(2)}, u32[]{:S(2)}) collective-permute-start(f32[544,128]{1,0:T(8,128)S(1)} %constant_dynamic-slice_fusion.3), channel_id=1, source_target_pairs={{0,8},{4,20},{8,0},{12,28},{16,24},{20,4},{24,16},{28,12},{1,9},{5... | collective-permute-start | bytes 835592 | tf_op jit(solution)/shard_map/ppermute | solution.py:309
  25.3 4.7 %collective-permute-start.3 = (f32[136,128]{1,0:T(8,128)S(1)}, f32[136,128]{1,0:T(8,128)S(1)}, u32[]{:S(2)}, u32[]{:S(2)}) collective-permute-start(f32[136,128]{1,0:T(8,128)S(1)} %get-tuple-element.31), channel_id=1, source_target_pairs={{0,1},{1,0},{2,3},{3,2},{4,5},{5,4},{6,7},{7,6},{8,9},{9,8},{10,11... | collective-permute-start | bytes 208904 | tf_op jit(solution)/shard_map/ppermute | solution.py:275
  27.4 6.2 %collective-permute-start.5 = (f32[136,128]{1,0:T(8,128)S(1)}, f32[136,128]{1,0:T(8,128)S(1)}, u32[]{:S(2)}, u32[]{:S(2)}) collective-permute-start(f32[136,128]{1,0:T(8,128)S(1)} %get-tuple-element.32), channel_id=1, source_target_pairs={{0,3},{1,2},{2,1},{3,0},{4,7},{5,6},{6,5},{7,4},{8,11},{9,10},{10,... | collective-permute-start | bytes 208904 | tf_op jit(solution)/shard_map/ppermute | solution.py:275
  29.9 6.5 %collective-permute-start.4 = (f32[136,128]{1,0:T(8,128)S(1)}, f32[136,128]{1,0:T(8,128)S(1)}, u32[]{:S(2)}, u32[]{:S(2)}) collective-permute-start(f32[136,128]{1,0:T(8,128)S(1)} %get-tuple-element.33), channel_id=1, source_target_pairs={{0,2},{1,3},{2,0},{3,1},{4,6},{5,7},{6,4},{7,5},{8,10},{9,11},{10,... | collective-permute-start | bytes 208904 | tf_op jit(solution)/shard_map/ppermute | solution.py:275
  36.4 6.2 %collective-permute-start.8 = (f32[136,128]{1,0:T(8,128)S(1)}, f32[136,128]{1,0:T(8,128)S(1)}, u32[]{:S(2)}, u32[]{:S(2)}) collective-permute-start(f32[136,128]{1,0:T(8,128)S(1)} %add_add_fusion), channel_id=1, source_target_pairs={{0,3},{1,2},{2,1},{3,0},{4,7},{5,6},{6,5},{7,4},{8,11},{9,10},{10,... | collective-permute-start | bytes 208904 | tf_op jit(solution)/shard_map/ppermute | solution.py:275
  38.2 5.9 %collective-permute-start.7 = (f32[136,128]{1,0:T(8,128)S(1)}, f32[136,128]{1,0:T(8,128)S(1)}, u32[]{:S(2)}, u32[]{:S(2)}) collective-permute-start(f32[136,128]{1,0:T(8,128)S(1)} %add_add_fusion), channel_id=1, source_target_pairs={{0,2},{1,3},{2,0},{3,1},{4,6},{5,7},{6,4},{7,5},{8,10},{9,11},{10,... | collective-permute-start | bytes 208904 | tf_op jit(solution)/shard_map/ppermute | solution.py:275
  38.2 5.9 %collective-permute-start.6 = (f32[136,128]{1,0:T(8,128)S(1)}, f32[136,128]{1,0:T(8,128)S(1)}, u32[]{:S(2)}, u32[]{:S(2)}) collective-permute-start(f32[136,128]{1,0:T(8,128)S(1)} %add_add_fusion), channel_id=1, source_target_pairs={{0,1},{1,0},{2,3},{3,2},{4,5},{5,4},{6,7},{7,6},{8,9},{9,8},{10,11... | collective-permute-start | bytes 208904 | tf_op jit(solution)/shard_map/ppermute | solution.py:275
  44.2 7.6 %collective-permute-start.14 = (f32[288,128]{1,0:T(8,128)S(1)}, f32[288,128]{1,0:T(8,128)S(1)}, u32[]{:S(2)}, u32[]{:S(2)}) collective-permute-start(f32[288,128]{1,0:T(8,128)S(1)} %bitcast.58), channel_id=1, source_target_pairs={{0,24},{4,28},{8,16},{12,20},{16,8},{20,12},{24,0},{28,4},{1,25},{... | collective-permute-start | bytes 442376 | tf_op jit(solution)/shard_map/ppermute | solution.py:275
  46.7 6.6 %collective-permute-start.13 = (f32[288,128]{1,0:T(8,128)S(1)}, f32[288,128]{1,0:T(8,128)S(1)}, u32[]{:S(2)}, u32[]{:S(2)}) collective-permute-start(f32[288,128]{1,0:T(8,128)S(1)} %bitcast.59), channel_id=1, source_target_pairs={{0,16},{4,20},{8,24},{12,28},{16,0},{20,4},{24,8},{28,12},{1,17},{... | collective-permute-start | bytes 442376 | tf_op jit(solution)/shard_map/ppermute | solution.py:275
  47.2 6.1 %collective-permute-start.12 = (f32[288,128]{1,0:T(8,128)S(1)}, f32[288,128]{1,0:T(8,128)S(1)}, u32[]{:S(2)}, u32[]{:S(2)}) collective-permute-start(f32[288,128]{1,0:T(8,128)S(1)} %bitcast.60), channel_id=1, source_target_pairs={{0,8},{4,12},{8,0},{12,4},{16,24},{20,28},{24,16},{28,20},{1,9},{5... | collective-permute-start | bytes 442376 | tf_op jit(solution)/shard_map/ppermute | solution.py:275
  47.8 18.5 %collective-permute-start.11 = (f32[256,128]{1,0:T(8,128)S(1)}, f32[256,128]{1,0:T(8,128)S(1)}, u32[]{:S(2)}, u32[]{:S(2)}) collective-permute-start(f32[256,128]{1,0:T(8,128)S(1)} %bitcast.62), channel_id=1, source_target_pairs={{0,24},{4,28},{8,16},{12,20},{16,8},{20,12},{24,0},{28,4},{1,25},{... | collective-permute-start | bytes 393224 | tf_op jit(solution)/shard_map/ppermute | solution.py:275
  50.3 16.0 %collective-permute-start.10 = (f32[256,128]{1,0:T(8,128)S(1)}, f32[256,128]{1,0:T(8,128)S(1)}, u32[]{:S(2)}, u32[]{:S(2)}) collective-permute-start(f32[256,128]{1,0:T(8,128)S(1)} %bitcast.63), channel_id=1, source_target_pairs={{0,16},{4,20},{8,24},{12,28},{16,0},{20,4},{24,8},{28,12},{1,17},{... | collective-permute-start | bytes 393224 | tf_op jit(solution)/shard_map/ppermute | solution.py:275
  51.8 14.5 %collective-permute-start.9 = (f32[256,128]{1,0:T(8,128)S(1)}, f32[256,128]{1,0:T(8,128)S(1)}, u32[]{:S(2)}, u32[]{:S(2)}) collective-permute-start(f32[256,128]{1,0:T(8,128)S(1)} %bitcast.64), channel_id=1, source_target_pairs={{0,8},{4,12},{8,0},{12,4},{16,24},{20,28},{24,16},{28,20},{1,9},{5... | collective-permute-start | bytes 393224 | tf_op jit(solution)/shard_map/ppermute | solution.py:275
  66.3 2.9 %collective-permute-start.15 = (f32[1280,128]{1,0:T(8,128)S(1)}, f32[1280,128]{1,0:T(8,128)S(1)}, u32[]{:S(2)}, u32[]{:S(2)}) collective-permute-start(f32[1280,128]{1,0:T(8,128)S(1)} %factor.1.wm_ref), channel_id=1, source_target_pairs={{0,4},{4,0},{8,12},{12,8},{16,20},{20,16},{24,28},{28,24},{1,5},{5... | collective-permute-start | bytes 1966088 | tf_op jit(solution)/shard_map/ppermute | solution.py:275
  66.4 2.8 %copy-start.1 = (bf16[1024,512]{1,0:T(8,128)(2,1)S(1)}, bf16[1024,512]{1,0:T(8,128)(2,1)}, u32[]{:S(2)}) copy-start(bf16[1024,512]{1,0:T(8,128)(2,1)} %x_ref.3) | copy-start | bytes 3145732
  66.4 2.8 %copy-start.3 = (bf16[1024,512]{1,0:T(8,128)(2,1)S(1)}, bf16[1024,512]{1,0:T(8,128)(2,1)}, u32[]{:S(2)}) copy-start(bf16[1024,512]{1,0:T(8,128)(2,1)} %y_ref.3) | copy-start | bytes 3145732
  66.5 2.7 %collective-permute-start.16 = (f32[1024,128]{1,0:T(8,128)S(1)}, f32[1024,128]{1,0:T(8,128)S(1)}, u32[]{:S(2)}, u32[]{:S(2)}) collective-permute-start(f32[1024,128]{1,0:T(8,128)S(1)} %maximum_multiply_fusion.cm_ref), channel_id=1, source_target_pairs={{0,4},{4,0},{8,12},{12,8},{16,20},{20,16},{24,28},{28,24},{1,5},{5... | collective-permute-start | bytes 1572872 | tf_op jit(solution)/shard_map/ppermute | solution.py:275

commit v7 on v6

--- a/solution.py
+++ b/solution.py
@@ -164,18 +164,25 @@
         write(other_ref, gx_ref, ex_ref, 0)
 
 
-def factor_kernel(total_rows, n, s_ref, e_ref, o_ref, f_ref):
+def factor_kernel(total_rows, n, shards, s_ref, o_ref, f_ref):
     r, c = block_iotas()
     at = lambda i: slice(B * i, B * (i + 1))
+    own, more = folded_rows(n) // shards, B // shards
     finish = lambda sums: sums / total_rows + jnp.where(r == c, RIDGE, 0.0)
+
+    def block(k):
+        starts = [(own + more) * (B * k // own + i) for i in range(B // own)]
+        return jnp.concatenate([s_ref[i : i + own, :] for i in starts], 0)
+
     for p in range(n // 2):
-        pair = s_ref[at(p), :]
+        pair = block(p)
         turned = pair.T
         f_ref[at(2 * p), at(2 * p)] = finish(jnp.where(r >= c, pair, turned))
-        high = jnp.where(r == c, e_ref[p : p + 1, :], jnp.where(r < c, pair, turned))
+        extra = (own + more) * (p // more) + own + p % more
+        high = jnp.where(r == c, s_ref[extra : extra + 1, :], jnp.where(r < c, pair, turned))
         f_ref[at(2 * p + 1), at(2 * p + 1)] = finish(high)
     for k, (i, j) in enumerate(off_diagonal(n)):
-        f_ref[at(i), at(j)] = s_ref[at(n // 2 + k), :] / total_rows
+        f_ref[at(i), at(j)] = block(n // 2 + k) / total_rows
     beside = []
     a = f_ref[at(0), at(0)]
     for b in range(n):
@@ -352,23 +359,22 @@
     sums = scatter_end(scatter_start(sums, "gc", gc, 1, plane))
     sums = gather_end(gather_start(sums, "gc", gc, 1), [plane ^ k for k in range(gc)])
     sums = jnp.reshape(sums, (gc, -1, B))
-    sizes = folded // shards, (folded + B) // shards
-    cov = gather_start(flat(sums[:, : sizes[1]]), "gr", chips, 2)
-    cxy = gather_start(flat(sums[:, sizes[1] :]), "gr", chips, 2)
-    cov = jnp.reshape(gather_end(cov, place), (shards, -1, B))
-    cov, extra = flat(cov[:, : sizes[0]]), flat(cov[:, sizes[0] :])
+    size = (folded + B) // shards
+    cov = gather_start(flat(sums[:, : size]), "gr", chips, 2)
+    cxy = gather_start(flat(sums[:, size :]), "gr", chips, 2)
+    cov = gather_end(cov, place)
 
     tri = B * len(lower_blocks(n))
     white = pl.pallas_call(
-        lambda *refs: factor_kernel(float(total_rows), n, *refs),
+        lambda *refs: factor_kernel(float(total_rows), n, shards, *refs),
         out_shape=jax.ShapeDtypeStruct((tri, B), F32),
-        in_specs=[vmem] * 2,
+        in_specs=[vmem],
         out_specs=vmem,
         scratch_shapes=[pltpu.VMEM((width, width), F32)],
         compiler_params=params(8),
         cost_estimate=pl.CostEstimate(flops=20_000_000_000, bytes_accessed=8 * tri * B, transcendentals=0),
         name="factor",
-    )(cov, extra)
+    )(cov)
     cxy, white = lax.optimization_barrier((cxy, white))
     cxy = gather_end(cxy, place) / total_rows
     cxy_other = shift(cxy, "gr", 1)

time: 76.3 us -> 76.3 us (level)
  no operation moved by 1% of the time
where the time goes in v7:
time: 76.3 us; the launch traced here: 76.1 us
  waiting for transfers between devices  27.5 us (36%)
  starting transfers between devices  23 us (30%)
  Pallas kernels  21.2 us (28%)
  local copies, waits for them, and re-layouts  2.78 us (4%)
  between operations  1.02 us (1%)
    ppermute x15, starting transfers between devices, shift(): lax.ppermute(v, axis, [(i, i ^ m) for i in range(lax.axis_size(axis))])  18 us
    ppermute x15, waiting for transfers between devices, shift(): lax.ppermute(v, axis, [(i, i ^ m) for i in range(lax.axis_size(axis))])  15.5 us
    pallas_call x1, Pallas kernels, on_device(): pl.pallas_call(lambda *refs: factor_kernel(float(total_rows), n, shards,...  12.7 us
    ppermute x2, waiting for transfers between devices, plane_scatter(): v = half(bit) + lax.ppermute(half(1 - bit), 'gr', pairs)  12.1 us
    pallas_call x1, Pallas kernels, on_device(): pl.pallas_call(project_kernel, out_shape=(jax.ShapeDtypeStruct((rows, wid...  6.78 us
    ppermute x2, starting transfers between devices, plane_scatter(): v = half(bit) + lax.ppermute(half(1 - bit), 'gr', pairs)  5 us
    unnamed x8, local copies, waits for them, and re-layouts  2.46 us
    pallas_call x1, Pallas kernels, on_device(): pl.pallas_call(gram_kernel, out_shape=(packed,) * 2, in_specs=[smem, vmem...  1.7 us
  transfers between devices with their start and end apart: 17, of which 10 were waited for; matrix products, arithmetic and copies ran while one was open for 0% of the time, Pallas kernels for 17%

profile of v7, /device:TPU:0, one launch (start us, length us, event | category | flops | bytes accessed | tf_op | source)
XLA Modules:
  0.0 76.1 jit_solution(6781964178440623232)
XLA Ops:
  0.6 0.0 copy-start
  0.7 1.2 %copy-done = bf16[1024,512]{1,0:T(8,128)(2,1)S(1)} copy-done((bf16[1024,512]{1,0:T(8,128)(2,1)S(1)}, bf16[1024,512]{1,0:T(8,128)(2,1)}, u32[]{:S(2)}) %copy-start) | copy-done | bytes 1048600
  1.9 1.2 %copy-done.2 = bf16[1024,512]{1,0:T(8,128)(2,1)S(1)} copy-done((bf16[1024,512]{1,0:T(8,128)(2,1)S(1)}, bf16[1024,512]{1,0:T(8,128)(2,1)}, u32[]{:S(2)}) %copy-start.2) | copy-done | bytes 1048600
  3.1 1.7 %gram.1 = (f32[2176,128]{1,0:T(8,128)S(1)}, f32[2176,128]{1,0:T(8,128)S(1)}) custom-call(s32[1]{0:T(128)} %bitcast.core_ref, bf16[1024,512]{1,0:T(8,128)(2,1)S(1)} %copy-done, bf16[1024,512]{1,0:T(8,128)(2,1)S(1)} %copy-done.2), custom_call_target="tpu_custom_call" | custom-call | flops 1073741824 | bytes 4194304 | tf_op jit(solution)/shard_map/gram/pallas_call | solution.py:341
  4.8 0.5 collective-permute-start
  5.3 2.4 %collective-permute-done = f32[2176,128]{1,0:T(8,128)S(1)} collective-permute-done((f32[2176,128]{1,0:T(8,128)S(1)}, f32[2176,128]{1,0:T(8,128)S(1)}, u32[]{:S(2)}, u32[]{:S(2)}) %collective-permute-start) | collective-permute-done | bytes 1114144 | tf_op jit(solution)/shard_map/ppermute | solution.py:282
  7.7 0.1 add.81
  7.8 0.1 fusion
  7.9 0.1 pad_maximum_fusion
  8.1 2.9 %collective-permute-start.1 = (f32[1088,128]{1,0:T(8,128)S(1)}, f32[1088,128]{1,0:T(8,128)S(1)}, u32[]{:S(2)}, u32[]{:S(2)}) collective-permute-start(f32[1088,128]{1,0:T(8,128)S(1)} %constant_dynamic-slice_fusion.4), channel_id=1, source_target_pairs={{0,16},{4,12},{8,24},{12,4},{16,0},{20,28},{24,8},{28,20},{1,17},{... | collective-permute-start | bytes 1671176 | tf_op jit(solution)/shard_map/ppermute | solution.py:316
  11.0 7.5 %collective-permute-done.1 = f32[1088,128]{1,0:T(8,128)S(1)} collective-permute-done((f32[1088,128]{1,0:T(8,128)S(1)}, f32[1088,128]{1,0:T(8,128)S(1)}, u32[]{:S(2)}, u32[]{:S(2)}) %collective-permute-start.1) | collective-permute-done | bytes 557088 | tf_op jit(solution)/shard_map/ppermute | solution.py:316
  18.5 0.1 dynamic-slice_add_fusion
  18.6 2.1 %collective-permute-start.2 = (f32[544,128]{1,0:T(8,128)S(1)}, f32[544,128]{1,0:T(8,128)S(1)}, u32[]{:S(2)}, u32[]{:S(2)}) collective-permute-start(f32[544,128]{1,0:T(8,128)S(1)} %constant_dynamic-slice_fusion.3), channel_id=1, source_target_pairs={{0,8},{4,20},{8,0},{12,28},{16,24},{20,4},{24,16},{28,12},{1,9},{5... | collective-permute-start | bytes 835592 | tf_op jit(solution)/shard_map/ppermute | solution.py:316
  20.7 4.6 %collective-permute-done.2 = f32[544,128]{1,0:T(8,128)S(1)} collective-permute-done((f32[544,128]{1,0:T(8,128)S(1)}, f32[544,128]{1,0:T(8,128)S(1)}, u32[]{:S(2)}, u32[]{:S(2)}) %collective-permute-start.2) | collective-permute-done | bytes 278560 | tf_op jit(solution)/shard_map/ppermute | solution.py:316
  25.3 2.1 %collective-permute-start.3 = (f32[136,128]{1,0:T(8,128)S(1)}, f32[136,128]{1,0:T(8,128)S(1)}, u32[]{:S(2)}, u32[]{:S(2)}) collective-permute-start(f32[136,128]{1,0:T(8,128)S(1)} %get-tuple-element.31), channel_id=1, source_target_pairs={{0,1},{1,0},{2,3},{3,2},{4,5},{5,4},{6,7},{7,6},{8,9},{9,8},{10,11... | collective-permute-start | bytes 208904 | tf_op jit(solution)/shard_map/ppermute | solution.py:282
  27.4 2.5 %collective-permute-start.5 = (f32[136,128]{1,0:T(8,128)S(1)}, f32[136,128]{1,0:T(8,128)S(1)}, u32[]{:S(2)}, u32[]{:S(2)}) collective-permute-start(f32[136,128]{1,0:T(8,128)S(1)} %get-tuple-element.32), channel_id=1, source_target_pairs={{0,3},{1,2},{2,1},{3,0},{4,7},{5,6},{6,5},{7,4},{8,11},{9,10},{10,... | collective-permute-start | bytes 208904 | tf_op jit(solution)/shard_map/ppermute | solution.py:282
  29.9 0.1 collective-permute-start.4
  30.0 0.0 collective-permute-done.3
  30.0 3.6 %collective-permute-done.5 = f32[136,128]{1,0:T(8,128)S(1)} collective-permute-done((f32[136,128]{1,0:T(8,128)S(1)}, f32[136,128]{1,0:T(8,128)S(1)}, u32[]{:S(2)}, u32[]{:S(2)}) %collective-permute-start.5) | collective-permute-done | bytes 69664 | tf_op jit(solution)/shard_map/ppermute | solution.py:282
  33.6 2.8 %collective-permute-done.4 = f32[136,128]{1,0:T(8,128)S(1)} collective-permute-done((f32[136,128]{1,0:T(8,128)S(1)}, f32[136,128]{1,0:T(8,128)S(1)}, u32[]{:S(2)}, u32[]{:S(2)}) %collective-permute-start.4) | collective-permute-done | bytes 69664 | tf_op jit(solution)/shard_map/ppermute | solution.py:282
  36.4 1.7 %collective-permute-start.8 = (f32[136,128]{1,0:T(8,128)S(1)}, f32[136,128]{1,0:T(8,128)S(1)}, u32[]{:S(2)}, u32[]{:S(2)}) collective-permute-start(f32[136,128]{1,0:T(8,128)S(1)} %add_add_fusion), channel_id=1, source_target_pairs={{0,3},{1,2},{2,1},{3,0},{4,7},{5,6},{6,5},{7,4},{8,11},{9,10},{10,... | collective-permute-start | bytes 208904 | tf_op jit(solution)/shard_map/ppermute | solution.py:282
  38.2 0.0 collective-permute-start.7
  38.2 2.7 %collective-permute-start.6 = (f32[136,128]{1,0:T(8,128)S(1)}, f32[136,128]{1,0:T(8,128)S(1)}, u32[]{:S(2)}, u32[]{:S(2)}) collective-permute-start(f32[136,128]{1,0:T(8,128)S(1)} %add_add_fusion), channel_id=1, source_target_pairs={{0,1},{1,0},{2,3},{3,2},{4,5},{5,4},{6,7},{7,6},{8,9},{9,8},{10,11... | collective-permute-start | bytes 208904 | tf_op jit(solution)/shard_map/ppermute | solution.py:282
  40.9 1.7 %collective-permute-done.8 = f32[136,128]{1,0:T(8,128)S(1)} collective-permute-done((f32[136,128]{1,0:T(8,128)S(1)}, f32[136,128]{1,0:T(8,128)S(1)}, u32[]{:S(2)}, u32[]{:S(2)}) %collective-permute-start.8) | collective-permute-done | bytes 69664 | tf_op jit(solution)/shard_map/ppermute | solution.py:282
  42.6 1.5 %collective-permute-done.7 = f32[136,128]{1,0:T(8,128)S(1)} collective-permute-done((f32[136,128]{1,0:T(8,128)S(1)}, f32[136,128]{1,0:T(8,128)S(1)}, u32[]{:S(2)}, u32[]{:S(2)}) %collective-permute-start.7) | collective-permute-done | bytes 69664 | tf_op jit(solution)/shard_map/ppermute | solution.py:282
  44.1 0.0 collective-permute-done.6
  44.2 2.5 %collective-permute-start.14 = (f32[288,128]{1,0:T(8,128)S(1)}, f32[288,128]{1,0:T(8,128)S(1)}, u32[]{:S(2)}, u32[]{:S(2)}) collective-permute-start(f32[288,128]{1,0:T(8,128)S(1)} %bitcast.51), channel_id=1, source_target_pairs={{0,24},{4,28},{8,16},{12,20},{16,8},{20,12},{24,0},{28,4},{1,25},{... | collective-permute-start | bytes 442376 | tf_op jit(solution)/shard_map/ppermute | solution.py:282
  46.7 0.5 collective-permute-start.13
  47.2 0.5 collective-permute-start.12
  47.8 2.5 %collective-permute-start.11 = (f32[256,128]{1,0:T(8,128)S(1)}, f32[256,128]{1,0:T(8,128)S(1)}, u32[]{:S(2)}, u32[]{:S(2)}) collective-permute-start(f32[256,128]{1,0:T(8,128)S(1)} %bitcast.55), channel_id=1, source_target_pairs={{0,24},{4,28},{8,16},{12,20},{16,8},{20,12},{24,0},{28,4},{1,25},{... | collective-permute-start | bytes 393224 | tf_op jit(solution)/shard_map/ppermute | solution.py:282
  50.3 0.5 collective-permute-start.10
  50.8 1.0 %collective-permute-done.14 = f32[288,128]{1,0:T(8,128)S(1)} collective-permute-done((f32[288,128]{1,0:T(8,128)S(1)}, f32[288,128]{1,0:T(8,128)S(1)}, u32[]{:S(2)}, u32[]{:S(2)}) %collective-permute-start.14) | collective-permute-done | bytes 147488 | tf_op jit(solution)/shard_map/ppermute | solution.py:282
  51.8 1.1 %collective-permute-start.9 = (f32[256,128]{1,0:T(8,128)S(1)}, f32[256,128]{1,0:T(8,128)S(1)}, u32[]{:S(2)}, u32[]{:S(2)}) collective-permute-start(f32[256,128]{1,0:T(8,128)S(1)} %bitcast.57), channel_id=1, source_target_pairs={{0,8},{4,12},{8,0},{12,4},{16,24},{20,28},{24,16},{28,20},{1,9},{5... | collective-permute-start | bytes 393224 | tf_op jit(solution)/shard_map/ppermute | solution.py:282
  52.9 0.4 collective-permute-done.13
  53.3 0.0 collective-permute-done.12
  53.3 0.1 dynamic-slice_bitcast_fusion.3
  53.4 12.7 %factor.1.wm_ref = f32[1280,128]{1,0:T(8,128)S(1)} custom-call(f32[1152,128]{1,0:T(8,128)S(1)} %pad_maximum_fusion.2.refs_0_), custom_call_target="tpu_custom_call" | custom-call | flops 20000000000 | bytes 1310720 | tf_op jit(solution)/shard_map/factor/pallas_call | solution.py:368
  66.2 0.0 collective-permute-done.11
  66.2 0.0 collective-permute-done.10
  66.2 0.0 collective-permute-done.9
  66.2 0.1 collective-permute-start.15
  66.3 0.0 copy-start.1
  66.3 0.0 copy-start.3
  66.4 0.6 collective-permute-start.16
  67.0 2.1 %collective-permute-done.16.co_ref = f32[1024,128]{1,0:T(8,128)S(1)} collective-permute-done((f32[1024,128]{1,0:T(8,128)S(1)}, f32[1024,128]{1,0:T(8,128)S(1)}, u32[]{:S(2)}, u32[]{:S(2)}) %collective-permute-start.16) | collective-permute-done | bytes 524320 | tf_op jit(solution)/shard_map/ppermute | solution.py:282
  69.1 0.0 collective-permute-done.15.wo_ref
  69.1 0.0 copy-done.3
  69.1 6.8 %project.1 = (bf16[1024,512]{1,0:T(8,128)(2,1)}, bf16[1024,512]{1,0:T(8,128)(2,1)}, f32[512,512]{1,0:T(8,128)}) custom-call(s32[1]{0:T(128)} %bitcast.core_ref, bf16[1024,512]{1,0:T(8,128)(2,1)S(1)} %copy-done.1, bf16[1024,512]{1,0:T(8,128)(2,1)S(1)} %copy-done.3, f32[1280,128]{1,0:T(8,128)S(1)} %factor.1.wm_ref, ...), custom_call_target="tpu_custom_call" | custom-call | flops 2147483648 | bytes 8388608 | tf_op jit(solution)/shard_map/project/pallas_call | solution.py:383
  (18 shorter events, 0.5 us)
Async XLA Ops:
  0.6 1.2 %copy-start = (bf16[1024,512]{1,0:T(8,128)(2,1)S(1)}, bf16[1024,512]{1,0:T(8,128)(2,1)}, u32[]{:S(2)}) copy-start(bf16[1024,512]{1,0:T(8,128)(2,1)} %x_ref.3) | copy-start | bytes 3145732
  1.9 1.2 %copy-start.2 = (bf16[1024,512]{1,0:T(8,128)(2,1)S(1)}, bf16[1024,512]{1,0:T(8,128)(2,1)}, u32[]{:S(2)}) copy-start(bf16[1024,512]{1,0:T(8,128)(2,1)} %y_ref.3) | copy-start | bytes 3145732
  4.8 2.9 %collective-permute-start = (f32[2176,128]{1,0:T(8,128)S(1)}, f32[2176,128]{1,0:T(8,128)S(1)}, u32[]{:S(2)}, u32[]{:S(2)}) collective-permute-start(f32[2176,128]{1,0:T(8,128)S(1)} %get-tuple-element.11), channel_id=1, source_target_pairs={{0,4},{4,0},{8,12},{12,8},{16,20},{20,16},{24,28},{28,24},{1,5},{5... | collective-permute-start | bytes 3342344 | tf_op jit(solution)/shard_map/ppermute | solution.py:282
  8.1 10.5 %collective-permute-start.1 = (f32[1088,128]{1,0:T(8,128)S(1)}, f32[1088,128]{1,0:T(8,128)S(1)}, u32[]{:S(2)}, u32[]{:S(2)}) collective-permute-start(f32[1088,128]{1,0:T(8,128)S(1)} %constant_dynamic-slice_fusion.4), channel_id=1, source_target_pairs={{0,16},{4,12},{8,24},{12,4},{16,0},{20,28},{24,8},{28,20},{1,17},{... | collective-permute-start | bytes 1671176 | tf_op jit(solution)/shard_map/ppermute | solution.py:316
  18.6 6.6 %collective-permute-start.2 = (f32[544,128]{1,0:T(8,128)S(1)}, f32[544,128]{1,0:T(8,128)S(1)}, u32[]{:S(2)}, u32[]{:S(2)}) collective-permute-start(f32[544,128]{1,0:T(8,128)S(1)} %constant_dynamic-slice_fusion.3), channel_id=1, source_target_pairs={{0,8},{4,20},{8,0},{12,28},{16,24},{20,4},{24,16},{28,12},{1,9},{5... | collective-permute-start | bytes 835592 | tf_op jit(solution)/shard_map/ppermute | solution.py:316
  25.3 4.7 %collective-permute-start.3 = (f32[136,128]{1,0:T(8,128)S(1)}, f32[136,128]{1,0:T(8,128)S(1)}, u32[]{:S(2)}, u32[]{:S(2)}) collective-permute-start(f32[136,128]{1,0:T(8,128)S(1)} %get-tuple-element.31), channel_id=1, source_target_pairs={{0,1},{1,0},{2,3},{3,2},{4,5},{5,4},{6,7},{7,6},{8,9},{9,8},{10,11... | collective-permute-start | bytes 208904 | tf_op jit(solution)/shard_map/ppermute | solution.py:282
  27.4 6.2 %collective-permute-start.5 = (f32[136,128]{1,0:T(8,128)S(1)}, f32[136,128]{1,0:T(8,128)S(1)}, u32[]{:S(2)}, u32[]{:S(2)}) collective-permute-start(f32[136,128]{1,0:T(8,128)S(1)} %get-tuple-element.32), channel_id=1, source_target_pairs={{0,3},{1,2},{2,1},{3,0},{4,7},{5,6},{6,5},{7,4},{8,11},{9,10},{10,... | collective-permute-start | bytes 208904 | tf_op jit(solution)/shard_map/ppermute | solution.py:282
  29.9 6.5 %collective-permute-start.4 = (f32[136,128]{1,0:T(8,128)S(1)}, f32[136,128]{1,0:T(8,128)S(1)}, u32[]{:S(2)}, u32[]{:S(2)}) collective-permute-start(f32[136,128]{1,0:T(8,128)S(1)} %get-tuple-element.33), channel_id=1, source_target_pairs={{0,2},{1,3},{2,0},{3,1},{4,6},{5,7},{6,4},{7,5},{8,10},{9,11},{10,... | collective-permute-start | bytes 208904 | tf_op jit(solution)/shard_map/ppermute | solution.py:282
  36.4 6.2 %collective-permute-start.8 = (f32[136,128]{1,0:T(8,128)S(1)}, f32[136,128]{1,0:T(8,128)S(1)}, u32[]{:S(2)}, u32[]{:S(2)}) collective-permute-start(f32[136,128]{1,0:T(8,128)S(1)} %add_add_fusion), channel_id=1, source_target_pairs={{0,3},{1,2},{2,1},{3,0},{4,7},{5,6},{6,5},{7,4},{8,11},{9,10},{10,... | collective-permute-start | bytes 208904 | tf_op jit(solution)/shard_map/ppermute | solution.py:282
  38.2 5.9 %collective-permute-start.7 = (f32[136,128]{1,0:T(8,128)S(1)}, f32[136,128]{1,0:T(8,128)S(1)}, u32[]{:S(2)}, u32[]{:S(2)}) collective-permute-start(f32[136,128]{1,0:T(8,128)S(1)} %add_add_fusion), channel_id=1, source_target_pairs={{0,2},{1,3},{2,0},{3,1},{4,6},{5,7},{6,4},{7,5},{8,10},{9,11},{10,... | collective-permute-start | bytes 208904 | tf_op jit(solution)/shard_map/ppermute | solution.py:282
  38.2 5.9 %collective-permute-start.6 = (f32[136,128]{1,0:T(8,128)S(1)}, f32[136,128]{1,0:T(8,128)S(1)}, u32[]{:S(2)}, u32[]{:S(2)}) collective-permute-start(f32[136,128]{1,0:T(8,128)S(1)} %add_add_fusion), channel_id=1, source_target_pairs={{0,1},{1,0},{2,3},{3,2},{4,5},{5,4},{6,7},{7,6},{8,9},{9,8},{10,11... | collective-permute-start | bytes 208904 | tf_op jit(solution)/shard_map/ppermute | solution.py:282
  44.2 7.6 %collective-permute-start.14 = (f32[288,128]{1,0:T(8,128)S(1)}, f32[288,128]{1,0:T(8,128)S(1)}, u32[]{:S(2)}, u32[]{:S(2)}) collective-permute-start(f32[288,128]{1,0:T(8,128)S(1)} %bitcast.51), channel_id=1, source_target_pairs={{0,24},{4,28},{8,16},{12,20},{16,8},{20,12},{24,0},{28,4},{1,25},{... | collective-permute-start | bytes 442376 | tf_op jit(solution)/shard_map/ppermute | solution.py:282
  46.7 6.6 %collective-permute-start.13 = (f32[288,128]{1,0:T(8,128)S(1)}, f32[288,128]{1,0:T(8,128)S(1)}, u32[]{:S(2)}, u32[]{:S(2)}) collective-permute-start(f32[288,128]{1,0:T(8,128)S(1)} %bitcast.52), channel_id=1, source_target_pairs={{0,16},{4,20},{8,24},{12,28},{16,0},{20,4},{24,8},{28,12},{1,17},{... | collective-permute-start | bytes 442376 | tf_op jit(solution)/shard_map/ppermute | solution.py:282
  47.2 6.1 %collective-permute-start.12 = (f32[288,128]{1,0:T(8,128)S(1)}, f32[288,128]{1,0:T(8,128)S(1)}, u32[]{:S(2)}, u32[]{:S(2)}) collective-permute-start(f32[288,128]{1,0:T(8,128)S(1)} %bitcast.53), channel_id=1, source_target_pairs={{0,8},{4,12},{8,0},{12,4},{16,24},{20,28},{24,16},{28,20},{1,9},{5... | collective-permute-start | bytes 442376 | tf_op jit(solution)/shard_map/ppermute | solution.py:282
  47.8 18.4 %collective-permute-start.11 = (f32[256,128]{1,0:T(8,128)S(1)}, f32[256,128]{1,0:T(8,128)S(1)}, u32[]{:S(2)}, u32[]{:S(2)}) collective-permute-start(f32[256,128]{1,0:T(8,128)S(1)} %bitcast.55), channel_id=1, source_target_pairs={{0,24},{4,28},{8,16},{12,20},{16,8},{20,12},{24,0},{28,4},{1,25},{... | collective-permute-start | bytes 393224 | tf_op jit(solution)/shard_map/ppermute | solution.py:282
  50.3 15.9 %collective-permute-start.10 = (f32[256,128]{1,0:T(8,128)S(1)}, f32[256,128]{1,0:T(8,128)S(1)}, u32[]{:S(2)}, u32[]{:S(2)}) collective-permute-start(f32[256,128]{1,0:T(8,128)S(1)} %bitcast.56), channel_id=1, source_target_pairs={{0,16},{4,20},{8,24},{12,28},{16,0},{20,4},{24,8},{28,12},{1,17},{... | collective-permute-start | bytes 393224 | tf_op jit(solution)/shard_map/ppermute | solution.py:282
  51.8 14.4 %collective-permute-start.9 = (f32[256,128]{1,0:T(8,128)S(1)}, f32[256,128]{1,0:T(8,128)S(1)}, u32[]{:S(2)}, u32[]{:S(2)}) collective-permute-start(f32[256,128]{1,0:T(8,128)S(1)} %bitcast.57), channel_id=1, source_target_pairs={{0,8},{4,12},{8,0},{12,4},{16,24},{20,28},{24,16},{28,20},{1,9},{5... | collective-permute-start | bytes 393224 | tf_op jit(solution)/shard_map/ppermute | solution.py:282
  66.2 2.9 %collective-permute-start.15 = (f32[1280,128]{1,0:T(8,128)S(1)}, f32[1280,128]{1,0:T(8,128)S(1)}, u32[]{:S(2)}, u32[]{:S(2)}) collective-permute-start(f32[1280,128]{1,0:T(8,128)S(1)} %factor.1.wm_ref), channel_id=1, source_target_pairs={{0,4},{4,0},{8,12},{12,8},{16,20},{20,16},{24,28},{28,24},{1,5},{5... | collective-permute-start | bytes 1966088 | tf_op jit(solution)/shard_map/ppermute | solution.py:282
  66.3 2.8 %copy-start.1 = (bf16[1024,512]{1,0:T(8,128)(2,1)S(1)}, bf16[1024,512]{1,0:T(8,128)(2,1)}, u32[]{:S(2)}) copy-start(bf16[1024,512]{1,0:T(8,128)(2,1)} %x_ref.3) | copy-start | bytes 3145732
  66.3 2.8 %copy-start.3 = (bf16[1024,512]{1,0:T(8,128)(2,1)S(1)}, bf16[1024,512]{1,0:T(8,128)(2,1)}, u32[]{:S(2)}) copy-start(bf16[1024,512]{1,0:T(8,128)(2,1)} %y_ref.3) | copy-start | bytes 3145732
  66.4 2.7 %collective-permute-start.16 = (f32[1024,128]{1,0:T(8,128)S(1)}, f32[1024,128]{1,0:T(8,128)S(1)}, u32[]{:S(2)}, u32[]{:S(2)}) collective-permute-start(f32[1024,128]{1,0:T(8,128)S(1)} %maximum_multiply_fusion.cm_ref), channel_id=1, source_target_pairs={{0,4},{4,0},{8,12},{12,8},{16,20},{20,16},{24,28},{28,24},{1,5},{5... | collective-permute-start | bytes 1572872 | tf_op jit(solution)/shard_map/ppermute | solution.py:282
